TPU v7x, 32 devices: a whole 2x2x4 slice. The times are simulated.
32 devices in a mesh: fsdp: 2 (over y), blk: 4 (over x, core), ulysses: 4 (over z).
Axes of the slice: x: 2, y: 2, z: 4, core: 2. Of those that a mesh axis runs over, the one named last changes fastest.
Arguments:
- tokens: bfloat16 [8192, 768], P(('fsdp', 'blk', 'ulysses')), may hold values from -6 to 6
- positions: int32 [8192], P(('fsdp', 'blk', 'ulysses')), may hold values from 0 to 4095, as said below
- cotangent: bfloat16 [8192, 768], P(('fsdp', 'blk', 'ulysses')), may hold values from -6 to 6
- ln1_gain: bfloat16 [768], P('fsdp'), may hold values from 0.099609375 to 1.8984375
- ln1_bias: bfloat16 [768], P('fsdp'), may hold values from -3 to 3
- ln2_gain: bfloat16 [768], P('fsdp'), may hold values from 0.099609375 to 1.8984375
- ln2_bias: bfloat16 [768], P('fsdp'), may hold values from -3 to 3
- qkv_weight: bfloat16 [768, 2304], P('fsdp'), may hold values from -0.21875 to 0.21875
- qkv_bias: bfloat16 [2304], P('fsdp'), may hold values from -2 to 2
- out_weight: bfloat16 [768, 768], P('fsdp'), may hold values from -3 to 3
- out_bias: bfloat16 [768], P('fsdp'), may hold values from -2 to 2
- up_weight: bfloat16 [768, 3072], P('fsdp'), may hold values from -0.21875 to 0.21875
- up_bias: bfloat16 [3072], P('fsdp'), may hold values from -2 to 2
- down_weight: bfloat16 [3072, 768], P('fsdp'), may hold values from -0.109375 to 0.109375
- down_bias: bfloat16 [768], P('fsdp'), may hold values from -2 to 2
Outputs:
- output: bfloat16 [8192, 768], P(('fsdp', 'blk', 'ulysses'))
- input_grad: bfloat16 [8192, 768], P(('fsdp', 'blk', 'ulysses'))
- ln1_gain_grad: float32 [768], P('fsdp')
- ln1_bias_grad: float32 [768], P('fsdp')
- ln2_gain_grad: float32 [768], P('fsdp')
- ln2_bias_grad: float32 [768], P('fsdp')
- qkv_weight_grad: float32 [768, 2304], P('fsdp')
- qkv_bias_grad: float32 [2304], P('fsdp')
- out_weight_grad: float32 [768, 768], P('fsdp')
- out_bias_grad: float32 [768], P('fsdp')
- up_weight_grad: float32 [768, 3072], P('fsdp')
- up_bias_grad: float32 [3072], P('fsdp')
- down_weight_grad: float32 [3072, 768], P('fsdp')
- down_bias_grad: float32 [768], P('fsdp')
Inputs may be any that keep to these rules, and one draw needn't show every extreme that they name: Each sequence of 4096 tokens holds every position from 0 once; positions run in blocks of 128 consecutive ascending values, and the order of the blocks within a sequence is drawn.
All inputs are finite; a program needn't handle non-finite values.
Results may differ from a plain program's by a relative error of at most 0.018.
Values may be sent and summed in bfloat16 or wider, within the bound.
No kernel may reach another device: no remote copies, remote signals or barrier semaphores. Data moves between devices by JAX's collectives and lax.ppermute only.
A program may use at most 128 MiB of HBM per device.

v0:
```python
import jax
import jax.numpy as jnp
import numpy as np
from jax import lax
from jax.experimental import pallas as pl
from jax.experimental.pallas import tpu as pltpu
from jax.sharding import PartitionSpec as P

HEAD = 64
ROT = 16
STRETCH = 128
CHUNK = 8
BIG_NEG = -1e30

f32 = jnp.float32
bf16 = jnp.bfloat16


def layer_norm(values, gain, shift):
    center = jnp.mean(values, -1, keepdims=True)
    offset = values - center
    spread = jnp.mean(offset * offset, -1, keepdims=True)
    return offset * lax.rsqrt(spread + 1e-05) * gain + shift


def gelu_exact(values):
    return jax.nn.gelu(values, approximate=False)


def swap(values, axis, bits):
    count = lax.axis_size(axis)
    return lax.ppermute(values, axis, [(i, i ^ bits) for i in range(count)])


def after(values, *earlier):
    return lax.optimization_barrier((values, earlier))[0]


def bit_of(axis, bit):
    return (lax.axis_index(axis) // bit) % 2


def in_order(bit, mine, other, axis=0):
    return jnp.concatenate([jnp.where(bit == 0, mine, other), jnp.where(bit == 0, other, mine)], axis)


def by_device(pieces, index):
    step = 1
    while step < len(pieces):
        odd = (index // step) % 2 == 1
        pieces = [jnp.where(odd, pieces[i ^ step], pieces[i]) for i in range(len(pieces))]
        step *= 2
    return pieces


def add_half(halves, axis, bit):
    which = bit_of(axis, bit)
    got = swap(jnp.where(which == 0, halves[1], halves[0]), axis, bit)
    kept = jnp.where(which == 0, halves[0], halves[1])
    return (kept.astype(f32) + got.astype(f32)).astype(bf16)


def halves_of(values, axis):
    half = values.shape[axis] // 2
    return (
        lax.slice_in_dim(values, 0, half, axis=axis),
        lax.slice_in_dim(values, half, 2 * half, axis=axis),
    )


def share_half(values, axis, bit, dim):
    return in_order(bit_of(axis, bit), values, swap(values, axis, bit), dim)


def gather_small(shard):
    if lax.axis_size("fsdp") != 2:
        return lax.all_gather(shard[None], "fsdp", axis=0, tiled=True)
    return in_order(lax.axis_index("fsdp"), shard[None], swap(shard[None], "fsdp", 1))


def quarter_of(shard):
    quarter = shard.shape[0] // 4
    place = bit_of("blk", 1) * 2 + bit_of("blk", 2)
    return lax.dynamic_slice_in_dim(shard, place * quarter, quarter)


def both_shards(shard, half):
    return in_order(lax.axis_index("fsdp"), shard, share_half(half, "blk", 1, 0))


def attend_kernel(rank, q_ref, g_ref, *refs):
    kv_refs = refs[:-9]
    o_ref, dq_ref, keep_ref, send_ref, rows, lanes, sums, probs, order = refs[-9:]
    heads = range(q_ref.shape[0])
    cols = q_ref.shape[0] * HEAD
    n_keys = rank.shape[0]
    own = q_ref.shape[-1] // STRETCH
    wide = 2 * STRETCH
    span = CHUNK * STRETCH

    for t in range(n_keys):
        i, at = t // own, (t % own) * STRETCH
        place = rank[t]
        for h in heads:
            both = jnp.concatenate(
                [
                    kv_refs[i][first : first + HEAD, at : at + STRETCH]
                    for first in (h * HEAD, cols + h * HEAD)
                ],
                0,
            )
            lanes[h, place] = both
            rows[h, place] = both.T
            sums[h, t] = jnp.zeros((STRETCH, 2 * HEAD), f32)
    for a in range(own):
        before = jnp.int32(0)
        for b in range(own):
            before += (rank[b] < rank[a]).astype(jnp.int32)
        order[before] = a

    def side(h, j, part):
        first = part * HEAD
        return jnp.concatenate(
            [lanes[h, j * CHUNK + i, first : first + HEAD, :] for i in range(CHUNK)], 1
        )

    def keys(h, j):
        return rows[h, pl.ds(j * CHUNK, CHUNK)].reshape(span, 2 * HEAD)

    def pair(p, carry):
        a, b = order[2 * p], order[2 * p + 1]
        ra, rb = rank[a], rank[b]
        at_a = pl.ds(pl.multiple_of(a * STRETCH, STRETCH), STRETCH)
        at_b = pl.ds(pl.multiple_of(b * STRETCH, STRETCH), STRETCH)
        q = [jnp.concatenate([q_ref[h, :, at_a], q_ref[h, :, at_b]], 1) for h in heads]
        g = [jnp.concatenate([g_ref[h, :, at_a], g_ref[h, :, at_b]], 1) for h in heads]
        none = jnp.zeros_like(q[0])
        q_low = [jnp.concatenate([v, none], 0) for v in q]
        g_high = [jnp.concatenate([none, v], 0) for v in g]
        lane = lax.broadcasted_iota(jnp.int32, (1, wide), 1)
        q_place = jnp.where(lane < STRETCH, ra * STRETCH + lane, rb * STRETCH + lane - STRETCH)
        clear = ra // CHUNK
        total = (rb + CHUNK) // CHUNK

        def score(j, tops, masked):
            result = []
            for h in heads:
                s = jnp.dot(keys(h, j), q_low[h], preferred_element_type=f32)
                if masked:
                    k_place = j * span + lax.broadcasted_iota(jnp.int32, (span, 1), 0)
                    s = jnp.where(k_place <= q_place, s, BIG_NEG)
                probs[h, j] = s
                result.append(jnp.maximum(tops[h], jnp.max(s.reshape(span // 8, 8, wide), 0)))
            return tuple(result)

        tops = tuple(jnp.full((8, wide), BIG_NEG, f32) for _ in heads)
        tops = lax.fori_loop(0, clear, lambda j, v: score(j, v, False), tops)
        tops = lax.fori_loop(clear, total, lambda j, v: score(j, v, True), tops)
        tops = [jnp.max(v, 0, keepdims=True) for v in tops]

        def weigh(j, state):
            result = []
            for h in heads:
                count, out = state[h]
                weight = jnp.exp(probs[h, j] - tops[h])
                probs[h, j] = weight
                count = count + jnp.sum(weight.reshape(span // 8, 8, wide), 0)
                out = out + jnp.dot(side(h, j, 1), weight.astype(bf16), preferred_element_type=f32)
                result.append((count, out))
            return tuple(result)

        state = tuple((jnp.zeros((8, wide), f32), jnp.zeros((HEAD, wide), f32)) for _ in heads)
        state = lax.fori_loop(0, total, weigh, state)
        inverse, delta, right = [], [], []
        for h in heads:
            count, out = state[h]
            inverse.append(1.0 / jnp.sum(count, 0, keepdims=True))
            out = out * inverse[h]
            delta.append(jnp.sum(out * g[h].astype(f32), 0, keepdims=True))
            o_ref[h, :, at_a] = out[:, :STRETCH].astype(bf16)
            o_ref[h, :, at_b] = out[:, STRETCH:].astype(bf16)
            top = jnp.concatenate([g[h], none], 0).T
            right.append(jnp.concatenate([top, jnp.concatenate([none, q[h]], 0).T], 0))

        def back(j, d_q):
            result = []
            for h in heads:
                weight = probs[h, j] * inverse[h]
                d_weight = jnp.dot(keys(h, j), g_high[h], preferred_element_type=f32)
                d_score = (weight * (d_weight - delta[h])).astype(bf16)
                left = jnp.concatenate([weight.astype(bf16), d_score], 1)
                sums[h, pl.ds(j * CHUNK, CHUNK)] += jnp.dot(
                    left, right[h], preferred_element_type=f32
                ).reshape(CHUNK, STRETCH, 2 * HEAD)
                result.append(d_q[h] + jnp.dot(side(h, j, 0), d_score, preferred_element_type=f32))
            return tuple(result)

        d_q = lax.fori_loop(0, total, back, tuple(jnp.zeros((HEAD, wide), f32) for _ in heads))
        for h in heads:
            scaled = d_q[h] * HEAD ** (-0.5)
            dq_ref[h, :, at_a] = scaled[:, :STRETCH]
            dq_ref[h, :, at_b] = scaled[:, STRETCH:]
        return carry

    lax.fori_loop(0, own // 2, pair, 0)
    for t in range(n_keys):
        i, at = t // own, (t % own) * STRETCH
        to = keep_ref if i % 2 == 0 else send_ref
        for h in heads:
            turned = sums[h, rank[t]].T.astype(bf16)
            first = h * HEAD
            to[i // 2, cols + first : cols + first + HEAD, at : at + STRETCH] = turned[:HEAD]
            to[i // 2, first : first + HEAD, at : at + STRETCH] = turned[HEAD:]


def attend(ranks, q, g, kv):
    heads, _, count = q.shape
    devices = len(kv)
    n_keys = devices * count // STRETCH
    pairs = heads * 4 * HEAD * count * count * devices
    half = (devices // 2, 2 * heads * HEAD, count)
    q_spec = pl.BlockSpec(q.shape, lambda i, *_: (0, 0, 0))
    half_spec = pl.BlockSpec(half, lambda i, *_: (0, 0, 0))
    return pl.pallas_call(
        attend_kernel,
        grid_spec=pltpu.PrefetchScalarGridSpec(
            num_scalar_prefetch=1,
            grid=(1,),
            in_specs=[q_spec, q_spec] + [pl.BlockSpec(v.shape, lambda i, *_: (0, 0)) for v in kv],
            out_specs=[q_spec, q_spec, half_spec, half_spec],
            scratch_shapes=[
                pltpu.VMEM((heads, n_keys, STRETCH, 2 * HEAD), bf16),
                pltpu.VMEM((heads, n_keys, 2 * HEAD, STRETCH), bf16),
                pltpu.VMEM((heads, n_keys, STRETCH, 2 * HEAD), f32),
                pltpu.VMEM((heads, n_keys // CHUNK, CHUNK * STRETCH, 2 * STRETCH), f32),
                pltpu.SMEM((count // STRETCH,), jnp.int32),
            ],
        ),
        out_shape=[
            jax.ShapeDtypeStruct(q.shape, bf16),
            jax.ShapeDtypeStruct(q.shape, f32),
            jax.ShapeDtypeStruct(half, bf16),
            jax.ShapeDtypeStruct(half, bf16),
        ],
        compiler_params=pltpu.CompilerParams(vmem_limit_bytes=56 * 2**20),
        cost_estimate=pl.CostEstimate(
            flops=12 * pairs, bytes_accessed=16 * q.size * devices, transcendentals=pairs // 512
        ),
        name="attend",
    )(ranks, q, g, *kv)


def prepare_kernel(freqs, gain, shift, weight, bias, *refs):
    groups = len(refs) - 5
    x_refs = refs[:groups]
    normed_ref, q_ref, kv_ref, cos_ref, sin_ref = refs[groups:]
    count = normed_ref.shape[0] // groups
    cols = q_ref.shape[0]
    halfway = ROT // 2
    blocks = count // STRETCH
    lane = lax.broadcasted_iota(jnp.int32, (1, STRETCH), 1).astype(f32)
    kv_ref[2 * cols :, :] = jnp.zeros((kv_ref.shape[0] - 2 * cols, kv_ref.shape[1]), bf16)
    spots = lax.broadcasted_iota(jnp.int32, (1, STRETCH), 1)
    table = jnp.zeros((1, STRETCH), f32)
    for i, x_ref in enumerate(x_refs):
        at = i * count
        normed = layer_norm(x_ref[:count].astype(f32), gain[...], shift[...]).astype(bf16)
        normed_ref[at : at + count] = normed
        joined = jnp.dot(normed, weight[...], preferred_element_type=f32) + bias[...]
        joined = joined.T
        ranks = x_ref[count : count + 16, :STRETCH].astype(f32)[:1]
        places = []
        for b in range(blocks):
            rank = jnp.sum(jnp.where(spots == b, ranks, 0.0), 1, keepdims=True)
            places.append(rank * STRETCH + lane)
            table = jnp.where(spots == i * blocks + b, rank, table)
        angles = freqs[...] * jnp.concatenate(places, 1)
        cosine, sine = jnp.cos(angles), jnp.sin(angles)
        cos_ref[:, at : at + count] = cosine
        sin_ref[:, at : at + count] = sine
        for to, first, scale in ((q_ref, 0, HEAD ** (-0.5)), (kv_ref, cols, 1.0)):
            for h in range(cols // HEAD):
                low = first + h * HEAD
                one = joined[low : low + halfway]
                two = joined[low + halfway : low + ROT]
                rest = joined[low + ROT : low + HEAD]
                turned = jnp.concatenate(
                    [one * cosine - two * sine, two * cosine + one * sine, rest], 0
                ).astype(bf16)
                to[h * HEAD : (h + 1) * HEAD, at : at + count] = turned * jnp.bfloat16(scale)
        kv_ref[cols : 2 * cols, at : at + count] = joined[2 * cols :].astype(bf16)
    kv_ref[2 * cols :, :STRETCH] = jnp.broadcast_to(table, (16, STRETCH)).astype(bf16)


def prepare(gain, shift, weight, bias, x_all, count):
    width = weight.shape[0]
    cols = weight.shape[1] // 3
    rows = count * len(x_all)
    halfway = ROT // 2
    freqs = jnp.asarray(10000.0 ** (-np.arange(halfway) * 2.0 / ROT), f32)[:, None]
    return pl.pallas_call(
        prepare_kernel,
        out_shape=[
            jax.ShapeDtypeStruct((rows, width), bf16),
            jax.ShapeDtypeStruct((cols, rows), bf16),
            jax.ShapeDtypeStruct((2 * cols + 16, rows), bf16),
            jax.ShapeDtypeStruct((ROT // 2, rows), f32),
            jax.ShapeDtypeStruct((ROT // 2, rows), f32),
        ],
        compiler_params=pltpu.CompilerParams(vmem_limit_bytes=40 * 2**20),
        cost_estimate=pl.CostEstimate(
            flops=6 * cols * rows * width, bytes_accessed=8 * rows * width, transcendentals=0
        ),
        name="prepare",
    )(freqs, gain[None], shift[None], weight, bias[None], *x_all)


def rotate(heads, cosine, sine):
    halfway = ROT // 2
    first = heads[:, :halfway]
    second = heads[:, halfway:ROT]
    return jnp.concatenate(
        [first * cosine - second * sine, second * cosine + first * sine, heads[:, ROT:]], 1
    )


def around(values):
    return [values] + [swap(values, "ulysses", j) for j in range(1, lax.axis_size("ulysses"))]


def to_tokens(values):
    groups = lax.axis_size("ulysses")
    count = values.shape[1] // groups
    pieces = [values[:, j * count : (j + 1) * count] for j in range(groups)]
    return [pieces[0]] + [swap(pieces[j], "ulysses", j) for j in range(1, groups)]


def units_of(up_weight, side):
    units = up_weight.shape[1] // 2
    return jnp.where(side == 0, up_weight[:, :units], up_weight[:, units:])


def mlp_pair(x_both, e_both, gain, shift, up, up_bias, down_weight, *meanwhile):
    side = lax.axis_index("fsdp")
    rows, width = x_both.shape[0] // 2, x_both.shape[1]
    units = up.shape[1]
    normed = layer_norm(x_both.astype(f32), gain, shift).astype(bf16)
    hidden = jnp.dot(normed, up, preferred_element_type=f32) + up_bias.astype(f32)
    active_f, pull_gelu = jax.vjp(gelu_exact, hidden)
    active = active_f.astype(bf16)
    part = jnp.dot(active, down_weight, preferred_element_type=f32)
    out = part[:rows] + swap(part[rows:].astype(bf16), "fsdp", 1).astype(f32)
    d_active = jnp.einsum("td,fd->tf", e_both, down_weight, preferred_element_type=f32)
    d_hidden = pull_gelu(d_active)[0].astype(bf16)
    g_up_bias = jnp.sum(d_hidden.astype(f32), 0)
    d_part = jnp.einsum("tf,df->td", d_hidden, up, preferred_element_type=f32)
    d_normed = d_part[:rows] + swap(d_part[rows:].astype(bf16), "fsdp", 1).astype(f32)
    active, d_hidden = after((active, d_hidden), *meanwhile)
    g_up = jnp.einsum(
        "td,tcf->cdf", normed, d_hidden.reshape(2 * rows, 2, units // 2), preferred_element_type=f32
    ).astype(bf16)
    g_down = jnp.einsum("tf,td->fd", active, e_both, preferred_element_type=f32).astype(bf16)
    g_down = g_down.reshape(2, units // 2, width)
    pieces = jnp.stack([g_up, g_down], 1).reshape(2, 2, 2, width // 2, width)
    first = add_half((pieces[0], pieces[1]), "blk", 1)
    sums = add_half(halves_of(first, 2), "blk", 2)
    side, none = lax.axis_index("fsdp"), jnp.zeros_like(g_up_bias)
    g_up_bias = jnp.concatenate([jnp.where(side == 0, g_up_bias, none), jnp.where(side == 0, none, g_up_bias)])
    return out, d_normed, first, sums, g_up_bias


def finish_pair(sums, earlier):
    side = lax.axis_index("fsdp")
    sums = after(sums, earlier)
    sums = add_half(halves_of(sums, 2), "ulysses", 1)
    sums = add_half(halves_of(sums, 2), "ulysses", 2)
    got = swap(jnp.where(side == 0, sums[0, 1], sums[0, 0]), "fsdp", 1)
    kept = jnp.where(side == 0, sums[0, 0], sums[0, 1])
    sums = jnp.concatenate([in_order(side, kept[None], got[None]), sums[1]], 0)
    sums = share_half(sums, "ulysses", 2, 1)
    sums = share_half(sums, "ulysses", 1, 1)
    sums = share_half(sums, "blk", 2, 1)
    return place_mlp(bit_of("blk", 1), sums, swap(sums, "blk", 1))


def place_mlp_kernel(which, mine, other, up_ref, down_ref):
    width = mine.shape[-1]
    for c, ref in ((which[0], mine), (1 - which[0], other)):
        for f in range(2):
            at = pl.multiple_of((2 * f + c) * width, STRETCH)
            up_ref[:, pl.ds(at, width)] = ref[f].astype(f32)
            down_ref[c, f] = ref[2 + f].astype(f32)


def place_mlp(which, mine, other):
    _, rows, width = mine.shape
    step = rows // 4
    whole = pl.BlockSpec((4, step, width), lambda i, *_: (0, i, 0))
    up, down = pl.pallas_call(
        place_mlp_kernel,
        grid_spec=pltpu.PrefetchScalarGridSpec(
            num_scalar_prefetch=1,
            grid=(4,),
            in_specs=[whole, whole],
            out_specs=[
                pl.BlockSpec((step, 4 * width), lambda i, *_: (i, 0)),
                pl.BlockSpec((2, 2, step, width), lambda i, *_: (0, 0, i, 0)),
            ],
        ),
        out_shape=[
            jax.ShapeDtypeStruct((rows, 4 * width), f32),
            jax.ShapeDtypeStruct((2, 2, rows, width), f32),
        ],
        compiler_params=pltpu.CompilerParams(vmem_limit_bytes=32 * 2**20),
        cost_estimate=pl.CostEstimate(flops=0, bytes_accessed=12 * mine.size, transcendentals=0),
        name="place_mlp",
    )(which[None], mine, other)
    return up, down.reshape(4 * rows, width)


def place_qkv_kernel(which, mine, other, qkv_ref, out_ref):
    first = which[0] == 0
    rows, half = mine.shape[1:]
    width = 2 * half
    groups = mine.shape[0] // 4
    for t in range(3):
        blocks = []
        for z in range(groups):
            a, b = mine[3 * z + t], other[3 * z + t]
            blocks += [jnp.where(first, a, b), jnp.where(first, b, a)]
        qkv_ref[:, t * width : (t + 1) * width] = jnp.concatenate(blocks, 0).astype(f32).T
    for z in range(groups // 2):
        for side in range(2):
            a, b = mine[3 * groups + 2 * z + side], other[3 * groups + 2 * z + side]
            at = 2 * z * rows
            both = jnp.concatenate([jnp.where(first, a, b), jnp.where(first, b, a)], 0)
            out_ref[at : at + 2 * rows, side * half : (side + 1) * half] = both.astype(f32)


def place_qkv(which, mine, other):
    _, rows, half = mine.shape
    groups = mine.shape[0] // 4
    return pl.pallas_call(
        place_qkv_kernel,
        grid_spec=pltpu.PrefetchScalarGridSpec(
            num_scalar_prefetch=1,
            grid=(1,),
            in_specs=[pl.BlockSpec(v.shape, lambda i, *_: (0, 0, 0)) for v in (mine, other)],
            out_specs=[
                pl.BlockSpec((half, 6 * half), lambda i, *_: (0, 0)),
                pl.BlockSpec((groups * rows, 2 * half), lambda i, *_: (0, 0)),
            ],
        ),
        out_shape=[
            jax.ShapeDtypeStruct((half, 6 * half), f32),
            jax.ShapeDtypeStruct((groups * rows, 2 * half), f32),
        ],
        compiler_params=pltpu.CompilerParams(vmem_limit_bytes=40 * 2**20),
        cost_estimate=pl.CostEstimate(flops=0, bytes_accessed=12 * mine.size, transcendentals=0),
        name="place_qkv",
    )(which[None], mine, other)


def mlp_gathered(x, e, gain, shift, up, bias, down, *meanwhile):
    normed = layer_norm(x.astype(f32), gain, shift).astype(bf16)
    hidden = jnp.dot(normed, up, preferred_element_type=f32) + bias.astype(f32)
    active_f, pull_gelu = jax.vjp(gelu_exact, hidden)
    active = active_f.astype(bf16)
    out = jnp.dot(active, down, preferred_element_type=f32)
    g_down = jnp.einsum("tf,td->fd", active, e, preferred_element_type=f32)
    d_active = jnp.einsum("td,fd->tf", e, down, preferred_element_type=f32)
    d_hidden = pull_gelu(d_active)[0].astype(bf16)
    g_up = jnp.einsum("td,tf->df", normed, d_hidden, preferred_element_type=f32)
    d_normed = jnp.einsum("tf,df->td", d_hidden, up, preferred_element_type=f32)
    g_up, g_down = (
        lax.psum(
            lax.psum_scatter(g.astype(bf16), "fsdp", scatter_dimension=0, tiled=True),
            ("blk", "ulysses"),
        ).astype(f32)
        for g in (g_up, g_down)
    )
    return out, d_normed, d_hidden, (g_up, g_down), jnp.sum(d_hidden.astype(f32), 0)


def add_blks(grads):
    if lax.axis_size("fsdp") != 2:
        return lax.psum(grads, "blk")
    return add_half(halves_of(add_half(halves_of(grads, 1), "blk", 1), 1), "blk", 2)


def attention_grads(grads, vector):
    side = lax.axis_index("fsdp")
    group = lax.axis_index("ulysses")
    groups = lax.axis_size("ulysses")
    _, rows, width = grads.shape
    if lax.axis_size("fsdp") != 2:
        total = lax.all_gather(lax.psum(grads, "fsdp"), "ulysses", axis=1, tiled=True)
        part = width // lax.axis_size("fsdp")
        g_qkv = lax.dynamic_slice_in_dim(total[:3], side * part, part, 2)
        g_out = lax.dynamic_slice_in_dim(total[3], side * part, part, 0)
        g_qkv = g_qkv.reshape(3 * width, part).T.astype(f32)
        return g_qkv, g_out.astype(f32), sum_everywhere(vector)
    half = width // 2
    size = vector.shape[0]
    small = jnp.pad(vector.astype(bf16), (0, rows * half - size)).reshape(1, rows, half)
    low, high = grads[:, :, :half], grads[:, :, half:]
    kept = jnp.where(side == 0, low[:3], high[:3])
    sent = jnp.where(side == 0, high[:3], low[:3])
    whole = jnp.stack([low[3], high[3]])
    kept = jnp.concatenate([kept, whole, small])
    got = swap(jnp.concatenate([sent, whole, small]), "fsdp", 1)
    kept = (kept.astype(f32) + got.astype(f32)).astype(bf16)
    kept = by_device(around(kept), group)
    small = sum(v[5:].astype(f32) for v in kept).astype(bf16)
    of_qkv = jnp.concatenate([v[:3] for v in kept])
    of_out = [jnp.where(side == 0, a[3:5], b[3:5]) for a, b in zip(kept[: groups // 2], kept[groups // 2 :])]
    kept = jnp.concatenate([of_qkv] + of_out)
    units = kept.shape[0]
    got = swap(jnp.concatenate([kept, small]), "blk", 2)
    kept = in_order(bit_of("blk", 2), kept, got[:units], 1)
    small = (small.astype(f32) + got[units:].astype(f32)).astype(bf16)
    wide = jnp.pad(small, ((0, 0), (0, rows), (0, 0)))
    got = swap(jnp.concatenate([kept, wide]), "blk", 1)
    small = small.astype(f32) + got[units:, :rows].astype(f32)
    g_qkv, g_out = place_qkv(bit_of("blk", 1), kept, got)
    return g_qkv, g_out, small.reshape(-1)[:size]


def sum_everywhere(values):
    for axis in ("blk", "ulysses", "fsdp"):
        step = 1
        while step < lax.axis_size(axis):
            values = values + swap(values, axis, step)
            step *= 2
    return values


def on_device(
    tokens,
    positions,
    cotangent,
    ln1_gain,
    ln1_bias,
    ln2_gain,
    ln2_bias,
    qkv_weight,
    qkv_bias,
    out_weight,
    out_bias,
    up_weight,
    up_bias,
    down_weight,
    down_bias,
):
    count, width = tokens.shape
    groups = lax.axis_size("ulysses")
    group = lax.axis_index("ulysses")
    shards = lax.axis_size("fsdp")
    cols = width // groups
    heads = cols // HEAD
    rows = count * groups

    ranks = (positions[::STRETCH] // STRETCH).astype(bf16)[None]
    ranks = jnp.pad(ranks, ((0, 15), (0, width - ranks.shape[1])))
    x_ranks = jnp.concatenate([tokens, ranks])
    if shards == 2:
        side = lax.axis_index("fsdp")
        part_qkv = swap(quarter_of(qkv_weight), "fsdp", 1)
        half_up = jnp.concatenate([units_of(up_weight, 1 - side), out_weight], 1)
        part_up = swap(after(quarter_of(half_up), part_qkv), "fsdp", 1)
        x_e = swap(after(jnp.stack([tokens, cotangent]), part_up), "fsdp", 1)
        w_qkv = both_shards(qkv_weight, share_half(part_qkv, "blk", 2, 0))
        half_up = share_half(part_up, "blk", 2, 0)
        x_all = around(x_ranks)
        mine = jnp.concatenate([units_of(up_weight, side), out_weight], 1)
        half_up = both_shards(mine, half_up)
        w_up, w_out = half_up[:, :-width], half_up[:, -width:]
        x_mlp = jnp.concatenate([tokens, x_e[0]])
        e_mlp = jnp.concatenate([cotangent, x_e[1]])
        b_up, w_down, mlp, finish = up_bias, down_weight, mlp_pair, finish_pair
    else:
        x_all, part_qkv = around(x_ranks), x_ranks
        w_qkv, w_up, w_out, w_down = (
            lax.all_gather(w, "fsdp", axis=0, tiled=True)
            for w in (qkv_weight, up_weight, out_weight, down_weight)
        )
        b_up = gather_small(up_bias).reshape(-1)
        x_mlp, e_mlp, mlp, finish = tokens, cotangent, mlp_gathered, lambda v, _: v
    small = jnp.concatenate([ln1_gain, ln1_bias, ln2_gain, ln2_bias, out_bias, down_bias, qkv_bias])
    small = gather_small(after(small, part_qkv))
    part = width // shards
    ln1_g, ln1_b, ln2_g, ln2_b, b_out, b_down = (
        small[:, i * part : (i + 1) * part].reshape(width).astype(f32) for i in range(6)
    )
    b_qkv = small[:, 6 * part :].reshape(3 * width).astype(f32)
    starts = [i * width + group * cols for i in range(3)]
    w_mine = jnp.concatenate([lax.dynamic_slice_in_dim(w_qkv, v, cols, 1) for v in starts], 1)
    b_mine = jnp.concatenate([lax.dynamic_slice_in_dim(b_qkv, v, cols, 0) for v in starts])
    x_all = after(x_all, w_mine)
    normed, queries, kv, cosine, sine = prepare(ln1_g, ln1_b, w_mine, b_mine, x_all, count)
    queries = queries.reshape(heads, HEAD, rows)
    pieces = {0: kv}
    step = lax.axis_size("blk") // 2
    while step >= 1:
        for i in list(pieces):
            pieces[i ^ step] = swap(pieces[i], "blk", step)
        step //= 2
    kv_all = [pieces[i] for i in range(len(pieces))]
    ranks = jnp.concatenate([v[2 * cols, : rows // STRETCH] for v in kv_all]).astype(jnp.int32)

    d_mixed = jnp.einsum("ed,td->et", w_out, after(cotangent, kv), preferred_element_type=f32).astype(bf16)
    d_heads = [lax.dynamic_slice_in_dim(d_mixed, (group ^ j) * cols, cols) for j in range(groups)]
    d_heads = [d_heads[0]] + [swap(d_heads[j], "ulysses", j) for j in range(1, groups)]
    d_heads = jnp.concatenate(d_heads, 1).reshape(heads, HEAD, rows)

    x_mlp, w_up = after((x_mlp, w_up), kv, d_mixed)
    mlp_out, d_norm_two, begun, terms, g_up_bias = mlp(
        x_mlp, e_mlp, ln2_g, ln2_b, w_up, b_up, w_down, pieces[lax.axis_size("blk") // 2], pieces[1], d_heads
    )

    e_around = around(after(cotangent, begun))
    d_heads = after(d_heads, begun)
    mixed, d_q, kept, sent = attend(ranks, queries, d_heads, kv_all)

    sent, e_around, terms, mlp_out, d_norm_two = after((sent, e_around, terms, mlp_out, d_norm_two))
    total = kept.astype(f32) + swap(sent, "blk", 1).astype(f32)
    g_up, g_down = finish(terms, total)
    d_q = rotate(d_q, cosine, -sine).astype(bf16).reshape(cols, rows)
    mixed = mixed.reshape(cols, rows)
    back_q = to_tokens(after(jnp.concatenate([d_q, mixed]), total))
    step = 1
    while total.shape[0] > 1:
        step *= 2
        sent = swap(total[1::2].astype(bf16), "blk", step)
        total = total[0::2] + sent.astype(f32)
    e_all = jnp.concatenate(e_around, 0)
    g_out = jnp.dot(mixed, e_all, preferred_element_type=f32).astype(bf16)
    d_k = rotate(total[0, :cols].reshape(heads, HEAD, rows), cosine, -sine).reshape(cols, rows)
    d_kv = jnp.concatenate([d_k, total[0, cols:]]).astype(bf16)
    d_joined = jnp.concatenate([d_q, d_kv])
    g_bias_mine = jnp.sum(d_joined.astype(f32), 1)
    g_qkv = jnp.dot(d_joined, normed, preferred_element_type=f32).astype(bf16)
    back_kv = to_tokens(d_kv)
    grads = jnp.concatenate([g_qkv.reshape(3, cols, width), g_out[None]])
    grads = add_blks(grads)
    back_q, back_kv = by_device(back_q, group), by_device(back_kv, group)
    d_mine = jnp.concatenate(
        [v[:cols] for v in back_q] + [v[:cols] for v in back_kv] + [v[cols:] for v in back_kv], 0
    )
    d_norm_one = jnp.einsum("et,de->td", d_mine, w_qkv, preferred_element_type=f32)
    x_float = tokens.astype(f32)
    _, pull_one = jax.vjp(layer_norm, x_float, ln1_g, ln1_b)
    _, pull_two = jax.vjp(layer_norm, x_float, ln2_g, ln2_b)
    d_x_one, g_ln1_g, g_ln1_b = pull_one(d_norm_one)
    d_x_two, g_ln2_g, g_ln2_b = pull_two(d_norm_two)
    e_float = cotangent.astype(f32)

    back = jnp.concatenate([v[cols:] for v in back_q], 0)
    attn_out = jnp.einsum("et,ed->td", back, w_out, preferred_element_type=f32)
    output = (x_float + (attn_out + b_out) + (mlp_out + b_down)).astype(bf16)
    input_grad = (e_float + d_x_one + d_x_two).astype(bf16)

    g_qkv_bias = jnp.zeros((3, groups, cols), f32)
    g_qkv_bias = lax.dynamic_update_slice(g_qkv_bias, g_bias_mine.reshape(3, 1, cols), (0, group, 0))
    vectors = [g_ln1_g, g_ln1_b, g_ln2_g, g_ln2_b, jnp.sum(e_float, 0), g_qkv_bias.reshape(-1), g_up_bias]
    g_qkv, g_out, summed = attention_grads(grads, jnp.concatenate(vectors))
    results, start = [], 0
    for vector in vectors:
        mine = vector.shape[0] // shards
        results.append(lax.dynamic_slice_in_dim(summed, start + lax.axis_index("fsdp") * mine, mine))
        start += vector.shape[0]
    g_ln1_g, g_ln1_b, g_ln2_g, g_ln2_b, g_e, g_qkv_bias, g_up_bias = results
    return (
        output,
        input_grad,
        g_ln1_g,
        g_ln1_b,
        g_ln2_g,
        g_ln2_b,
        g_qkv,
        g_qkv_bias,
        g_out,
        g_e,
        g_up,
        g_up_bias,
        g_down,
        g_e,
    )


def solution(mesh):
    rows = P(("fsdp", "blk", "ulysses"), None)
    split, matrix = P("fsdp"), P("fsdp", None)
    return jax.shard_map(
        on_device,
        mesh=mesh,
        in_specs=(
            rows,
            P(("fsdp", "blk", "ulysses")),
            rows,
            split,
            split,
            split,
            split,
            matrix,
            split,
            matrix,
            split,
            matrix,
            split,
            matrix,
            split,
        ),
        out_specs=(
            rows,
            rows,
            split,
            split,
            split,
            split,
            matrix,
            split,
            matrix,
            split,
            matrix,
            split,
            matrix,
            split,
        ),
        check_vma=False,
    )
```

profile of v0, /device:TPU:9, one launch (start us, length us, event | category | flops | bytes accessed | tf_op | source)
XLA Modules:
  0.0 331.4 jit_solution(18247708735535616015)
XLA Ops:
  9.3 3.2 broadcast_select_fusion.10
  23.0 7.8 %collective-permute-done.10 = bf16[96,2304]{1,0:T(8,128)(2,1)} collective-permute-done((bf16[96,2304]{1,0:T(8,128)(2,1)}, bf16[96,2304]{1,0:T(8,128)(2,1)}, u32[]{:S(2)}, u32[]{:S(2)}) %collective-permute-start.10) | collective-permute-done | bytes 442400 | tf_op jit(solution)/shard_map/ppermute | solution.py:32
  32.5 7.9 %collective-permute-done.11 = bf16[96,2304]{1,0:T(8,128)(2,1)} collective-permute-done((bf16[96,2304]{1,0:T(8,128)(2,1)}, bf16[96,2304]{1,0:T(8,128)(2,1)}, u32[]{:S(2)}, u32[]{:S(2)}) %collective-permute-start.11) | collective-permute-done | bytes 442400 | tf_op jit(solution)/shard_map/ppermute | solution.py:32
  43.9 3.7 %collective-permute-start.3 = (bf16[192,2304]{1,0:T(8,128)(2,1)}, bf16[192,2304]{1,0:T(8,128)(2,1)}, u32[]{:S(2)}, u32[]{:S(2)}) collective-permute-start(bf16[192,2304]{1,0:T(8,128)(2,1)} %pad_maximum_fusion.13), channel_id=1, source_target_pairs={{0,4},{4,0},{8,12},{12,8},{1,5},{5,1},{9,13},{13,9},{2,6},{6,2},{1... | collective-permute-start | bytes 2654216 | tf_op jit(solution)/shard_map/ppermute | solution.py:32
  49.1 3.4 %collective-permute-start.12 = (bf16[192,2304]{1,0:T(8,128)(2,1)S(1)}, bf16[192,2304]{1,0:T(8,128)(2,1)S(1)}, u32[]{:S(2)}, u32[]{:S(2)}) collective-permute-start(bf16[192,2304]{1,0:T(8,128)(2,1)S(1)} %pad_maximum_fusion.14), channel_id=1, source_target_pairs={{0,4},{4,0},{8,12},{12,8},{1,5},{5,1},{9,13},{13,9},{2,6},{6,2},{1... | collective-permute-start | bytes 2654216 | tf_op jit(solution)/shard_map/ppermute | solution.py:32
  58.7 3.5 %prepare.1 = (bf16[1024,768]{1,0:T(8,128)(2,1)S(1)}, bf16[192,1024]{1,0:T(8,128)(2,1)S(1)}, bf16[400,1024]{1,0:T(8,128)(2,1)S(1)}, f32[8,1024]{1,0:T(8,128)S(1)}, f32[8,1024]{1,0:T(8,128)S(1)}) custom-call(f32[8,1]{1,0:T(8,128)S(1)} %copy-done.6, f32[1,768]{1,0:T(1,128)S(1)} %bitcast.78, f32[1,768]{1,0:T(1,128)S(1)} %bitcast.77, ...), custom_call_target="tpu_custom_call" | custom-call | flops 905969664 | bytes 6291456 | tf_op jit(solution)/shard_map/prepare/pallas_call | solution.py:301
  70.8 8.1 %multiply_convert_fusion = (bf16[512,1536]{1,0:T(8,128)(2,1)S(1)}, f32[512,1536]{1,0:T(8,128)S(1)}, f32[512,1536]{1,0:T(8,128)S(1)}) fusion(f32[1536]{0:T(1024)S(1)} %convert_element_type.278, bf16[768,1536]{1,0:T(8,128)(2,1)S(1)} %pad_maximum_fusion.3, bf16[512,768]{1,0:T(8,128)(2,1)S(1)} %pad_maximum_fusion.16, f32[768]{0:T(1024)S(1)} %reshape.221, ...), kind=kOutput, calls=%fused_computation.19 | convolution fusion | flops 1262223360 | bytes 11026432 | tf_op jit(solution)/shard_map/dot_general | solution.py:348
  92.1 7.2 %collective-permute-done.23 = bf16[256,768]{1,0:T(8,128)(2,1)S(1)} collective-permute-done((bf16[256,768]{1,0:T(8,128)(2,1)S(1)}, bf16[256,768]{1,0:T(8,128)(2,1)S(1)}, u32[]{:S(2)}, u32[]{:S(2)}) %collective-permute-start.23) | collective-permute-done | bytes 393248 | tf_op jit(solution)/shard_map/ppermute | solution.py:32
  99.4 8.3 %collective-permute-done.22 = bf16[256,768]{1,0:T(8,128)(2,1)S(1)} collective-permute-done((bf16[256,768]{1,0:T(8,128)(2,1)S(1)}, bf16[256,768]{1,0:T(8,128)(2,1)S(1)}, u32[]{:S(2)}, u32[]{:S(2)}) %collective-permute-start.22) | collective-permute-done | bytes 393248 | tf_op jit(solution)/shard_map/ppermute | solution.py:32
  114.1 40.0 %attend.1 = (bf16[3,64,1024]{2,1,0:T(8,128)(2,1)}, f32[3,64,1024]{2,1,0:T(8,128)}, bf16[2,384,1024]{2,1,0:T(8,128)(2,1)}, bf16[2,384,1024]{2,1,0:T(8,128)(2,1)}) custom-call(s32[32]{0:T(128)} %maximum_convert_fusion.5.rank, bf16[3,64,1024]{2,1,0:T(8,128)(2,1)} %bitcast.79, bf16[3,64,1024]{2,1,0:T(8,128)(2,1)} %bitcast.96, bf16[400,1024]{1,0:T(8,128)(2,1)} %copy-done.4, ...), custom_call_target="tpu_custom_call" | custom-call | flops 38654705664 | bytes 12582912 | tf_op jit(solution)/shard_map/attend/pallas_call | solution.py:224
  155.2 3.2 collective-permute-done.24
  158.4 4.2 %convert_add_fusion.1 = f32[2,384,1024]{2,1,0:T(8,128)} fusion(bf16[2,384,1024]{2,1,0:T(8,128)(2,1)} %collective-permute-done.24, bf16[2,384,1024]{2,1,0:T(8,128)(2,1)} %get-tuple-element.70), kind=kLoop, calls=%fused_computation.17 | loop fusion | flops 2359296 | bytes 6291456 | tf_op jit(solution)/shard_map/add | solution.py:626
  166.9 7.0 %collective-permute-start.28 = (bf16[1,384,1024]{2,1,0:T(8,128)(2,1)S(1)}, bf16[1,384,1024]{2,1,0:T(8,128)(2,1)S(1)}, u32[]{:S(2)}, u32[]{:S(2)}) collective-permute-start(bf16[1,384,1024]{2,1,0:T(8,128)(2,1)S(1)} %slice.646), channel_id=1, source_target_pairs={{0,8},{4,12},{8,0},{12,4},{1,9},{5,13},{9,1},{13,5},{2,10},{6,14},... | collective-permute-start | bytes 2359304 | tf_op jit(solution)/shard_map/ppermute | solution.py:32
  183.8 7.7 %collective-permute-done.28 = bf16[1,384,1024]{2,1,0:T(8,128)(2,1)S(1)} collective-permute-done((bf16[1,384,1024]{2,1,0:T(8,128)(2,1)S(1)}, bf16[1,384,1024]{2,1,0:T(8,128)(2,1)S(1)}, u32[]{:S(2)}, u32[]{:S(2)}) %collective-permute-start.28) | collective-permute-done | bytes 786464 | tf_op jit(solution)/shard_map/ppermute | solution.py:32
  213.2 3.1 collective-permute-start.32
  216.3 8.4 %collective-permute-done.25 = bf16[384,256]{1,0:T(8,128)(2,1)S(1)} collective-permute-done((bf16[384,256]{1,0:T(8,128)(2,1)S(1)}, bf16[384,256]{1,0:T(8,128)(2,1)S(1)}, u32[]{:S(2)}, u32[]{:S(2)}) %collective-permute-start.25) | collective-permute-done | bytes 196640 | tf_op jit(solution)/shard_map/ppermute | solution.py:32
  227.7 4.6 %collective-permute-done.29 = bf16[384,256]{1,0:T(8,128)(2,1)S(1)} collective-permute-done((bf16[384,256]{1,0:T(8,128)(2,1)S(1)}, bf16[384,256]{1,0:T(8,128)(2,1)S(1)}, u32[]{:S(2)}, u32[]{:S(2)}) %collective-permute-start.29) | collective-permute-done | bytes 196640 | tf_op jit(solution)/shard_map/ppermute | solution.py:32
  232.2 7.3 %collective-permute-done.30 = bf16[384,256]{1,0:T(8,128)(2,1)S(1)} collective-permute-done((bf16[384,256]{1,0:T(8,128)(2,1)S(1)}, bf16[384,256]{1,0:T(8,128)(2,1)S(1)}, u32[]{:S(2)}, u32[]{:S(2)}) %collective-permute-start.30) | collective-permute-done | bytes 196640 | tf_op jit(solution)/shard_map/ppermute | solution.py:32
  246.6 4.4 %collective-permute-start.33 = (bf16[4,48,768]{2,1,0:T(8,128)(2,1)S(1)}, bf16[4,48,768]{2,1,0:T(8,128)(2,1)S(1)}, u32[]{:S(2)}, u32[]{:S(2)}) collective-permute-start(bf16[4,48,768]{2,1,0:T(8,128)(2,1)S(1)} %broadcast_select_fusion.28), channel_id=1, source_target_pairs={{0,8},{4,12},{8,0},{12,4},{1,9},{5,13},{9,1},{13,5},{2,10},{6,14},... | collective-permute-start | bytes 884744 | tf_op jit(solution)/shard_map/ppermute | solution.py:32
  253.2 4.7 %collective-permute-done.33 = bf16[4,48,768]{2,1,0:T(8,128)(2,1)S(1)} collective-permute-done((bf16[4,48,768]{2,1,0:T(8,128)(2,1)S(1)}, bf16[4,48,768]{2,1,0:T(8,128)(2,1)S(1)}, u32[]{:S(2)}, u32[]{:S(2)}) %collective-permute-start.33) | collective-permute-done | bytes 294944 | tf_op jit(solution)/shard_map/ppermute | solution.py:32
  259.7 4.4 %collective-permute-done.34 = bf16[6,48,384]{2,1,0:T(8,128)(2,1)S(1)} collective-permute-done((bf16[6,48,384]{2,1,0:T(8,128)(2,1)S(1)}, bf16[6,48,384]{2,1,0:T(8,128)(2,1)S(1)}, u32[]{:S(2)}, u32[]{:S(2)}) %collective-permute-start.34) | collective-permute-done | bytes 221216 | tf_op jit(solution)/shard_map/ppermute | solution.py:32
  264.2 3.2 collective-permute-start.36
  268.8 3.6 %collective-permute-done.37 = bf16[6,48,384]{2,1,0:T(8,128)(2,1)S(1)} collective-permute-done((bf16[6,48,384]{2,1,0:T(8,128)(2,1)S(1)}, bf16[6,48,384]{2,1,0:T(8,128)(2,1)S(1)}, u32[]{:S(2)}, u32[]{:S(2)}) %collective-permute-start.37) | collective-permute-done | bytes 221216 | tf_op jit(solution)/shard_map/ppermute | solution.py:32
  272.4 4.6 %collective-permute-done.36 = bf16[6,48,384]{2,1,0:T(8,128)(2,1)S(1)} collective-permute-done((bf16[6,48,384]{2,1,0:T(8,128)(2,1)S(1)}, bf16[6,48,384]{2,1,0:T(8,128)(2,1)S(1)}, u32[]{:S(2)}, u32[]{:S(2)}) %collective-permute-start.36) | collective-permute-done | bytes 221216 | tf_op jit(solution)/shard_map/ppermute | solution.py:32
  277.0 8.3 %collective-permute-done.35 = bf16[6,48,384]{2,1,0:T(8,128)(2,1)S(1)} collective-permute-done((bf16[6,48,384]{2,1,0:T(8,128)(2,1)S(1)}, bf16[6,48,384]{2,1,0:T(8,128)(2,1)S(1)}, u32[]{:S(2)}, u32[]{:S(2)}) %collective-permute-start.35) | collective-permute-done | bytes 221216 | tf_op jit(solution)/shard_map/ppermute | solution.py:32
  286.8 6.1 %collective-permute-done.45 = bf16[4,192,768]{2,1,0:T(8,128)(2,1)S(1)} collective-permute-done((bf16[4,192,768]{2,1,0:T(8,128)(2,1)S(1)}, bf16[4,192,768]{2,1,0:T(8,128)(2,1)S(1)}, u32[]{:S(2)}, u32[]{:S(2)}) %collective-permute-start.45) | collective-permute-done | bytes 1179680 | tf_op jit(solution)/shard_map/ppermute | solution.py:32
  294.9 6.5 %collective-permute-start.46 = (bf16[4,384,768]{2,1,0:T(8,128)(2,1)}, bf16[4,384,768]{2,1,0:T(8,128)(2,1)}, u32[]{:S(2)}, u32[]{:S(2)}) collective-permute-start(bf16[4,384,768]{2,1,0:T(8,128)(2,1)} %pad_maximum_fusion.4.mine), channel_id=1, source_target_pairs={{0,4},{4,0},{8,12},{12,8},{1,5},{5,1},{9,13},{13,9},{2,6},{6,2},{1... | collective-permute-start | bytes 7077896 | tf_op jit(solution)/shard_map/ppermute | solution.py:32
  301.4 4.9 %collective-permute-done.38 = bf16[17,48,384]{2,1,0:T(8,128)(2,1)S(1)} collective-permute-done((bf16[17,48,384]{2,1,0:T(8,128)(2,1)S(1)}, bf16[17,48,384]{2,1,0:T(8,128)(2,1)S(1)}, u32[]{:S(2)}, u32[]{:S(2)}) %collective-permute-start.38) | collective-permute-done | bytes 626720 | tf_op jit(solution)/shard_map/ppermute | solution.py:32
  308.5 3.5 %collective-permute-start.39 = (bf16[17,96,384]{2,1,0:T(8,128)(2,1)}, bf16[17,96,384]{2,1,0:T(8,128)(2,1)S(1)}, u32[]{:S(2)}, u32[]{:S(2)}) collective-permute-start(bf16[17,96,384]{2,1,0:T(8,128)(2,1)} %fusion.27), channel_id=1, source_target_pairs={{0,4},{4,0},{8,12},{12,8},{1,5},{5,1},{9,13},{13,9},{2,6},{6,2},{1... | collective-permute-start | bytes 3760136 | tf_op jit(solution)/shard_map/ppermute | solution.py:32
  312.6 2.9 add_convert_fusion.5
  321.4 2.8 place_qkv.1
  324.2 6.4 %place_mlp.1 = (f32[384,3072]{1,0:T(8,128)}, f32[2,2,384,768]{3,2,1,0:T(8,128)}) custom-call(s32[1]{0:T(128)} %bitcast.24.which, bf16[4,384,768]{2,1,0:T(8,128)(2,1)} %pad_maximum_fusion.4.mine, bf16[4,384,768]{2,1,0:T(8,128)(2,1)} %collective-permute-done.46.other), custom_call_target="tpu_custom_call" | custom-call | bytes 14155776 | tf_op jit(solution)/shard_map/place_mlp/pallas_call | solution.py:399
  (372 shorter events, 124.1 us)
Async XLA Ops:
  2.6 55.7 %collective-permute-start.6 = (bf16[272,768]{1,0:T(8,128)(2,1)S(1)}, bf16[272,768]{1,0:T(8,128)(2,1)S(1)}, u32[]{:S(2)}, u32[]{:S(2)}) collective-permute-start(bf16[272,768]{1,0:T(8,128)(2,1)S(1)} %fusion.52.refs_0_), channel_id=1, source_target_pairs={{0,3},{1,2},{2,1},{3,0},{4,7},{5,6},{6,5},{7,4},{8,11},{9,10},{10,... | collective-permute-start | bytes 1253384 | tf_op jit(solution)/shard_map/ppermute | solution.py:32
  4.0 54.4 %collective-permute-start.5 = (bf16[272,768]{1,0:T(8,128)(2,1)S(1)}, bf16[272,768]{1,0:T(8,128)(2,1)}, u32[]{:S(2)}, u32[]{:S(2)}) collective-permute-start(bf16[272,768]{1,0:T(8,128)(2,1)S(1)} %fusion.52.refs_0_), channel_id=1, source_target_pairs={{0,2},{1,3},{2,0},{3,1},{4,6},{5,7},{6,4},{7,5},{8,10},{9,11},{10,... | collective-permute-start | bytes 1253384 | tf_op jit(solution)/shard_map/ppermute | solution.py:32
  5.1 53.3 %collective-permute-start.4 = (bf16[272,768]{1,0:T(8,128)(2,1)S(1)}, bf16[272,768]{1,0:T(8,128)(2,1)}, u32[]{:S(2)}, u32[]{:S(2)}) collective-permute-start(bf16[272,768]{1,0:T(8,128)(2,1)S(1)} %fusion.52.refs_0_), channel_id=1, source_target_pairs={{0,1},{1,0},{2,3},{3,2},{4,5},{5,4},{6,7},{7,6},{8,9},{9,8},{10,11... | collective-permute-start | bytes 1253384 | tf_op jit(solution)/shard_map/ppermute | solution.py:32
  32.2 16.9 %collective-permute-start.16 = (bf16[2,256,768]{2,1,0:T(8,128)(2,1)}, bf16[2,256,768]{2,1,0:T(8,128)(2,1)}, u32[]{:S(2)}, u32[]{:S(2)}) collective-permute-start(bf16[2,256,768]{2,1,0:T(8,128)(2,1)} %pad_maximum_fusion.15), channel_id=1, source_target_pairs={{0,16},{16,0},{1,17},{17,1},{2,18},{18,2},{3,19},{19,3},{4,20},{20... | collective-permute-start | bytes 2359304 | tf_op jit(solution)/shard_map/ppermute | solution.py:32
  49.1 13.8 %collective-permute-start.12 = (bf16[192,2304]{1,0:T(8,128)(2,1)S(1)}, bf16[192,2304]{1,0:T(8,128)(2,1)S(1)}, u32[]{:S(2)}, u32[]{:S(2)}) collective-permute-start(bf16[192,2304]{1,0:T(8,128)(2,1)S(1)} %pad_maximum_fusion.14), channel_id=1, source_target_pairs={{0,4},{4,0},{8,12},{12,8},{1,5},{5,1},{9,13},{13,9},{2,6},{6,2},{1... | collective-permute-start | bytes 2654216 | tf_op jit(solution)/shard_map/ppermute | solution.py:32
  62.3 19.9 %collective-permute-start.8 = (bf16[400,1024]{1,0:T(8,128)(2,1)S(1)}, bf16[400,1024]{1,0:T(8,128)(2,1)S(1)}, u32[]{:S(2)}, u32[]{:S(2)}) collective-permute-start(bf16[400,1024]{1,0:T(8,128)(2,1)S(1)} %get-tuple-element.56.refs_0_), channel_id=1, source_target_pairs={{0,8},{4,12},{8,0},{12,4},{1,9},{5,13},{9,1},{13,5},{2,10},{6,14},... | collective-permute-start | bytes 2457608 | tf_op jit(solution)/shard_map/ppermute | solution.py:32
  62.6 19.6 %collective-permute-start.7 = (bf16[400,1024]{1,0:T(8,128)(2,1)S(1)}, bf16[400,1024]{1,0:T(8,128)(2,1)S(1)}, u32[]{:S(2)}, u32[]{:S(2)}) collective-permute-start(bf16[400,1024]{1,0:T(8,128)(2,1)S(1)} %get-tuple-element.56.refs_0_), channel_id=1, source_target_pairs={{0,4},{4,0},{8,12},{12,8},{1,5},{5,1},{9,13},{13,9},{2,6},{6,2},{1... | collective-permute-start | bytes 2457608 | tf_op jit(solution)/shard_map/ppermute | solution.py:32
  67.2 14.1 %collective-permute-start.15 = (bf16[192,256]{1,0:T(8,128)(2,1)S(1)}, bf16[192,256]{1,0:T(8,128)(2,1)S(1)}, u32[]{:S(2)}, u32[]{:S(2)}) collective-permute-start(bf16[192,256]{1,0:T(8,128)(2,1)S(1)} %get-tuple-element.165), channel_id=1, source_target_pairs={{0,3},{1,2},{2,1},{3,0},{4,7},{5,6},{6,5},{7,4},{8,11},{9,10},{10,... | collective-permute-start | bytes 294920 | tf_op jit(solution)/shard_map/ppermute | solution.py:32
  86.2 23.3 %collective-permute-start.17 = (bf16[2,2,384,768]{3,2,1,0:T(8,128)(2,1)S(1)}, bf16[2,2,384,768]{3,2,1,0:T(8,128)(2,1)S(1)}, u32[]{:S(2)}, u32[]{:S(2)}) collective-permute-start(bf16[2,2,384,768]{3,2,1,0:T(8,128)(2,1)S(1)} %bitcast.92), channel_id=1, source_target_pairs={{0,4},{4,0},{8,12},{12,8},{1,5},{5,1},{9,13},{13,9},{2,6},{6,2},{1... | collective-permute-start | bytes 7077896 | tf_op jit(solution)/shard_map/ppermute | solution.py:32
  90.2 17.5 %collective-permute-start.22 = (bf16[256,768]{1,0:T(8,128)(2,1)S(1)}, bf16[256,768]{1,0:T(8,128)(2,1)S(1)}, u32[]{:S(2)}, u32[]{:S(2)}) collective-permute-start(bf16[256,768]{1,0:T(8,128)(2,1)S(1)} %slice.648), channel_id=1, source_target_pairs={{0,16},{16,0},{1,17},{17,1},{2,18},{18,2},{3,19},{19,3},{4,20},{20... | collective-permute-start | bytes 1179656 | tf_op jit(solution)/shard_map/ppermute | solution.py:32
  91.5 17.2 %collective-permute-start.9 = (bf16[400,1024]{1,0:T(8,128)(2,1)S(1)}, bf16[400,1024]{1,0:T(8,128)(2,1)S(1)}, u32[]{:S(2)}, u32[]{:S(2)}) collective-permute-start(bf16[400,1024]{1,0:T(8,128)(2,1)S(1)} %collective-permute-done.8.refs_2_), channel_id=1, source_target_pairs={{0,4},{4,0},{8,12},{12,8},{1,5},{5,1},{9,13},{13,9},{2,6},{6,2},{1... | collective-permute-start | bytes 2457608 | tf_op jit(solution)/shard_map/ppermute | solution.py:32
  110.0 44.5 %collective-permute-start.20 = (bf16[256,768]{1,0:T(8,128)(2,1)S(1)}, bf16[256,768]{1,0:T(8,128)(2,1)S(1)}, u32[]{:S(2)}, u32[]{:S(2)}) collective-permute-start(bf16[256,768]{1,0:T(8,128)(2,1)S(1)} %copy-done.23), channel_id=1, source_target_pairs={{0,3},{1,2},{2,1},{3,0},{4,7},{5,6},{6,5},{7,4},{8,11},{9,10},{10,... | collective-permute-start | bytes 1179656 | tf_op jit(solution)/shard_map/ppermute | solution.py:32
  111.3 43.2 %collective-permute-start.19 = (bf16[256,768]{1,0:T(8,128)(2,1)S(1)}, bf16[256,768]{1,0:T(8,128)(2,1)}, u32[]{:S(2)}, u32[]{:S(2)}) collective-permute-start(bf16[256,768]{1,0:T(8,128)(2,1)S(1)} %copy-done.23), channel_id=1, source_target_pairs={{0,2},{1,3},{2,0},{3,1},{4,6},{5,7},{6,4},{7,5},{8,10},{9,11},{10,... | collective-permute-start | bytes 1179656 | tf_op jit(solution)/shard_map/ppermute | solution.py:32
  112.8 41.7 %collective-permute-start.18 = (bf16[256,768]{1,0:T(8,128)(2,1)S(1)}, bf16[256,768]{1,0:T(8,128)(2,1)}, u32[]{:S(2)}, u32[]{:S(2)}) collective-permute-start(bf16[256,768]{1,0:T(8,128)(2,1)S(1)} %copy-done.23), channel_id=1, source_target_pairs={{0,1},{1,0},{2,3},{3,2},{4,5},{5,4},{6,7},{7,6},{8,9},{9,8},{10,11... | collective-permute-start | bytes 1179656 | tf_op jit(solution)/shard_map/ppermute | solution.py:32
  113.8 40.3 %collective-permute-start.21 = (bf16[2,2,192,768]{3,2,1,0:T(8,128)(2,1)S(1)}, bf16[2,2,192,768]{3,2,1,0:T(8,128)(2,1)S(1)}, u32[]{:S(2)}, u32[]{:S(2)}) collective-permute-start(bf16[2,2,192,768]{3,2,1,0:T(8,128)(2,1)S(1)} %broadcast_select_fusion.8), channel_id=1, source_target_pairs={{0,8},{4,12},{8,0},{12,4},{1,9},{5,13},{9,1},{13,5},{2,10},{6,14},... | collective-permute-start | bytes 3538952 | tf_op jit(solution)/shard_map/ppermute | solution.py:32
  163.4 15.1 %collective-permute-start.40 = (bf16[2,2,96,768]{3,2,1,0:T(8,128)(2,1)}, bf16[2,2,96,768]{3,2,1,0:T(8,128)(2,1)}, u32[]{:S(2)}, u32[]{:S(2)}) collective-permute-start(bf16[2,2,96,768]{3,2,1,0:T(8,128)(2,1)} %broadcast_select_fusion.15), channel_id=1, source_target_pairs={{0,1},{1,0},{2,3},{3,2},{4,5},{5,4},{6,7},{7,6},{8,9},{9,8},{10,11... | collective-permute-start | bytes 1769480 | tf_op jit(solution)/shard_map/ppermute | solution.py:32
  166.9 24.6 %collective-permute-start.28 = (bf16[1,384,1024]{2,1,0:T(8,128)(2,1)S(1)}, bf16[1,384,1024]{2,1,0:T(8,128)(2,1)S(1)}, u32[]{:S(2)}, u32[]{:S(2)}) collective-permute-start(bf16[1,384,1024]{2,1,0:T(8,128)(2,1)S(1)} %slice.646), channel_id=1, source_target_pairs={{0,8},{4,12},{8,0},{12,4},{1,9},{5,13},{9,1},{13,5},{2,10},{6,14},... | collective-permute-start | bytes 2359304 | tf_op jit(solution)/shard_map/ppermute | solution.py:32
  181.5 23.3 %collective-permute-start.41 = (bf16[2,2,48,768]{3,2,1,0:T(8,128)(2,1)}, bf16[2,2,48,768]{3,2,1,0:T(8,128)(2,1)}, u32[]{:S(2)}, u32[]{:S(2)}) collective-permute-start(bf16[2,2,48,768]{3,2,1,0:T(8,128)(2,1)} %broadcast_select_fusion.25), channel_id=1, source_target_pairs={{0,2},{1,3},{2,0},{3,1},{4,6},{5,7},{6,4},{7,5},{8,10},{9,11},{10,... | collective-permute-start | bytes 884744 | tf_op jit(solution)/shard_map/ppermute | solution.py:32
  197.2 14.7 %collective-permute-start.27 = (bf16[384,256]{1,0:T(8,128)(2,1)S(1)}, bf16[384,256]{1,0:T(8,128)(2,1)S(1)}, u32[]{:S(2)}, u32[]{:S(2)}) collective-permute-start(bf16[384,256]{1,0:T(8,128)(2,1)S(1)} %get-tuple-element.150), channel_id=1, source_target_pairs={{0,1},{1,0},{2,3},{3,2},{4,5},{5,4},{6,7},{7,6},{8,9},{9,8},{10,11... | collective-permute-start | bytes 589832 | tf_op jit(solution)/shard_map/ppermute | solution.py:32
  197.9 15.3 %collective-permute-start.26 = (bf16[384,256]{1,0:T(8,128)(2,1)S(1)}, bf16[384,256]{1,0:T(8,128)(2,1)S(1)}, u32[]{:S(2)}, u32[]{:S(2)}) collective-permute-start(bf16[384,256]{1,0:T(8,128)(2,1)S(1)} %get-tuple-element.151), channel_id=1, source_target_pairs={{0,2},{1,3},{2,0},{3,1},{4,6},{5,7},{6,4},{7,5},{8,10},{9,11},{10,... | collective-permute-start | bytes 589832 | tf_op jit(solution)/shard_map/ppermute | solution.py:32
  200.3 24.3 %collective-permute-start.25 = (bf16[384,256]{1,0:T(8,128)(2,1)S(1)}, bf16[384,256]{1,0:T(8,128)(2,1)S(1)}, u32[]{:S(2)}, u32[]{:S(2)}) collective-permute-start(bf16[384,256]{1,0:T(8,128)(2,1)S(1)} %get-tuple-element.152), channel_id=1, source_target_pairs={{0,3},{1,2},{2,1},{3,0},{4,7},{5,6},{6,5},{7,4},{8,11},{9,10},{10,... | collective-permute-start | bytes 589832 | tf_op jit(solution)/shard_map/ppermute | solution.py:32
  200.3 27.4 %collective-permute-start.31 = (bf16[384,256]{1,0:T(8,128)(2,1)}, bf16[384,256]{1,0:T(8,128)(2,1)S(1)}, u32[]{:S(2)}, u32[]{:S(2)}) collective-permute-start(bf16[384,256]{1,0:T(8,128)(2,1)} %get-tuple-element.147), channel_id=1, source_target_pairs={{0,1},{1,0},{2,3},{3,2},{4,5},{5,4},{6,7},{7,6},{8,9},{9,8},{10,11... | collective-permute-start | bytes 589832 | tf_op jit(solution)/shard_map/ppermute | solution.py:32
  210.0 22.2 %collective-permute-start.29 = (bf16[384,256]{1,0:T(8,128)(2,1)S(1)}, bf16[384,256]{1,0:T(8,128)(2,1)S(1)}, u32[]{:S(2)}, u32[]{:S(2)}) collective-permute-start(bf16[384,256]{1,0:T(8,128)(2,1)S(1)} %copy-done.53), channel_id=1, source_target_pairs={{0,3},{1,2},{2,1},{3,0},{4,7},{5,6},{6,5},{7,4},{8,11},{9,10},{10,... | collective-permute-start | bytes 589832 | tf_op jit(solution)/shard_map/ppermute | solution.py:32
  211.9 27.6 %collective-permute-start.30 = (bf16[384,256]{1,0:T(8,128)(2,1)S(1)}, bf16[384,256]{1,0:T(8,128)(2,1)S(1)}, u32[]{:S(2)}, u32[]{:S(2)}) collective-permute-start(bf16[384,256]{1,0:T(8,128)(2,1)S(1)} %copy-done.52), channel_id=1, source_target_pairs={{0,2},{1,3},{2,0},{3,1},{4,6},{5,7},{6,4},{7,5},{8,10},{9,11},{10,... | collective-permute-start | bytes 589832 | tf_op jit(solution)/shard_map/ppermute | solution.py:32
  213.2 33.1 %collective-permute-start.32 = (bf16[4,96,768]{2,1,0:T(8,128)(2,1)}, bf16[4,96,768]{2,1,0:T(8,128)(2,1)S(1)}, u32[]{:S(2)}, u32[]{:S(2)}) collective-permute-start(bf16[4,96,768]{2,1,0:T(8,128)(2,1)} %broadcast_select_fusion.20), channel_id=1, source_target_pairs={{0,4},{4,0},{8,12},{12,8},{1,5},{5,1},{9,13},{13,9},{2,6},{6,2},{1... | collective-permute-start | bytes 1769480 | tf_op jit(solution)/shard_map/ppermute | solution.py:32
  224.6 26.4 %collective-permute-start.43 = (bf16[4,48,768]{2,1,0:T(8,128)(2,1)}, bf16[4,48,768]{2,1,0:T(8,128)(2,1)}, u32[]{:S(2)}, u32[]{:S(2)}) collective-permute-start(bf16[4,48,768]{2,1,0:T(8,128)(2,1)} %pad_maximum_fusion.29), channel_id=1, source_target_pairs={{0,2},{1,3},{2,0},{3,1},{4,6},{5,7},{6,4},{7,5},{8,10},{9,11},{10,... | collective-permute-start | bytes 884744 | tf_op jit(solution)/shard_map/ppermute | solution.py:32
  252.1 15.5 %collective-permute-start.44 = (bf16[4,96,768]{2,1,0:T(8,128)(2,1)S(1)}, bf16[4,96,768]{2,1,0:T(8,128)(2,1)S(1)}, u32[]{:S(2)}, u32[]{:S(2)}) collective-permute-start(bf16[4,96,768]{2,1,0:T(8,128)(2,1)S(1)} %pad_maximum_fusion.20), channel_id=1, source_target_pairs={{0,1},{1,0},{2,3},{3,2},{4,5},{5,4},{6,7},{7,6},{8,9},{9,8},{10,11... | collective-permute-start | bytes 1769480 | tf_op jit(solution)/shard_map/ppermute | solution.py:32
  264.2 12.8 %collective-permute-start.36 = (bf16[6,48,384]{2,1,0:T(8,128)(2,1)S(1)}, bf16[6,48,384]{2,1,0:T(8,128)(2,1)S(1)}, u32[]{:S(2)}, u32[]{:S(2)}) collective-permute-start(bf16[6,48,384]{2,1,0:T(8,128)(2,1)S(1)} %add_convert_fusion.8), channel_id=1, source_target_pairs={{0,2},{1,3},{2,0},{3,1},{4,6},{5,7},{6,4},{7,5},{8,10},{9,11},{10,... | collective-permute-start | bytes 663560 | tf_op jit(solution)/shard_map/ppermute | solution.py:32
  267.4 18.0 %collective-permute-start.35 = (bf16[6,48,384]{2,1,0:T(8,128)(2,1)S(1)}, bf16[6,48,384]{2,1,0:T(8,128)(2,1)S(1)}, u32[]{:S(2)}, u32[]{:S(2)}) collective-permute-start(bf16[6,48,384]{2,1,0:T(8,128)(2,1)S(1)} %add_convert_fusion.8), channel_id=1, source_target_pairs={{0,3},{1,2},{2,1},{3,0},{4,7},{5,6},{6,5},{7,4},{8,11},{9,10},{10,... | collective-permute-start | bytes 663560 | tf_op jit(solution)/shard_map/ppermute | solution.py:32
  267.9 25.0 %collective-permute-start.45 = (bf16[4,192,768]{2,1,0:T(8,128)(2,1)S(1)}, bf16[4,192,768]{2,1,0:T(8,128)(2,1)S(1)}, u32[]{:S(2)}, u32[]{:S(2)}) collective-permute-start(bf16[4,192,768]{2,1,0:T(8,128)(2,1)S(1)} %pad_maximum_fusion.11), channel_id=1, source_target_pairs={{0,8},{4,12},{8,0},{12,4},{1,9},{5,13},{9,1},{13,5},{2,10},{6,14},... | collective-permute-start | bytes 3538952 | tf_op jit(solution)/shard_map/ppermute | solution.py:32
  285.8 20.5 %collective-permute-start.38 = (bf16[17,48,384]{2,1,0:T(8,128)(2,1)S(1)}, bf16[17,48,384]{2,1,0:T(8,128)(2,1)S(1)}, u32[]{:S(2)}, u32[]{:S(2)}) collective-permute-start(bf16[17,48,384]{2,1,0:T(8,128)(2,1)S(1)} %get-tuple-element.99), channel_id=1, source_target_pairs={{0,8},{4,12},{8,0},{12,4},{1,9},{5,13},{9,1},{13,5},{2,10},{6,14},... | collective-permute-start | bytes 1880072 | tf_op jit(solution)/shard_map/ppermute | solution.py:32
  294.9 29.3 %collective-permute-start.46 = (bf16[4,384,768]{2,1,0:T(8,128)(2,1)}, bf16[4,384,768]{2,1,0:T(8,128)(2,1)}, u32[]{:S(2)}, u32[]{:S(2)}) collective-permute-start(bf16[4,384,768]{2,1,0:T(8,128)(2,1)} %pad_maximum_fusion.4.mine), channel_id=1, source_target_pairs={{0,4},{4,0},{8,12},{12,8},{1,5},{5,1},{9,13},{13,9},{2,6},{6,2},{1... | collective-permute-start | bytes 7077896 | tf_op jit(solution)/shard_map/ppermute | solution.py:32
  (83 other events, 688.7 us)
where the time goes:
time: 337 us; the launch traced here: 331 us
  waiting for transfers between devices  107 us (32%)
  starting transfers between devices  70.8 us (21%)
  Pallas kernels  52.7 us (16%)
  other arithmetic  45.8 us (14%)
  local copies, waits for them, and re-layouts  27.6 us (8%)
  matrix products  25.7 us (8%)
    ppermute x47, waiting for transfers between devices, swap(): return lax.ppermute(values, axis, [(i, i ^ bits) for i in range(count)])  107 us
    ppermute x47, starting transfers between devices, swap(): return lax.ppermute(values, axis, [(i, i ^ bits) for i in range(count)])  70.8 us
    pallas_call x1, Pallas kernels, attend(): pl.pallas_call(attend_kernel, grid_spec=pltpu.PrefetchScalarGridSpec(num_...  40 us
    unnamed x167, local copies, waits for them, and re-layouts  16.5 us
    dot_general x1, matrix products, mlp_pair(): jnp.dot(normed, up, preferred_element_type=f32) + up_bias.astype(f32)  8.13 us
    select_n x10, other arithmetic, in_order(): jnp.where(bit == 0, mine, other)  6.86 us
  transfers between devices with their start and end apart: 47, of which 21 were waited for; matrix products, arithmetic and copies ran while one was open for 23% of the time, Pallas kernels for 14%

commit v1 on v0

--- a/solution.py
+++ b/solution.py
@@ -328,6 +328,10 @@
     return [values] + [swap(values, "ulysses", j) for j in range(1, lax.axis_size("ulysses"))]
 
 
+def stacked_terms(lists):
+    return [jnp.stack(v) for v in zip(*lists)]
+
+
 def to_tokens(values):
     groups = lax.axis_size("ulysses")
     count = values.shape[1] // groups
@@ -349,12 +353,11 @@
     active_f, pull_gelu = jax.vjp(gelu_exact, hidden)
     active = active_f.astype(bf16)
     part = jnp.dot(active, down_weight, preferred_element_type=f32)
-    out = part[:rows] + swap(part[rows:].astype(bf16), "fsdp", 1).astype(f32)
     d_active = jnp.einsum("td,fd->tf", e_both, down_weight, preferred_element_type=f32)
     d_hidden = pull_gelu(d_active)[0].astype(bf16)
     g_up_bias = jnp.sum(d_hidden.astype(f32), 0)
     d_part = jnp.einsum("tf,df->td", d_hidden, up, preferred_element_type=f32)
-    d_normed = d_part[:rows] + swap(d_part[rows:].astype(bf16), "fsdp", 1).astype(f32)
+    sent = jnp.concatenate([part[rows:], d_part[rows:]]).astype(bf16)
     active, d_hidden = after((active, d_hidden), *meanwhile)
     g_up = jnp.einsum(
         "td,tcf->cdf", normed, d_hidden.reshape(2 * rows, 2, units // 2), preferred_element_type=f32
@@ -363,6 +366,8 @@
     g_down = g_down.reshape(2, units // 2, width)
     pieces = jnp.stack([g_up, g_down], 1).reshape(2, 2, 2, width // 2, width)
     first = add_half((pieces[0], pieces[1]), "blk", 1)
+    got = swap(after(sent, first), "fsdp", 1).astype(f32)
+    out, d_normed = part[:rows] + got[:rows], d_part[:rows] + got[rows:]
     sums = add_half(halves_of(first, 2), "blk", 2)
     side, none = lax.axis_index("fsdp"), jnp.zeros_like(g_up_bias)
     g_up_bias = jnp.concatenate([jnp.where(side == 0, g_up_bias, none), jnp.where(side == 0, none, g_up_bias)])
@@ -377,7 +382,10 @@
     got = swap(jnp.where(side == 0, sums[0, 1], sums[0, 0]), "fsdp", 1)
     kept = jnp.where(side == 0, sums[0, 0], sums[0, 1])
     sums = jnp.concatenate([in_order(side, kept[None], got[None]), sums[1]], 0)
-    sums = share_half(sums, "ulysses", 2, 1)
+    return share_half(sums, "ulysses", 2, 1)
+
+
+def spread_pair(sums):
     sums = share_half(sums, "ulysses", 1, 1)
     sums = share_half(sums, "blk", 2, 1)
     return place_mlp(bit_of("blk", 1), sums, swap(sums, "blk", 1))
@@ -488,7 +496,7 @@
     return add_half(halves_of(add_half(halves_of(grads, 1), "blk", 1), 1), "blk", 2)
 
 
-def attention_grads(grads, vector):
+def attention_grads(grads, vector, output, g_up):
     side = lax.axis_index("fsdp")
     group = lax.axis_index("ulysses")
     groups = lax.axis_size("ulysses")
@@ -516,11 +524,11 @@
     of_out = [jnp.where(side == 0, a[3:5], b[3:5]) for a, b in zip(kept[: groups // 2], kept[groups // 2 :])]
     kept = jnp.concatenate([of_qkv] + of_out)
     units = kept.shape[0]
-    got = swap(jnp.concatenate([kept, small]), "blk", 2)
+    got = after(swap(jnp.concatenate([kept, small]), "blk", 2), output)
     kept = in_order(bit_of("blk", 2), kept, got[:units], 1)
     small = (small.astype(f32) + got[units:].astype(f32)).astype(bf16)
     wide = jnp.pad(small, ((0, 0), (0, rows), (0, 0)))
-    got = swap(jnp.concatenate([kept, wide]), "blk", 1)
+    got = after(swap(jnp.concatenate([kept, wide]), "blk", 1), g_up)
     small = small.astype(f32) + got[units:, :rows].astype(f32)
     g_qkv, g_out = place_qkv(bit_of("blk", 1), kept, got)
     return g_qkv, g_out, small.reshape(-1)[:size]
@@ -569,15 +577,17 @@
         half_up = jnp.concatenate([units_of(up_weight, 1 - side), out_weight], 1)
         part_up = swap(after(quarter_of(half_up), part_qkv), "fsdp", 1)
         x_e = swap(after(jnp.stack([tokens, cotangent]), part_up), "fsdp", 1)
-        w_qkv = both_shards(qkv_weight, share_half(part_qkv, "blk", 2, 0))
-        half_up = share_half(part_up, "blk", 2, 0)
+        half_qkv = share_half(part_qkv, "blk", 2, 0)
+        w_qkv = both_shards(qkv_weight, half_qkv)
+        half_up = share_half(after(part_up, half_qkv), "blk", 2, 0)
         x_all = around(x_ranks)
         mine = jnp.concatenate([units_of(up_weight, side), out_weight], 1)
         half_up = both_shards(mine, half_up)
         w_up, w_out = half_up[:, :-width], half_up[:, -width:]
         x_mlp = jnp.concatenate([tokens, x_e[0]])
         e_mlp = jnp.concatenate([cotangent, x_e[1]])
-        b_up, w_down, mlp, finish = up_bias, down_weight, mlp_pair, finish_pair
+        b_up, w_down = up_bias, down_weight
+        mlp, finish, spread = mlp_pair, finish_pair, spread_pair
     else:
         x_all, part_qkv = around(x_ranks), x_ranks
         w_qkv, w_up, w_out, w_down = (
@@ -585,7 +595,8 @@
             for w in (qkv_weight, up_weight, out_weight, down_weight)
         )
         b_up = gather_small(up_bias).reshape(-1)
-        x_mlp, e_mlp, mlp, finish = tokens, cotangent, mlp_gathered, lambda v, _: v
+        x_mlp, e_mlp = tokens, cotangent
+        mlp, finish, spread = mlp_gathered, lambda v, _: v, lambda v: v
     small = jnp.concatenate([ln1_gain, ln1_bias, ln2_gain, ln2_bias, out_bias, down_bias, qkv_bias])
     small = gather_small(after(small, part_qkv))
     part = width // shards
@@ -623,26 +634,30 @@
     mixed, d_q, kept, sent = attend(ranks, queries, d_heads, kv_all)
 
     sent, e_around, terms, mlp_out, d_norm_two = after((sent, e_around, terms, mlp_out, d_norm_two))
-    total = kept.astype(f32) + swap(sent, "blk", 1).astype(f32)
-    g_up, g_down = finish(terms, total)
+    got = swap(sent, "blk", 1)
+    step, kept = 1, [[kept[i], got[i]] for i in range(kept.shape[0])]
+    while len(kept) > 1:
+        step *= 2
+        sent = sum(v.astype(f32) for v in stacked_terms(kept[1::2])).astype(bf16)
+        terms = finish(terms, sent) if step == 2 else terms
+        got = swap(sent, "blk", step)
+        kept = [kept[2 * i] + [got[i]] for i in range(got.shape[0])]
+    total = sum(v.astype(f32) for v in kept[0])
     d_q = rotate(d_q, cosine, -sine).astype(bf16).reshape(cols, rows)
     mixed = mixed.reshape(cols, rows)
-    back_q = to_tokens(after(jnp.concatenate([d_q, mixed]), total))
-    step = 1
-    while total.shape[0] > 1:
-        step *= 2
-        sent = swap(total[1::2].astype(bf16), "blk", step)
-        total = total[0::2] + sent.astype(f32)
+    back_q = to_tokens(after(jnp.concatenate([d_q, mixed]), sent))
     e_all = jnp.concatenate(e_around, 0)
     g_out = jnp.dot(mixed, e_all, preferred_element_type=f32).astype(bf16)
-    d_k = rotate(total[0, :cols].reshape(heads, HEAD, rows), cosine, -sine).reshape(cols, rows)
-    d_kv = jnp.concatenate([d_k, total[0, cols:]]).astype(bf16)
+    d_k = rotate(total[:cols].reshape(heads, HEAD, rows), cosine, -sine).reshape(cols, rows)
+    d_kv = jnp.concatenate([d_k, total[cols:]]).astype(bf16)
     d_joined = jnp.concatenate([d_q, d_kv])
     g_bias_mine = jnp.sum(d_joined.astype(f32), 1)
     g_qkv = jnp.dot(d_joined, normed, preferred_element_type=f32).astype(bf16)
     back_kv = to_tokens(d_kv)
     grads = jnp.concatenate([g_qkv.reshape(3, cols, width), g_out[None]])
     grads = add_blks(grads)
+    back_kv = after(back_kv, grads, terms)
+    g_up, g_down = spread(terms)
     back_q, back_kv = by_device(back_q, group), by_device(back_kv, group)
     d_mine = jnp.concatenate(
         [v[:cols] for v in back_q] + [v[:cols] for v in back_kv] + [v[cols:] for v in back_kv], 0
@@ -655,15 +670,15 @@
     d_x_two, g_ln2_g, g_ln2_b = pull_two(d_norm_two)
     e_float = cotangent.astype(f32)
 
+    g_qkv_bias = jnp.zeros((3, groups, cols), f32)
+    g_qkv_bias = lax.dynamic_update_slice(g_qkv_bias, g_bias_mine.reshape(3, 1, cols), (0, group, 0))
+    vectors = [g_ln1_g, g_ln1_b, g_ln2_g, g_ln2_b, jnp.sum(e_float, 0), g_qkv_bias.reshape(-1), g_up_bias]
     back = jnp.concatenate([v[cols:] for v in back_q], 0)
     attn_out = jnp.einsum("et,ed->td", back, w_out, preferred_element_type=f32)
     output = (x_float + (attn_out + b_out) + (mlp_out + b_down)).astype(bf16)
     input_grad = (e_float + d_x_one + d_x_two).astype(bf16)
 
-    g_qkv_bias = jnp.zeros((3, groups, cols), f32)
-    g_qkv_bias = lax.dynamic_update_slice(g_qkv_bias, g_bias_mine.reshape(3, 1, cols), (0, group, 0))
-    vectors = [g_ln1_g, g_ln1_b, g_ln2_g, g_ln2_b, jnp.sum(e_float, 0), g_qkv_bias.reshape(-1), g_up_bias]
-    g_qkv, g_out, summed = attention_grads(grads, jnp.concatenate(vectors))
+    g_qkv, g_out, summed = attention_grads(grads, jnp.concatenate(vectors), output, g_up)
     results, start = [], 0
     for vector in vectors:
         mine = vector.shape[0] // shards

time: 337 us -> 337 us (level)
  waiting for transfers between devices: 107 us -> 95.3 us
  other arithmetic: 45.8 us -> 52.8 us
  Pallas kernels: 52.7 us -> 59.2 us
    ppermute x47 -> x46, waiting for transfers between devices: 107 us -> 95.3 us  [swap(): return lax.ppermute(values, axis, [(i, i ^ bits) for i in range(count)])]
    pallas_call x1, Pallas kernels: 40 us -> 45.7 us  [attend(): pl.pallas_call(attend_kernel, grid_spec=pltpu.PrefetchScalarGridSpec(num_...]
    convert_element_type x0 -> x2, other arithmetic: none -> 3.92 us  [the longest x1 2.56 us: on_device(): sent = sum((v.astype(f32) for v in stacked_terms(kept[1::2]))).astype(bf16)]
    unnamed x167 -> x181, local copies, waits for them, and re-layouts: 16.5 us -> 19.2 us
    ppermute x47 -> x46, starting transfers between devices: 70.8 us -> 68.9 us  [swap(): return lax.ppermute(values, axis, [(i, i ^ bits) for i in range(count)])]
    select_n x10 -> x11, other arithmetic: 6.86 us -> 6.64 us  [in_order(): jnp.where(bit == 0, mine, other)]
  transfers between devices with their start and end apart: 47 -> 46, of which waited for: 21 -> 18; matrix products, arithmetic and copies ran while one was open for 23% -> 25% of each run, Pallas kernels for 14% -> 17%
where the time goes in v1:
time: 337 us; the launch traced here: 331 us
  waiting for transfers between devices  95.3 us (28%)
  starting transfers between devices  68.9 us (20%)
  Pallas kernels  59.2 us (18%)
  other arithmetic  52.8 us (16%)
  local copies, waits for them, and re-layouts  28 us (8%)
  matrix products  24.6 us (7%)
    ppermute x46, waiting for transfers between devices, swap(): return lax.ppermute(values, axis, [(i, i ^ bits) for i in range(count)])  95.3 us
    ppermute x46, starting transfers between devices, swap(): return lax.ppermute(values, axis, [(i, i ^ bits) for i in range(count)])  68.9 us
    pallas_call x1, Pallas kernels, attend(): pl.pallas_call(attend_kernel, grid_spec=pltpu.PrefetchScalarGridSpec(num_...  45.7 us
    unnamed x181, local copies, waits for them, and re-layouts  19.2 us
    dot_general x1, matrix products, mlp_pair(): jnp.dot(normed, up, preferred_element_type=f32) + up_bias.astype(f32)  8.14 us
  transfers between devices with their start and end apart: 46, of which 18 were waited for; matrix products, arithmetic and copies ran while one was open for 25% of the time, Pallas kernels for 17%

profile of v1, /device:TPU:9, one launch (start us, length us, event | category | flops | bytes accessed | tf_op | source)
XLA Modules:
  0.0 331.0 jit_solution(7365166746488507775)
XLA Ops:
  2.7 2.5 collective-permute-start.5
  8.4 3.2 broadcast_select_fusion.10
  15.3 2.3 collective-permute-done
  21.9 7.4 %collective-permute-done.2 = bf16[96,2304]{1,0:T(8,128)(2,1)} collective-permute-done((bf16[96,2304]{1,0:T(8,128)(2,1)}, bf16[96,2304]{1,0:T(8,128)(2,1)}, u32[]{:S(2)}, u32[]{:S(2)}) %collective-permute-start.2) | collective-permute-done | bytes 442400 | tf_op jit(solution)/shard_map/ppermute | solution.py:32
  34.3 4.5 %collective-permute-start.3 = (bf16[192,2304]{1,0:T(8,128)(2,1)}, bf16[192,2304]{1,0:T(8,128)(2,1)S(1)}, u32[]{:S(2)}, u32[]{:S(2)}) collective-permute-start(bf16[192,2304]{1,0:T(8,128)(2,1)} %pad_maximum_fusion.13), channel_id=1, source_target_pairs={{0,4},{4,0},{8,12},{12,8},{1,5},{5,1},{9,13},{13,9},{2,6},{6,2},{1... | collective-permute-start | bytes 2654216 | tf_op jit(solution)/shard_map/ppermute | solution.py:32
  41.8 11.7 %collective-permute-done.16 = bf16[2,256,768]{2,1,0:T(8,128)(2,1)S(1)} collective-permute-done((bf16[2,256,768]{2,1,0:T(8,128)(2,1)}, bf16[2,256,768]{2,1,0:T(8,128)(2,1)S(1)}, u32[]{:S(2)}, u32[]{:S(2)}) %collective-permute-start.16) | collective-permute-done | bytes 786464 | tf_op jit(solution)/shard_map/ppermute | solution.py:32
  53.5 6.0 %collective-permute-start.12 = (bf16[192,2304]{1,0:T(8,128)(2,1)S(1)}, bf16[192,2304]{1,0:T(8,128)(2,1)S(1)}, u32[]{:S(2)}, u32[]{:S(2)}) collective-permute-start(bf16[192,2304]{1,0:T(8,128)(2,1)S(1)} %pad_maximum_fusion.14), channel_id=1, source_target_pairs={{0,4},{4,0},{8,12},{12,8},{1,5},{5,1},{9,13},{13,9},{2,6},{6,2},{1... | collective-permute-start | bytes 2654216 | tf_op jit(solution)/shard_map/ppermute | solution.py:32
  64.3 3.6 %prepare.1 = (bf16[1024,768]{1,0:T(8,128)(2,1)S(1)}, bf16[192,1024]{1,0:T(8,128)(2,1)S(1)}, bf16[400,1024]{1,0:T(8,128)(2,1)S(1)}, f32[8,1024]{1,0:T(8,128)S(1)}, f32[8,1024]{1,0:T(8,128)S(1)}) custom-call(f32[8,1]{1,0:T(8,128)S(1)} %copy-done.6, f32[1,768]{1,0:T(1,128)S(1)} %bitcast.77, f32[1,768]{1,0:T(1,128)S(1)} %bitcast.78, ...), custom_call_target="tpu_custom_call" | custom-call | flops 905969664 | bytes 6291456 | tf_op jit(solution)/shard_map/prepare/pallas_call | solution.py:301
  77.5 8.1 %multiply_convert_fusion = (bf16[512,1536]{1,0:T(8,128)(2,1)S(1)}, f32[512,1536]{1,0:T(8,128)S(1)}, f32[512,1536]{1,0:T(8,128)S(1)}) fusion(f32[1536]{0:T(1024)S(1)} %convert_element_type.285, bf16[768,1536]{1,0:T(8,128)(2,1)S(1)} %pad_maximum_fusion.3, bf16[512,768]{1,0:T(8,128)(2,1)S(1)} %pad_maximum_fusion.16, f32[768]{0:T(1024)S(1)} %reshape.234, ...), kind=kOutput, calls=%fused_computation.18 | convolution fusion | flops 1262223360 | bytes 11026432 | tf_op jit(solution)/shard_map/dot_general | solution.py:352
  85.6 2.3 convert_reduce_fusion
  100.2 2.4 collective-permute-start.18
  106.1 45.7 %attend.1 = (bf16[3,64,1024]{2,1,0:T(8,128)(2,1)}, f32[3,64,1024]{2,1,0:T(8,128)}, bf16[2,384,1024]{2,1,0:T(8,128)(2,1)}, bf16[2,384,1024]{2,1,0:T(8,128)(2,1)}) custom-call(s32[32]{0:T(128)} %maximum_convert_fusion.5.rank, bf16[3,64,1024]{2,1,0:T(8,128)(2,1)} %bitcast.79, bf16[3,64,1024]{2,1,0:T(8,128)(2,1)} %bitcast.95, bf16[400,1024]{1,0:T(8,128)(2,1)} %copy-done.4, ...), custom_call_target="tpu_custom_call" | custom-call | flops 38654705664 | bytes 12582912 | tf_op jit(solution)/shard_map/attend/pallas_call | solution.py:224
  156.5 3.6 %collective-permute-done.23 = bf16[2,384,1024]{2,1,0:T(8,128)(2,1)} collective-permute-done((bf16[2,384,1024]{2,1,0:T(8,128)(2,1)}, bf16[2,384,1024]{2,1,0:T(8,128)(2,1)}, u32[]{:S(2)}, u32[]{:S(2)}) %collective-permute-start.23) | collective-permute-done | bytes 1572896 | tf_op jit(solution)/shard_map/ppermute | solution.py:32
  160.0 2.6 add_convert_fusion.2
  168.8 8.8 %collective-permute-done.33 = bf16[2,2,96,768]{3,2,1,0:T(8,128)(2,1)} collective-permute-done((bf16[2,2,96,768]{3,2,1,0:T(8,128)(2,1)S(1)}, bf16[2,2,96,768]{3,2,1,0:T(8,128)(2,1)}, u32[]{:S(2)}, u32[]{:S(2)}) %collective-permute-start.33) | collective-permute-done | bytes 589856 | tf_op jit(solution)/shard_map/ppermute | solution.py:32
  179.7 3.3 collective-permute-start.34
  182.9 3.2 collective-permute-done.27
  200.3 3.4 %collective-permute-done.35 = bf16[48,768]{1,0:T(8,128)(2,1)S(1)} collective-permute-done((bf16[48,768]{1,0:T(8,128)(2,1)S(1)}, bf16[48,768]{1,0:T(8,128)(2,1)S(1)}, u32[]{:S(2)}, u32[]{:S(2)}) %collective-permute-start.35) | collective-permute-done | bytes 73760 | tf_op jit(solution)/shard_map/ppermute | solution.py:32
  204.6 3.9 %collective-permute-start.29 = (bf16[384,256]{1,0:T(8,128)(2,1)}, bf16[384,256]{1,0:T(8,128)(2,1)S(1)}, u32[]{:S(2)}, u32[]{:S(2)}) collective-permute-start(bf16[384,256]{1,0:T(8,128)(2,1)} %get-tuple-element.167), channel_id=1, source_target_pairs={{0,2},{1,3},{2,0},{3,1},{4,6},{5,7},{6,4},{7,5},{8,10},{9,11},{10,... | collective-permute-start | bytes 589832 | tf_op jit(solution)/shard_map/ppermute | solution.py:32
  208.5 6.0 %collective-permute-done.25 = bf16[384,256]{1,0:T(8,128)(2,1)S(1)} collective-permute-done((bf16[384,256]{1,0:T(8,128)(2,1)S(1)}, bf16[384,256]{1,0:T(8,128)(2,1)S(1)}, u32[]{:S(2)}, u32[]{:S(2)}) %collective-permute-start.25) | collective-permute-done | bytes 196640 | tf_op jit(solution)/shard_map/ppermute | solution.py:32
  214.8 6.9 %collective-permute-start.36 = (bf16[4,48,768]{2,1,0:T(8,128)(2,1)S(1)}, bf16[4,48,768]{2,1,0:T(8,128)(2,1)S(1)}, u32[]{:S(2)}, u32[]{:S(2)}) collective-permute-start(bf16[4,48,768]{2,1,0:T(8,128)(2,1)S(1)} %pad_maximum_fusion.30), channel_id=1, source_target_pairs={{0,2},{1,3},{2,0},{3,1},{4,6},{5,7},{6,4},{7,5},{8,10},{9,11},{10,... | collective-permute-start | bytes 884744 | tf_op jit(solution)/shard_map/ppermute | solution.py:32
  225.7 18.2 %collective-permute-done.36 = bf16[4,48,768]{2,1,0:T(8,128)(2,1)S(1)} collective-permute-done((bf16[4,48,768]{2,1,0:T(8,128)(2,1)S(1)}, bf16[4,48,768]{2,1,0:T(8,128)(2,1)S(1)}, u32[]{:S(2)}, u32[]{:S(2)}) %collective-permute-start.36) | collective-permute-done | bytes 294944 | tf_op jit(solution)/shard_map/ppermute | solution.py:32
  255.8 5.8 %collective-permute-done.37 = bf16[6,48,384]{2,1,0:T(8,128)(2,1)S(1)} collective-permute-done((bf16[6,48,384]{2,1,0:T(8,128)(2,1)S(1)}, bf16[6,48,384]{2,1,0:T(8,128)(2,1)S(1)}, u32[]{:S(2)}, u32[]{:S(2)}) %collective-permute-start.37) | collective-permute-done | bytes 221216 | tf_op jit(solution)/shard_map/ppermute | solution.py:32
  265.8 11.6 %collective-permute-done.38 = bf16[6,48,384]{2,1,0:T(8,128)(2,1)S(1)} collective-permute-done((bf16[6,48,384]{2,1,0:T(8,128)(2,1)S(1)}, bf16[6,48,384]{2,1,0:T(8,128)(2,1)S(1)}, u32[]{:S(2)}, u32[]{:S(2)}) %collective-permute-start.38) | collective-permute-done | bytes 221216 | tf_op jit(solution)/shard_map/ppermute | solution.py:32
  277.4 3.4 %collective-permute-done.39 = bf16[6,48,384]{2,1,0:T(8,128)(2,1)S(1)} collective-permute-done((bf16[6,48,384]{2,1,0:T(8,128)(2,1)S(1)}, bf16[6,48,384]{2,1,0:T(8,128)(2,1)S(1)}, u32[]{:S(2)}, u32[]{:S(2)}) %collective-permute-start.39) | collective-permute-done | bytes 221216 | tf_op jit(solution)/shard_map/ppermute | solution.py:32
  285.8 4.6 %collective-permute-done.44 = bf16[4,192,768]{2,1,0:T(8,128)(2,1)S(1)} collective-permute-done((bf16[4,192,768]{2,1,0:T(8,128)(2,1)S(1)}, bf16[4,192,768]{2,1,0:T(8,128)(2,1)S(1)}, u32[]{:S(2)}, u32[]{:S(2)}) %collective-permute-start.44) | collective-permute-done | bytes 1179680 | tf_op jit(solution)/shard_map/ppermute | solution.py:32
  291.0 7.3 %collective-permute-start.45 = (bf16[4,384,768]{2,1,0:T(8,128)(2,1)S(1)}, bf16[4,384,768]{2,1,0:T(8,128)(2,1)}, u32[]{:S(2)}, u32[]{:S(2)}) collective-permute-start(bf16[4,384,768]{2,1,0:T(8,128)(2,1)S(1)} %pad_maximum_fusion.4.mine), channel_id=1, source_target_pairs={{0,4},{4,0},{8,12},{12,8},{1,5},{5,1},{9,13},{13,9},{2,6},{6,2},{1... | collective-permute-start | bytes 7077896 | tf_op jit(solution)/shard_map/ppermute | solution.py:32
  299.0 3.0 add_convert_fusion.6
  307.9 3.8 %collective-permute-start.42 = (bf16[17,96,384]{2,1,0:T(8,128)(2,1)}, bf16[17,96,384]{2,1,0:T(8,128)(2,1)}, u32[]{:S(2)}, u32[]{:S(2)}) collective-permute-start(bf16[17,96,384]{2,1,0:T(8,128)(2,1)} %fusion.27), channel_id=1, source_target_pairs={{0,4},{4,0},{8,12},{12,8},{1,5},{5,1},{9,13},{13,9},{2,6},{6,2},{1... | collective-permute-start | bytes 3760136 | tf_op jit(solution)/shard_map/ppermute | solution.py:32
  313.2 2.5 add_convert_fusion.5
  317.4 5.9 %place_mlp.1 = (f32[384,3072]{1,0:T(8,128)}, f32[2,2,384,768]{3,2,1,0:T(8,128)}) custom-call(s32[1]{0:T(128)} %bitcast.29.which, bf16[4,384,768]{2,1,0:T(8,128)(2,1)S(1)} %copy-done.3, bf16[4,384,768]{2,1,0:T(8,128)(2,1)} %collective-permute-done.45.other), custom_call_target="tpu_custom_call" | custom-call | bytes 14155776 | tf_op jit(solution)/shard_map/place_mlp/pallas_call | solution.py:407
  324.1 4.0 %place_qkv.1 = (f32[384,2304]{1,0:T(8,128)}, f32[384,768]{1,0:T(8,128)}) custom-call(s32[1]{0:T(128)} %bitcast.29.which, bf16[16,96,384]{2,1,0:T(8,128)(2,1)S(1)} %pad_maximum_fusion.10.mine, bf16[17,96,384]{2,1,0:T(8,128)(2,1)} %collective-permute-done.42.other), custom_call_target="tpu_custom_call" | custom-call | bytes 7077888 | tf_op jit(solution)/shard_map/place_qkv/pallas_call | solution.py:451
  (383 shorter events, 117.3 us)
Async XLA Ops:
  2.6 61.4 %collective-permute-start.4 = (bf16[272,768]{1,0:T(8,128)(2,1)S(1)}, bf16[272,768]{1,0:T(8,128)(2,1)S(1)}, u32[]{:S(2)}, u32[]{:S(2)}) collective-permute-start(bf16[272,768]{1,0:T(8,128)(2,1)S(1)} %fusion.52.refs_0_), channel_id=1, source_target_pairs={{0,1},{1,0},{2,3},{3,2},{4,5},{5,4},{6,7},{7,6},{8,9},{9,8},{10,11... | collective-permute-start | bytes 1253384 | tf_op jit(solution)/shard_map/ppermute | solution.py:32
  2.7 61.3 %collective-permute-start.5 = (bf16[272,768]{1,0:T(8,128)(2,1)S(1)}, bf16[272,768]{1,0:T(8,128)(2,1)}, u32[]{:S(2)}, u32[]{:S(2)}) collective-permute-start(bf16[272,768]{1,0:T(8,128)(2,1)S(1)} %fusion.52.refs_0_), channel_id=1, source_target_pairs={{0,2},{1,3},{2,0},{3,1},{4,6},{5,7},{6,4},{7,5},{8,10},{9,11},{10,... | collective-permute-start | bytes 1253384 | tf_op jit(solution)/shard_map/ppermute | solution.py:32
  5.2 58.8 %collective-permute-start.6 = (bf16[272,768]{1,0:T(8,128)(2,1)S(1)}, bf16[272,768]{1,0:T(8,128)(2,1)}, u32[]{:S(2)}, u32[]{:S(2)}) collective-permute-start(bf16[272,768]{1,0:T(8,128)(2,1)S(1)} %fusion.52.refs_0_), channel_id=1, source_target_pairs={{0,3},{1,2},{2,1},{3,0},{4,7},{5,6},{6,5},{7,4},{8,11},{9,10},{10,... | collective-permute-start | bytes 1253384 | tf_op jit(solution)/shard_map/ppermute | solution.py:32
  34.3 25.5 %collective-permute-start.3 = (bf16[192,2304]{1,0:T(8,128)(2,1)}, bf16[192,2304]{1,0:T(8,128)(2,1)S(1)}, u32[]{:S(2)}, u32[]{:S(2)}) collective-permute-start(bf16[192,2304]{1,0:T(8,128)(2,1)} %pad_maximum_fusion.13), channel_id=1, source_target_pairs={{0,4},{4,0},{8,12},{12,8},{1,5},{5,1},{9,13},{13,9},{2,6},{6,2},{1... | collective-permute-start | bytes 2654216 | tf_op jit(solution)/shard_map/ppermute | solution.py:32
  39.4 14.1 %collective-permute-start.16 = (bf16[2,256,768]{2,1,0:T(8,128)(2,1)}, bf16[2,256,768]{2,1,0:T(8,128)(2,1)S(1)}, u32[]{:S(2)}, u32[]{:S(2)}) collective-permute-start(bf16[2,256,768]{2,1,0:T(8,128)(2,1)} %pad_maximum_fusion.15), channel_id=1, source_target_pairs={{0,16},{16,0},{1,17},{17,1},{2,18},{18,2},{3,19},{19,3},{4,20},{20... | collective-permute-start | bytes 2359304 | tf_op jit(solution)/shard_map/ppermute | solution.py:32
  53.5 15.8 %collective-permute-start.12 = (bf16[192,2304]{1,0:T(8,128)(2,1)S(1)}, bf16[192,2304]{1,0:T(8,128)(2,1)S(1)}, u32[]{:S(2)}, u32[]{:S(2)}) collective-permute-start(bf16[192,2304]{1,0:T(8,128)(2,1)S(1)} %pad_maximum_fusion.14), channel_id=1, source_target_pairs={{0,4},{4,0},{8,12},{12,8},{1,5},{5,1},{9,13},{13,9},{2,6},{6,2},{1... | collective-permute-start | bytes 2654216 | tf_op jit(solution)/shard_map/ppermute | solution.py:32
  67.9 20.8 %collective-permute-start.7 = (bf16[400,1024]{1,0:T(8,128)(2,1)S(1)}, bf16[400,1024]{1,0:T(8,128)(2,1)S(1)}, u32[]{:S(2)}, u32[]{:S(2)}) collective-permute-start(bf16[400,1024]{1,0:T(8,128)(2,1)S(1)} %get-tuple-element.64.refs_0_), channel_id=1, source_target_pairs={{0,4},{4,0},{8,12},{12,8},{1,5},{5,1},{9,13},{13,9},{2,6},{6,2},{1... | collective-permute-start | bytes 2457608 | tf_op jit(solution)/shard_map/ppermute | solution.py:32
  68.0 20.8 %collective-permute-start.8 = (bf16[400,1024]{1,0:T(8,128)(2,1)S(1)}, bf16[400,1024]{1,0:T(8,128)(2,1)S(1)}, u32[]{:S(2)}, u32[]{:S(2)}) collective-permute-start(bf16[400,1024]{1,0:T(8,128)(2,1)S(1)} %get-tuple-element.64.refs_0_), channel_id=1, source_target_pairs={{0,8},{4,12},{8,0},{12,4},{1,9},{5,13},{9,1},{13,5},{2,10},{6,14},... | collective-permute-start | bytes 2457608 | tf_op jit(solution)/shard_map/ppermute | solution.py:32
  73.9 14.0 %collective-permute-start.13 = (bf16[192,256]{1,0:T(8,128)(2,1)S(1)}, bf16[192,256]{1,0:T(8,128)(2,1)S(1)}, u32[]{:S(2)}, u32[]{:S(2)}) collective-permute-start(bf16[192,256]{1,0:T(8,128)(2,1)S(1)} %get-tuple-element.185), channel_id=1, source_target_pairs={{0,1},{1,0},{2,3},{3,2},{4,5},{5,4},{6,7},{7,6},{8,9},{9,8},{10,11... | collective-permute-start | bytes 294920 | tf_op jit(solution)/shard_map/ppermute | solution.py:32
  100.2 56.0 %collective-permute-start.18 = (bf16[256,768]{1,0:T(8,128)(2,1)S(1)}, bf16[256,768]{1,0:T(8,128)(2,1)}, u32[]{:S(2)}, u32[]{:S(2)}) collective-permute-start(bf16[256,768]{1,0:T(8,128)(2,1)S(1)} %copy-done.21), channel_id=1, source_target_pairs={{0,1},{1,0},{2,3},{3,2},{4,5},{5,4},{6,7},{7,6},{8,9},{9,8},{10,11... | collective-permute-start | bytes 1179656 | tf_op jit(solution)/shard_map/ppermute | solution.py:32
  102.6 53.7 %collective-permute-start.19 = (bf16[256,768]{1,0:T(8,128)(2,1)S(1)}, bf16[256,768]{1,0:T(8,128)(2,1)}, u32[]{:S(2)}, u32[]{:S(2)}) collective-permute-start(bf16[256,768]{1,0:T(8,128)(2,1)S(1)} %copy-done.21), channel_id=1, source_target_pairs={{0,2},{1,3},{2,0},{3,1},{4,6},{5,7},{6,4},{7,5},{8,10},{9,11},{10,... | collective-permute-start | bytes 1179656 | tf_op jit(solution)/shard_map/ppermute | solution.py:32
  103.9 52.4 %collective-permute-start.20 = (bf16[256,768]{1,0:T(8,128)(2,1)S(1)}, bf16[256,768]{1,0:T(8,128)(2,1)}, u32[]{:S(2)}, u32[]{:S(2)}) collective-permute-start(bf16[256,768]{1,0:T(8,128)(2,1)S(1)} %copy-done.21), channel_id=1, source_target_pairs={{0,3},{1,2},{2,1},{3,0},{4,7},{5,6},{6,5},{7,4},{8,11},{9,10},{10,... | collective-permute-start | bytes 1179656 | tf_op jit(solution)/shard_map/ppermute | solution.py:32
  104.1 47.7 %collective-permute-start.22 = (bf16[512,768]{1,0:T(8,128)(2,1)S(1)}, bf16[512,768]{1,0:T(8,128)(2,1)}, u32[]{:S(2)}, u32[]{:S(2)}) collective-permute-start(bf16[512,768]{1,0:T(8,128)(2,1)S(1)} %pad_maximum_fusion.19), channel_id=1, source_target_pairs={{0,16},{16,0},{1,17},{17,1},{2,18},{18,2},{3,19},{19,3},{4,20},{20... | collective-permute-start | bytes 2359304 | tf_op jit(solution)/shard_map/ppermute | solution.py:32
  104.9 49.9 %collective-permute-start.21 = (bf16[2,2,192,768]{3,2,1,0:T(8,128)(2,1)S(1)}, bf16[2,2,192,768]{3,2,1,0:T(8,128)(2,1)S(1)}, u32[]{:S(2)}, u32[]{:S(2)}) collective-permute-start(bf16[2,2,192,768]{3,2,1,0:T(8,128)(2,1)S(1)} %broadcast_select_fusion.8), channel_id=1, source_target_pairs={{0,8},{4,12},{8,0},{12,4},{1,9},{5,13},{9,1},{13,5},{2,10},{6,14},... | collective-permute-start | bytes 3538952 | tf_op jit(solution)/shard_map/ppermute | solution.py:32
  162.7 15.0 %collective-permute-start.33 = (bf16[2,2,96,768]{3,2,1,0:T(8,128)(2,1)S(1)}, bf16[2,2,96,768]{3,2,1,0:T(8,128)(2,1)}, u32[]{:S(2)}, u32[]{:S(2)}) collective-permute-start(bf16[2,2,96,768]{3,2,1,0:T(8,128)(2,1)S(1)} %broadcast_select_fusion.19), channel_id=1, source_target_pairs={{0,1},{1,0},{2,3},{3,2},{4,5},{5,4},{6,7},{7,6},{8,9},{9,8},{10,11... | collective-permute-start | bytes 1769480 | tf_op jit(solution)/shard_map/ppermute | solution.py:32
  167.0 19.1 %collective-permute-start.27 = (bf16[1,384,1024]{2,1,0:T(8,128)(2,1)}, bf16[1,384,1024]{2,1,0:T(8,128)(2,1)S(1)}, u32[]{:S(2)}, u32[]{:S(2)}) collective-permute-start(bf16[1,384,1024]{2,1,0:T(8,128)(2,1)} %add_convert_fusion.2), channel_id=1, source_target_pairs={{0,8},{4,12},{8,0},{12,4},{1,9},{5,13},{9,1},{13,5},{2,10},{6,14},... | collective-permute-start | bytes 2359304 | tf_op jit(solution)/shard_map/ppermute | solution.py:32
  179.7 19.4 %collective-permute-start.34 = (bf16[2,2,48,768]{3,2,1,0:T(8,128)(2,1)}, bf16[2,2,48,768]{3,2,1,0:T(8,128)(2,1)}, u32[]{:S(2)}, u32[]{:S(2)}) collective-permute-start(bf16[2,2,48,768]{3,2,1,0:T(8,128)(2,1)} %broadcast_select_fusion.25), channel_id=1, source_target_pairs={{0,2},{1,3},{2,0},{3,1},{4,6},{5,7},{6,4},{7,5},{8,10},{9,11},{10,... | collective-permute-start | bytes 884744 | tf_op jit(solution)/shard_map/ppermute | solution.py:32
  194.3 31.1 %collective-permute-start.31 = (bf16[4,96,768]{2,1,0:T(8,128)(2,1)}, bf16[4,96,768]{2,1,0:T(8,128)(2,1)S(1)}, u32[]{:S(2)}, u32[]{:S(2)}) collective-permute-start(bf16[4,96,768]{2,1,0:T(8,128)(2,1)} %broadcast_select_fusion.20), channel_id=1, source_target_pairs={{0,4},{4,0},{8,12},{12,8},{1,5},{5,1},{9,13},{13,9},{2,6},{6,2},{1... | collective-permute-start | bytes 1769480 | tf_op jit(solution)/shard_map/ppermute | solution.py:32
  195.4 52.5 %collective-permute-start.28 = (bf16[384,256]{1,0:T(8,128)(2,1)}, bf16[384,256]{1,0:T(8,128)(2,1)S(1)}, u32[]{:S(2)}, u32[]{:S(2)}) collective-permute-start(bf16[384,256]{1,0:T(8,128)(2,1)} %get-tuple-element.166), channel_id=1, source_target_pairs={{0,1},{1,0},{2,3},{3,2},{4,5},{5,4},{6,7},{7,6},{8,9},{9,8},{10,11... | collective-permute-start | bytes 589832 | tf_op jit(solution)/shard_map/ppermute | solution.py:32
  197.8 16.7 %collective-permute-start.25 = (bf16[384,256]{1,0:T(8,128)(2,1)S(1)}, bf16[384,256]{1,0:T(8,128)(2,1)S(1)}, u32[]{:S(2)}, u32[]{:S(2)}) collective-permute-start(bf16[384,256]{1,0:T(8,128)(2,1)S(1)} %get-tuple-element.169), channel_id=1, source_target_pairs={{0,2},{1,3},{2,0},{3,1},{4,6},{5,7},{6,4},{7,5},{8,10},{9,11},{10,... | collective-permute-start | bytes 589832 | tf_op jit(solution)/shard_map/ppermute | solution.py:32
  204.6 43.4 %collective-permute-start.29 = (bf16[384,256]{1,0:T(8,128)(2,1)}, bf16[384,256]{1,0:T(8,128)(2,1)S(1)}, u32[]{:S(2)}, u32[]{:S(2)}) collective-permute-start(bf16[384,256]{1,0:T(8,128)(2,1)} %get-tuple-element.167), channel_id=1, source_target_pairs={{0,2},{1,3},{2,0},{3,1},{4,6},{5,7},{6,4},{7,5},{8,10},{9,11},{10,... | collective-permute-start | bytes 589832 | tf_op jit(solution)/shard_map/ppermute | solution.py:32
  214.5 33.5 %collective-permute-start.30 = (bf16[384,256]{1,0:T(8,128)(2,1)}, bf16[384,256]{1,0:T(8,128)(2,1)S(1)}, u32[]{:S(2)}, u32[]{:S(2)}) collective-permute-start(bf16[384,256]{1,0:T(8,128)(2,1)} %get-tuple-element.164), channel_id=1, source_target_pairs={{0,3},{1,2},{2,1},{3,0},{4,7},{5,6},{6,5},{7,4},{8,11},{9,10},{10,... | collective-permute-start | bytes 589832 | tf_op jit(solution)/shard_map/ppermute | solution.py:32
  214.8 29.1 %collective-permute-start.36 = (bf16[4,48,768]{2,1,0:T(8,128)(2,1)S(1)}, bf16[4,48,768]{2,1,0:T(8,128)(2,1)S(1)}, u32[]{:S(2)}, u32[]{:S(2)}) collective-permute-start(bf16[4,48,768]{2,1,0:T(8,128)(2,1)S(1)} %pad_maximum_fusion.30), channel_id=1, source_target_pairs={{0,2},{1,3},{2,0},{3,1},{4,6},{5,7},{6,4},{7,5},{8,10},{9,11},{10,... | collective-permute-start | bytes 884744 | tf_op jit(solution)/shard_map/ppermute | solution.py:32
  225.6 21.5 %collective-permute-start.32 = (bf16[4,48,768]{2,1,0:T(8,128)(2,1)S(1)}, bf16[4,48,768]{2,1,0:T(8,128)(2,1)S(1)}, u32[]{:S(2)}, u32[]{:S(2)}) collective-permute-start(bf16[4,48,768]{2,1,0:T(8,128)(2,1)S(1)} %broadcast_select_fusion.28), channel_id=1, source_target_pairs={{0,8},{4,12},{8,0},{12,4},{1,9},{5,13},{9,1},{13,5},{2,10},{6,14},... | collective-permute-start | bytes 884744 | tf_op jit(solution)/shard_map/ppermute | solution.py:32
  244.8 19.6 %collective-permute-start.43 = (bf16[4,96,768]{2,1,0:T(8,128)(2,1)}, bf16[4,96,768]{2,1,0:T(8,128)(2,1)}, u32[]{:S(2)}, u32[]{:S(2)}) collective-permute-start(bf16[4,96,768]{2,1,0:T(8,128)(2,1)} %pad_maximum_fusion.21), channel_id=1, source_target_pairs={{0,1},{1,0},{2,3},{3,2},{4,5},{5,4},{6,7},{7,6},{8,9},{9,8},{10,11... | collective-permute-start | bytes 1769480 | tf_op jit(solution)/shard_map/ppermute | solution.py:32
  261.7 15.8 %collective-permute-start.38 = (bf16[6,48,384]{2,1,0:T(8,128)(2,1)S(1)}, bf16[6,48,384]{2,1,0:T(8,128)(2,1)S(1)}, u32[]{:S(2)}, u32[]{:S(2)}) collective-permute-start(bf16[6,48,384]{2,1,0:T(8,128)(2,1)S(1)} %add_convert_fusion.9), channel_id=1, source_target_pairs={{0,3},{1,2},{2,1},{3,0},{4,7},{5,6},{6,5},{7,4},{8,11},{9,10},{10,... | collective-permute-start | bytes 663560 | tf_op jit(solution)/shard_map/ppermute | solution.py:32
  262.5 18.3 %collective-permute-start.39 = (bf16[6,48,384]{2,1,0:T(8,128)(2,1)S(1)}, bf16[6,48,384]{2,1,0:T(8,128)(2,1)S(1)}, u32[]{:S(2)}, u32[]{:S(2)}) collective-permute-start(bf16[6,48,384]{2,1,0:T(8,128)(2,1)S(1)} %add_convert_fusion.9), channel_id=1, source_target_pairs={{0,2},{1,3},{2,0},{3,1},{4,6},{5,7},{6,4},{7,5},{8,10},{9,11},{10,... | collective-permute-start | bytes 663560 | tf_op jit(solution)/shard_map/ppermute | solution.py:32
  264.2 16.6 %collective-permute-start.40 = (bf16[6,48,384]{2,1,0:T(8,128)(2,1)S(1)}, bf16[6,48,384]{2,1,0:T(8,128)(2,1)S(1)}, u32[]{:S(2)}, u32[]{:S(2)}) collective-permute-start(bf16[6,48,384]{2,1,0:T(8,128)(2,1)S(1)} %add_convert_fusion.9), channel_id=1, source_target_pairs={{0,1},{1,0},{2,3},{3,2},{4,5},{5,4},{6,7},{7,6},{8,9},{9,8},{10,11... | collective-permute-start | bytes 663560 | tf_op jit(solution)/shard_map/ppermute | solution.py:32
  265.7 24.6 %collective-permute-start.44 = (bf16[4,192,768]{2,1,0:T(8,128)(2,1)S(1)}, bf16[4,192,768]{2,1,0:T(8,128)(2,1)S(1)}, u32[]{:S(2)}, u32[]{:S(2)}) collective-permute-start(bf16[4,192,768]{2,1,0:T(8,128)(2,1)S(1)} %pad_maximum_fusion.11), channel_id=1, source_target_pairs={{0,8},{4,12},{8,0},{12,4},{1,9},{5,13},{9,1},{13,5},{2,10},{6,14},... | collective-permute-start | bytes 3538952 | tf_op jit(solution)/shard_map/ppermute | solution.py:32
  285.7 18.3 %collective-permute-start.41 = (bf16[17,48,384]{2,1,0:T(8,128)(2,1)}, bf16[17,48,384]{2,1,0:T(8,128)(2,1)}, u32[]{:S(2)}, u32[]{:S(2)}) collective-permute-start(bf16[17,48,384]{2,1,0:T(8,128)(2,1)} %get-tuple-element.115), channel_id=1, source_target_pairs={{0,8},{4,12},{8,0},{12,4},{1,9},{5,13},{9,1},{13,5},{2,10},{6,14},... | collective-permute-start | bytes 1880072 | tf_op jit(solution)/shard_map/ppermute | solution.py:32
  291.0 24.9 %collective-permute-start.45 = (bf16[4,384,768]{2,1,0:T(8,128)(2,1)S(1)}, bf16[4,384,768]{2,1,0:T(8,128)(2,1)}, u32[]{:S(2)}, u32[]{:S(2)}) collective-permute-start(bf16[4,384,768]{2,1,0:T(8,128)(2,1)S(1)} %pad_maximum_fusion.4.mine), channel_id=1, source_target_pairs={{0,4},{4,0},{8,12},{12,8},{1,5},{5,1},{9,13},{13,9},{2,6},{6,2},{1... | collective-permute-start | bytes 7077896 | tf_op jit(solution)/shard_map/ppermute | solution.py:32
  307.9 15.4 %collective-permute-start.42 = (bf16[17,96,384]{2,1,0:T(8,128)(2,1)}, bf16[17,96,384]{2,1,0:T(8,128)(2,1)}, u32[]{:S(2)}, u32[]{:S(2)}) collective-permute-start(bf16[17,96,384]{2,1,0:T(8,128)(2,1)} %fusion.27), channel_id=1, source_target_pairs={{0,4},{4,0},{8,12},{12,8},{1,5},{5,1},{9,13},{13,9},{2,6},{6,2},{1... | collective-permute-start | bytes 3760136 | tf_op jit(solution)/shard_map/ppermute | solution.py:32
  (89 other events, 574.5 us)

commit v2 on v1

--- a/solution.py
+++ b/solution.py
@@ -207,7 +207,7 @@
         i, at = t // own, (t % own) * STRETCH
         to = keep_ref if i % 2 == 0 else send_ref
         for h in heads:
-            turned = sums[h, rank[t]].T.astype(bf16)
+            turned = sums[h, rank[t]].astype(bf16).T
             first = h * HEAD
             to[i // 2, cols + first : cols + first + HEAD, at : at + STRETCH] = turned[:HEAD]
             to[i // 2, first : first + HEAD, at : at + STRETCH] = turned[HEAD:]
@@ -368,17 +368,16 @@
     first = add_half((pieces[0], pieces[1]), "blk", 1)
     got = swap(after(sent, first), "fsdp", 1).astype(f32)
     out, d_normed = part[:rows] + got[:rows], d_part[:rows] + got[rows:]
-    sums = add_half(halves_of(first, 2), "blk", 2)
+    sums = add_half(halves_of(first, 2), "ulysses", 1)
     side, none = lax.axis_index("fsdp"), jnp.zeros_like(g_up_bias)
     g_up_bias = jnp.concatenate([jnp.where(side == 0, g_up_bias, none), jnp.where(side == 0, none, g_up_bias)])
     return out, d_normed, first, sums, g_up_bias
 
 
-def finish_pair(sums, earlier):
+def finish_pair(sums, earlier, later):
     side = lax.axis_index("fsdp")
-    sums = after(sums, earlier)
-    sums = add_half(halves_of(sums, 2), "ulysses", 1)
-    sums = add_half(halves_of(sums, 2), "ulysses", 2)
+    sums = add_half(halves_of(after(sums, earlier), 2), "blk", 2)
+    sums = add_half(halves_of(after(sums, later), 2), "ulysses", 2)
     got = swap(jnp.where(side == 0, sums[0, 1], sums[0, 0]), "fsdp", 1)
     kept = jnp.where(side == 0, sums[0, 0], sums[0, 1])
     sums = jnp.concatenate([in_order(side, kept[None], got[None]), sums[1]], 0)
@@ -386,8 +385,9 @@
 
 
 def spread_pair(sums):
-    sums = share_half(sums, "ulysses", 1, 1)
-    sums = share_half(sums, "blk", 2, 1)
+    kinds, rows, width = sums.shape
+    sums = share_half(sums[:, None], "ulysses", 1, 1)
+    sums = share_half(sums[:, :, None], "blk", 2, 2).reshape(kinds, 4 * rows, width)
     return place_mlp(bit_of("blk", 1), sums, swap(sums, "blk", 1))
 
 
@@ -582,7 +582,7 @@
         half_up = share_half(after(part_up, half_qkv), "blk", 2, 0)
         x_all = around(x_ranks)
         mine = jnp.concatenate([units_of(up_weight, side), out_weight], 1)
-        half_up = both_shards(mine, half_up)
+        half_up = both_shards(mine, after(half_up, w_qkv))
         w_up, w_out = half_up[:, :-width], half_up[:, -width:]
         x_mlp = jnp.concatenate([tokens, x_e[0]])
         e_mlp = jnp.concatenate([cotangent, x_e[1]])
@@ -596,7 +596,7 @@
         )
         b_up = gather_small(up_bias).reshape(-1)
         x_mlp, e_mlp = tokens, cotangent
-        mlp, finish, spread = mlp_gathered, lambda v, _: v, lambda v: v
+        mlp, finish, spread = mlp_gathered, lambda v, *_: v, lambda v: v
     small = jnp.concatenate([ln1_gain, ln1_bias, ln2_gain, ln2_bias, out_bias, down_bias, qkv_bias])
     small = gather_small(after(small, part_qkv))
     part = width // shards
@@ -639,13 +639,13 @@
     while len(kept) > 1:
         step *= 2
         sent = sum(v.astype(f32) for v in stacked_terms(kept[1::2])).astype(bf16)
-        terms = finish(terms, sent) if step == 2 else terms
         got = swap(sent, "blk", step)
         kept = [kept[2 * i] + [got[i]] for i in range(got.shape[0])]
     total = sum(v.astype(f32) for v in kept[0])
     d_q = rotate(d_q, cosine, -sine).astype(bf16).reshape(cols, rows)
     mixed = mixed.reshape(cols, rows)
-    back_q = to_tokens(after(jnp.concatenate([d_q, mixed]), sent))
+    back_q = to_tokens(jnp.concatenate([d_q, mixed]))
+    terms = finish(terms, sent, back_q)
     e_all = jnp.concatenate(e_around, 0)
     g_out = jnp.dot(mixed, e_all, preferred_element_type=f32).astype(bf16)
     d_k = rotate(total[:cols].reshape(heads, HEAD, rows), cosine, -sine).reshape(cols, rows)

time: 337 us -> 388 us (1.15)
  waiting for transfers between devices: 95.3 us -> 150 us
  Pallas kernels: 59.2 us -> 50.5 us
    ppermute x46, waiting for transfers between devices: 95.3 us -> 150 us  [swap(): return lax.ppermute(values, axis, [(i, i ^ bits) for i in range(count)])]
    pallas_call x1, Pallas kernels: 45.7 us -> 37 us  [attend(): pl.pallas_call(attend_kernel, grid_spec=pltpu.PrefetchScalarGridSpec(num_...]
    unnamed x181 -> x225, local copies, waits for them, and re-layouts: 19.2 us -> 19.7 us
  transfers between devices with their start and end apart: 46 -> 46, of which waited for: 18 -> 19; matrix products, arithmetic and copies ran while one was open for 25% -> 22% of each run, Pallas kernels for 17% -> 12%
where the time goes in v2:
time: 388 us; the launch traced here: 384 us
  waiting for transfers between devices  150 us (39%)
  starting transfers between devices  68.8 us (18%)
  other arithmetic  54.6 us (14%)
  Pallas kernels  50.5 us (13%)
  local copies, waits for them, and re-layouts  31 us (8%)
  matrix products  26.9 us (7%)
    ppermute x46, waiting for transfers between devices, swap(): return lax.ppermute(values, axis, [(i, i ^ bits) for i in range(count)])  150 us
    ppermute x46, starting transfers between devices, swap(): return lax.ppermute(values, axis, [(i, i ^ bits) for i in range(count)])  68.8 us
    pallas_call x1, Pallas kernels, attend(): pl.pallas_call(attend_kernel, grid_spec=pltpu.PrefetchScalarGridSpec(num_...  37 us
    unnamed x225, local copies, waits for them, and re-layouts  19.7 us
    dot_general x1, matrix products, mlp_pair(): jnp.dot(normed, up, preferred_element_type=f32) + up_bias.astype(f32)  8.14 us
  transfers between devices with their start and end apart: 46, of which 19 were waited for; matrix products, arithmetic and copies ran while one was open for 22% of the time, Pallas kernels for 12%

profile of v2, /device:TPU:9, one launch (start us, length us, event | category | flops | bytes accessed | tf_op | source)
XLA Modules:
  0.0 383.8 jit_solution(6085119397964777659)
XLA Ops:
  8.4 3.2 broadcast_select_fusion.10
  21.9 7.4 %collective-permute-done.2 = bf16[96,2304]{1,0:T(8,128)(2,1)} collective-permute-done((bf16[96,2304]{1,0:T(8,128)(2,1)}, bf16[96,2304]{1,0:T(8,128)(2,1)}, u32[]{:S(2)}, u32[]{:S(2)}) %collective-permute-start.2) | collective-permute-done | bytes 442400 | tf_op jit(solution)/shard_map/ppermute | solution.py:32
  34.2 4.5 %collective-permute-start.3 = (bf16[192,2304]{1,0:T(8,128)(2,1)}, bf16[192,2304]{1,0:T(8,128)(2,1)S(1)}, u32[]{:S(2)}, u32[]{:S(2)}) collective-permute-start(bf16[192,2304]{1,0:T(8,128)(2,1)} %pad_maximum_fusion.11), channel_id=1, source_target_pairs={{0,4},{4,0},{8,12},{12,8},{1,5},{5,1},{9,13},{13,9},{2,6},{6,2},{1... | collective-permute-start | bytes 2654216 | tf_op jit(solution)/shard_map/ppermute | solution.py:32
  41.8 11.7 %collective-permute-done.16 = bf16[2,256,768]{2,1,0:T(8,128)(2,1)S(1)} collective-permute-done((bf16[2,256,768]{2,1,0:T(8,128)(2,1)}, bf16[2,256,768]{2,1,0:T(8,128)(2,1)S(1)}, u32[]{:S(2)}, u32[]{:S(2)}) %collective-permute-start.16) | collective-permute-done | bytes 786464 | tf_op jit(solution)/shard_map/ppermute | solution.py:32
  53.5 6.0 %collective-permute-start.12 = (bf16[192,2304]{1,0:T(8,128)(2,1)S(1)}, bf16[192,2304]{1,0:T(8,128)(2,1)S(1)}, u32[]{:S(2)}, u32[]{:S(2)}) collective-permute-start(bf16[192,2304]{1,0:T(8,128)(2,1)S(1)} %pad_maximum_fusion.12), channel_id=1, source_target_pairs={{0,4},{4,0},{8,12},{12,8},{1,5},{5,1},{9,13},{13,9},{2,6},{6,2},{1... | collective-permute-start | bytes 2654216 | tf_op jit(solution)/shard_map/ppermute | solution.py:32
  64.4 3.6 prepare.1
  77.6 8.1 %multiply_convert_fusion = (bf16[512,1536]{1,0:T(8,128)(2,1)S(1)}, f32[512,1536]{1,0:T(8,128)S(1)}, f32[512,1536]{1,0:T(8,128)S(1)}) fusion(f32[1536]{0:T(1024)S(1)} %convert_element_type.285, bf16[768,1536]{1,0:T(8,128)(2,1)S(1)} %pad_maximum_fusion.2, bf16[512,768]{1,0:T(8,128)(2,1)S(1)} %pad_maximum_fusion.14, f32[768]{0:T(1024)S(1)} %reshape.238, ...), kind=kOutput, calls=%fused_computation.17 | convolution fusion | flops 1262223360 | bytes 11026432 | tf_op jit(solution)/shard_map/dot_general | solution.py:352
  93.2 2.9 broadcast_select_fusion
  97.3 3.7 fusion.93
  113.3 37.0 %attend.1 = (bf16[3,64,1024]{2,1,0:T(8,128)(2,1)}, f32[3,64,1024]{2,1,0:T(8,128)}, bf16[2,384,1024]{2,1,0:T(8,128)(2,1)}, bf16[2,384,1024]{2,1,0:T(8,128)(2,1)}) custom-call(s32[32]{0:T(128)} %maximum_convert_fusion.5.rank, bf16[3,64,1024]{2,1,0:T(8,128)(2,1)} %bitcast.92, bf16[3,64,1024]{2,1,0:T(8,128)(2,1)} %bitcast.111, bf16[400,1024]{1,0:T(8,128)(2,1)} %copy-done.4, ...), custom_call_target="tpu_custom_call" | custom-call | flops 38654705664 | bytes 12582912 | tf_op jit(solution)/shard_map/attend/pallas_call | solution.py:224
  153.3 7.4 %collective-permute-done.24 = bf16[2,2,192,768]{3,2,1,0:T(8,128)(2,1)S(1)} collective-permute-done((bf16[2,2,192,768]{3,2,1,0:T(8,128)(2,1)S(1)}, bf16[2,2,192,768]{3,2,1,0:T(8,128)(2,1)S(1)}, u32[]{:S(2)}, u32[]{:S(2)}) %collective-permute-start.24) | collective-permute-done | bytes 1179680 | tf_op jit(solution)/shard_map/ppermute | solution.py:32
  162.5 2.9 collective-permute-done.26
  166.8 5.4 %collective-permute-start.27 = (bf16[1,384,1024]{2,1,0:T(8,128)(2,1)S(1)}, bf16[1,384,1024]{2,1,0:T(8,128)(2,1)}, u32[]{:S(2)}, u32[]{:S(2)}) collective-permute-start(bf16[1,384,1024]{2,1,0:T(8,128)(2,1)S(1)} %add_convert_fusion.2), channel_id=1, source_target_pairs={{0,8},{4,12},{8,0},{12,4},{1,9},{5,13},{9,1},{13,5},{2,10},{6,14},... | collective-permute-start | bytes 2359304 | tf_op jit(solution)/shard_map/ppermute | solution.py:32
  178.0 24.8 %collective-permute-done.33 = bf16[2,2,96,768]{3,2,1,0:T(8,128)(2,1)} collective-permute-done((bf16[2,2,96,768]{3,2,1,0:T(8,128)(2,1)}, bf16[2,2,96,768]{3,2,1,0:T(8,128)(2,1)}, u32[]{:S(2)}, u32[]{:S(2)}) %collective-permute-start.33) | collective-permute-done | bytes 589856 | tf_op jit(solution)/shard_map/ppermute | solution.py:32
  215.2 8.1 %collective-permute-done.18 = bf16[384,256]{1,0:T(8,128)(2,1)S(1)} collective-permute-done((bf16[384,256]{1,0:T(8,128)(2,1)S(1)}, bf16[384,256]{1,0:T(8,128)(2,1)S(1)}, u32[]{:S(2)}, u32[]{:S(2)}) %collective-permute-start.18) | collective-permute-done | bytes 196640 | tf_op jit(solution)/shard_map/ppermute | solution.py:32
  223.4 2.8 collective-permute-done.19
  227.8 3.1 collective-permute-start.34
  234.7 17.2 %collective-permute-done.34 = bf16[2,2,48,768]{3,2,1,0:T(8,128)(2,1)} collective-permute-done((bf16[2,2,48,768]{3,2,1,0:T(8,128)(2,1)}, bf16[2,2,48,768]{3,2,1,0:T(8,128)(2,1)}, u32[]{:S(2)}, u32[]{:S(2)}) %collective-permute-start.34) | collective-permute-done | bytes 294944 | tf_op jit(solution)/shard_map/ppermute | solution.py:32
  256.3 6.1 %collective-permute-done.32 = bf16[4,48,768]{2,1,0:T(8,128)(2,1)S(1)} collective-permute-done((bf16[4,48,768]{2,1,0:T(8,128)(2,1)S(1)}, bf16[4,48,768]{2,1,0:T(8,128)(2,1)S(1)}, u32[]{:S(2)}, u32[]{:S(2)}) %collective-permute-start.32) | collective-permute-done | bytes 294944 | tf_op jit(solution)/shard_map/ppermute | solution.py:32
  273.5 3.2 collective-permute-start.36
  279.7 4.0 %collective-permute-start.39 = (bf16[6,48,384]{2,1,0:T(8,128)(2,1)S(1)}, bf16[6,48,384]{2,1,0:T(8,128)(2,1)S(1)}, u32[]{:S(2)}, u32[]{:S(2)}) collective-permute-start(bf16[6,48,384]{2,1,0:T(8,128)(2,1)S(1)} %add_convert_fusion.9), channel_id=1, source_target_pairs={{0,2},{1,3},{2,0},{3,1},{4,6},{5,7},{6,4},{7,5},{8,10},{9,11},{10,... | collective-permute-start | bytes 663560 | tf_op jit(solution)/shard_map/ppermute | solution.py:32
  283.7 14.9 %collective-permute-done.36 = bf16[4,48,768]{2,1,0:T(8,128)(2,1)S(1)} collective-permute-done((bf16[4,48,768]{2,1,0:T(8,128)(2,1)S(1)}, bf16[4,48,768]{2,1,0:T(8,128)(2,1)S(1)}, u32[]{:S(2)}, u32[]{:S(2)}) %collective-permute-start.36) | collective-permute-done | bytes 294944 | tf_op jit(solution)/shard_map/ppermute | solution.py:32
  298.7 2.7 collective-permute-start.43
  301.4 3.4 collective-permute-done.38
  304.7 3.4 collective-permute-done.39
  308.9 9.3 %collective-permute-done.43 = bf16[4,1,96,768]{3,2,1,0:T(8,128)(2,1)S(1)} collective-permute-done((bf16[4,1,96,768]{3,2,1,0:T(8,128)(2,1)S(1)}, bf16[4,1,96,768]{3,2,1,0:T(8,128)(2,1)S(1)}, u32[]{:S(2)}, u32[]{:S(2)}) %collective-permute-start.43) | collective-permute-done | bytes 589856 | tf_op jit(solution)/shard_map/ppermute | solution.py:32
  324.1 20.5 %collective-permute-done.44 = bf16[4,2,1,96,768]{4,3,2,1,0:T(8,128)(2,1)S(1)} collective-permute-done((bf16[4,2,1,96,768]{4,3,2,1,0:T(8,128)(2,1)S(1)}, bf16[4,2,1,96,768]{4,3,2,1,0:T(8,128)(2,1)S(1)}, u32[]{:S(2)}, u32[]{:S(2)}) %collective-permute-start.44) | collective-permute-done | bytes 1179680 | tf_op jit(solution)/shard_map/ppermute | solution.py:32
  345.0 4.4 %collective-permute-start.45 = (bf16[4,384,768]{2,1,0:T(8,128)(2,1)S(1)}, bf16[4,384,768]{2,1,0:T(8,128)(2,1)}, u32[]{:S(2)}, u32[]{:S(2)}) collective-permute-start(bf16[4,384,768]{2,1,0:T(8,128)(2,1)S(1)} %bitcast.88), channel_id=1, source_target_pairs={{0,4},{4,0},{8,12},{12,8},{1,5},{5,1},{9,13},{13,9},{2,6},{6,2},{1... | collective-permute-start | bytes 7077896 | tf_op jit(solution)/shard_map/ppermute | solution.py:32
  350.1 3.0 add_convert_fusion.6
  353.1 5.0 %collective-permute-done.41 = bf16[17,48,384]{2,1,0:T(8,128)(2,1)} collective-permute-done((bf16[17,48,384]{2,1,0:T(8,128)(2,1)}, bf16[17,48,384]{2,1,0:T(8,128)(2,1)}, u32[]{:S(2)}, u32[]{:S(2)}) %collective-permute-start.41) | collective-permute-done | bytes 626720 | tf_op jit(solution)/shard_map/ppermute | solution.py:32
  370.2 5.9 %place_mlp.1 = (f32[384,3072]{1,0:T(8,128)}, f32[2,2,384,768]{3,2,1,0:T(8,128)}) custom-call(s32[1]{0:T(128)} %bitcast.29.which, bf16[4,384,768]{2,1,0:T(8,128)(2,1)S(1)} %bitcast.89, bf16[4,384,768]{2,1,0:T(8,128)(2,1)} %collective-permute-done.45.other), custom_call_target="tpu_custom_call" | custom-call | bytes 14155776 | tf_op jit(solution)/shard_map/place_mlp/pallas_call | solution.py:407
  376.9 4.0 %place_qkv.1 = (f32[384,2304]{1,0:T(8,128)}, f32[384,768]{1,0:T(8,128)}) custom-call(s32[1]{0:T(128)} %bitcast.29.which, bf16[16,96,384]{2,1,0:T(8,128)(2,1)S(1)} %pad_maximum_fusion.9.mine, bf16[17,96,384]{2,1,0:T(8,128)(2,1)} %collective-permute-done.42.other), custom_call_target="tpu_custom_call" | custom-call | bytes 7077888 | tf_op jit(solution)/shard_map/place_qkv/pallas_call | solution.py:451
  (427 shorter events, 131.8 us)
Async XLA Ops:
  2.6 61.4 %collective-permute-start.4 = (bf16[272,768]{1,0:T(8,128)(2,1)S(1)}, bf16[272,768]{1,0:T(8,128)(2,1)S(1)}, u32[]{:S(2)}, u32[]{:S(2)}) collective-permute-start(bf16[272,768]{1,0:T(8,128)(2,1)S(1)} %fusion.51.refs_0_), channel_id=1, source_target_pairs={{0,1},{1,0},{2,3},{3,2},{4,5},{5,4},{6,7},{7,6},{8,9},{9,8},{10,11... | collective-permute-start | bytes 1253384 | tf_op jit(solution)/shard_map/ppermute | solution.py:32
  2.7 61.4 %collective-permute-start.5 = (bf16[272,768]{1,0:T(8,128)(2,1)S(1)}, bf16[272,768]{1,0:T(8,128)(2,1)}, u32[]{:S(2)}, u32[]{:S(2)}) collective-permute-start(bf16[272,768]{1,0:T(8,128)(2,1)S(1)} %fusion.51.refs_0_), channel_id=1, source_target_pairs={{0,2},{1,3},{2,0},{3,1},{4,6},{5,7},{6,4},{7,5},{8,10},{9,11},{10,... | collective-permute-start | bytes 1253384 | tf_op jit(solution)/shard_map/ppermute | solution.py:32
  5.2 58.9 %collective-permute-start.6 = (bf16[272,768]{1,0:T(8,128)(2,1)S(1)}, bf16[272,768]{1,0:T(8,128)(2,1)}, u32[]{:S(2)}, u32[]{:S(2)}) collective-permute-start(bf16[272,768]{1,0:T(8,128)(2,1)S(1)} %fusion.51.refs_0_), channel_id=1, source_target_pairs={{0,3},{1,2},{2,1},{3,0},{4,7},{5,6},{6,5},{7,4},{8,11},{9,10},{10,... | collective-permute-start | bytes 1253384 | tf_op jit(solution)/shard_map/ppermute | solution.py:32
  34.2 25.5 %collective-permute-start.3 = (bf16[192,2304]{1,0:T(8,128)(2,1)}, bf16[192,2304]{1,0:T(8,128)(2,1)S(1)}, u32[]{:S(2)}, u32[]{:S(2)}) collective-permute-start(bf16[192,2304]{1,0:T(8,128)(2,1)} %pad_maximum_fusion.11), channel_id=1, source_target_pairs={{0,4},{4,0},{8,12},{12,8},{1,5},{5,1},{9,13},{13,9},{2,6},{6,2},{1... | collective-permute-start | bytes 2654216 | tf_op jit(solution)/shard_map/ppermute | solution.py:32
  39.4 14.1 %collective-permute-start.16 = (bf16[2,256,768]{2,1,0:T(8,128)(2,1)}, bf16[2,256,768]{2,1,0:T(8,128)(2,1)S(1)}, u32[]{:S(2)}, u32[]{:S(2)}) collective-permute-start(bf16[2,256,768]{2,1,0:T(8,128)(2,1)} %pad_maximum_fusion.13), channel_id=1, source_target_pairs={{0,16},{16,0},{1,17},{17,1},{2,18},{18,2},{3,19},{19,3},{4,20},{20... | collective-permute-start | bytes 2359304 | tf_op jit(solution)/shard_map/ppermute | solution.py:32
  53.5 15.8 %collective-permute-start.12 = (bf16[192,2304]{1,0:T(8,128)(2,1)S(1)}, bf16[192,2304]{1,0:T(8,128)(2,1)S(1)}, u32[]{:S(2)}, u32[]{:S(2)}) collective-permute-start(bf16[192,2304]{1,0:T(8,128)(2,1)S(1)} %pad_maximum_fusion.12), channel_id=1, source_target_pairs={{0,4},{4,0},{8,12},{12,8},{1,5},{5,1},{9,13},{13,9},{2,6},{6,2},{1... | collective-permute-start | bytes 2654216 | tf_op jit(solution)/shard_map/ppermute | solution.py:32
  68.0 21.0 %collective-permute-start.7 = (bf16[400,1024]{1,0:T(8,128)(2,1)S(1)}, bf16[400,1024]{1,0:T(8,128)(2,1)S(1)}, u32[]{:S(2)}, u32[]{:S(2)}) collective-permute-start(bf16[400,1024]{1,0:T(8,128)(2,1)S(1)} %get-tuple-element.65.refs_0_), channel_id=1, source_target_pairs={{0,4},{4,0},{8,12},{12,8},{1,5},{5,1},{9,13},{13,9},{2,6},{6,2},{1... | collective-permute-start | bytes 2457608 | tf_op jit(solution)/shard_map/ppermute | solution.py:32
  68.1 20.9 %collective-permute-start.8 = (bf16[400,1024]{1,0:T(8,128)(2,1)S(1)}, bf16[400,1024]{1,0:T(8,128)(2,1)S(1)}, u32[]{:S(2)}, u32[]{:S(2)}) collective-permute-start(bf16[400,1024]{1,0:T(8,128)(2,1)S(1)} %get-tuple-element.65.refs_0_), channel_id=1, source_target_pairs={{0,8},{4,12},{8,0},{12,4},{1,9},{5,13},{9,1},{13,5},{2,10},{6,14},... | collective-permute-start | bytes 2457608 | tf_op jit(solution)/shard_map/ppermute | solution.py:32
  107.1 54.1 %collective-permute-start.21 = (bf16[256,768]{1,0:T(8,128)(2,1)S(1)}, bf16[256,768]{1,0:T(8,128)(2,1)}, u32[]{:S(2)}, u32[]{:S(2)}) collective-permute-start(bf16[256,768]{1,0:T(8,128)(2,1)S(1)} %copy-done.23), channel_id=1, source_target_pairs={{0,1},{1,0},{2,3},{3,2},{4,5},{5,4},{6,7},{7,6},{8,9},{9,8},{10,11... | collective-permute-start | bytes 1179656 | tf_op jit(solution)/shard_map/ppermute | solution.py:32
  109.5 51.7 %collective-permute-start.22 = (bf16[256,768]{1,0:T(8,128)(2,1)S(1)}, bf16[256,768]{1,0:T(8,128)(2,1)}, u32[]{:S(2)}, u32[]{:S(2)}) collective-permute-start(bf16[256,768]{1,0:T(8,128)(2,1)S(1)} %copy-done.23), channel_id=1, source_target_pairs={{0,2},{1,3},{2,0},{3,1},{4,6},{5,7},{6,4},{7,5},{8,10},{9,11},{10,... | collective-permute-start | bytes 1179656 | tf_op jit(solution)/shard_map/ppermute | solution.py:32
  110.8 50.5 %collective-permute-start.23 = (bf16[256,768]{1,0:T(8,128)(2,1)S(1)}, bf16[256,768]{1,0:T(8,128)(2,1)}, u32[]{:S(2)}, u32[]{:S(2)}) collective-permute-start(bf16[256,768]{1,0:T(8,128)(2,1)S(1)} %copy-done.23), channel_id=1, source_target_pairs={{0,3},{1,2},{2,1},{3,0},{4,7},{5,6},{6,5},{7,4},{8,11},{9,10},{10,... | collective-permute-start | bytes 1179656 | tf_op jit(solution)/shard_map/ppermute | solution.py:32
  111.0 39.3 %collective-permute-start.25 = (bf16[512,768]{1,0:T(8,128)(2,1)S(1)}, bf16[512,768]{1,0:T(8,128)(2,1)}, u32[]{:S(2)}, u32[]{:S(2)}) collective-permute-start(bf16[512,768]{1,0:T(8,128)(2,1)S(1)} %pad_maximum_fusion.16), channel_id=1, source_target_pairs={{0,16},{16,0},{1,17},{17,1},{2,18},{18,2},{3,19},{19,3},{4,20},{20... | collective-permute-start | bytes 2359304 | tf_op jit(solution)/shard_map/ppermute | solution.py:32
  111.9 48.9 %collective-permute-start.24 = (bf16[2,2,192,768]{3,2,1,0:T(8,128)(2,1)S(1)}, bf16[2,2,192,768]{3,2,1,0:T(8,128)(2,1)S(1)}, u32[]{:S(2)}, u32[]{:S(2)}) collective-permute-start(bf16[2,2,192,768]{3,2,1,0:T(8,128)(2,1)S(1)} %broadcast_select_fusion.8), channel_id=1, source_target_pairs={{0,1},{1,0},{2,3},{3,2},{4,5},{5,4},{6,7},{7,6},{8,9},{9,8},{10,11... | collective-permute-start | bytes 3538952 | tf_op jit(solution)/shard_map/ppermute | solution.py:32
  166.8 37.3 %collective-permute-start.27 = (bf16[1,384,1024]{2,1,0:T(8,128)(2,1)S(1)}, bf16[1,384,1024]{2,1,0:T(8,128)(2,1)}, u32[]{:S(2)}, u32[]{:S(2)}) collective-permute-start(bf16[1,384,1024]{2,1,0:T(8,128)(2,1)S(1)} %add_convert_fusion.2), channel_id=1, source_target_pairs={{0,8},{4,12},{8,0},{12,4},{1,9},{5,13},{9,1},{13,5},{2,10},{6,14},... | collective-permute-start | bytes 2359304 | tf_op jit(solution)/shard_map/ppermute | solution.py:32
  173.2 29.6 %collective-permute-start.33 = (bf16[2,2,96,768]{3,2,1,0:T(8,128)(2,1)}, bf16[2,2,96,768]{3,2,1,0:T(8,128)(2,1)}, u32[]{:S(2)}, u32[]{:S(2)}) collective-permute-start(bf16[2,2,96,768]{3,2,1,0:T(8,128)(2,1)} %broadcast_select_fusion.19), channel_id=1, source_target_pairs={{0,8},{4,12},{8,0},{12,4},{1,9},{5,13},{9,1},{13,5},{2,10},{6,14},... | collective-permute-start | bytes 1769480 | tf_op jit(solution)/shard_map/ppermute | solution.py:32
  207.3 16.1 %collective-permute-start.18 = (bf16[384,256]{1,0:T(8,128)(2,1)S(1)}, bf16[384,256]{1,0:T(8,128)(2,1)S(1)}, u32[]{:S(2)}, u32[]{:S(2)}) collective-permute-start(bf16[384,256]{1,0:T(8,128)(2,1)S(1)} %get-tuple-element.172), channel_id=1, source_target_pairs={{0,3},{1,2},{2,1},{3,0},{4,7},{5,6},{6,5},{7,4},{8,11},{9,10},{10,... | collective-permute-start | bytes 589832 | tf_op jit(solution)/shard_map/ppermute | solution.py:32
  209.6 16.6 %collective-permute-start.19 = (bf16[384,256]{1,0:T(8,128)(2,1)S(1)}, bf16[384,256]{1,0:T(8,128)(2,1)S(1)}, u32[]{:S(2)}, u32[]{:S(2)}) collective-permute-start(bf16[384,256]{1,0:T(8,128)(2,1)S(1)} %get-tuple-element.173), channel_id=1, source_target_pairs={{0,2},{1,3},{2,0},{3,1},{4,6},{5,7},{6,4},{7,5},{8,10},{9,11},{10,... | collective-permute-start | bytes 589832 | tf_op jit(solution)/shard_map/ppermute | solution.py:32
  209.6 16.6 %collective-permute-start.20 = (bf16[384,256]{1,0:T(8,128)(2,1)S(1)}, bf16[384,256]{1,0:T(8,128)(2,1)S(1)}, u32[]{:S(2)}, u32[]{:S(2)}) collective-permute-start(bf16[384,256]{1,0:T(8,128)(2,1)S(1)} %get-tuple-element.171), channel_id=1, source_target_pairs={{0,1},{1,0},{2,3},{3,2},{4,5},{5,4},{6,7},{7,6},{8,9},{9,8},{10,11... | collective-permute-start | bytes 589832 | tf_op jit(solution)/shard_map/ppermute | solution.py:32
  213.1 39.9 %collective-permute-start.31 = (bf16[4,96,768]{2,1,0:T(8,128)(2,1)}, bf16[4,96,768]{2,1,0:T(8,128)(2,1)}, u32[]{:S(2)}, u32[]{:S(2)}) collective-permute-start(bf16[4,96,768]{2,1,0:T(8,128)(2,1)} %broadcast_select_fusion.20), channel_id=1, source_target_pairs={{0,4},{4,0},{8,12},{12,8},{1,5},{5,1},{9,13},{13,9},{2,6},{6,2},{1... | collective-permute-start | bytes 1769480 | tf_op jit(solution)/shard_map/ppermute | solution.py:32
  227.8 24.1 %collective-permute-start.34 = (bf16[2,2,48,768]{3,2,1,0:T(8,128)(2,1)}, bf16[2,2,48,768]{3,2,1,0:T(8,128)(2,1)}, u32[]{:S(2)}, u32[]{:S(2)}) collective-permute-start(bf16[2,2,48,768]{3,2,1,0:T(8,128)(2,1)} %broadcast_select_fusion.25), channel_id=1, source_target_pairs={{0,2},{1,3},{2,0},{3,1},{4,6},{5,7},{6,4},{7,5},{8,10},{9,11},{10,... | collective-permute-start | bytes 884744 | tf_op jit(solution)/shard_map/ppermute | solution.py:32
  231.4 32.5 %collective-permute-start.28 = (bf16[384,256]{1,0:T(8,128)(2,1)}, bf16[384,256]{1,0:T(8,128)(2,1)S(1)}, u32[]{:S(2)}, u32[]{:S(2)}) collective-permute-start(bf16[384,256]{1,0:T(8,128)(2,1)} %get-tuple-element.166), channel_id=1, source_target_pairs={{0,1},{1,0},{2,3},{3,2},{4,5},{5,4},{6,7},{7,6},{8,9},{9,8},{10,11... | collective-permute-start | bytes 589832 | tf_op jit(solution)/shard_map/ppermute | solution.py:32
  231.4 32.5 %collective-permute-start.29 = (bf16[384,256]{1,0:T(8,128)(2,1)}, bf16[384,256]{1,0:T(8,128)(2,1)S(1)}, u32[]{:S(2)}, u32[]{:S(2)}) collective-permute-start(bf16[384,256]{1,0:T(8,128)(2,1)} %get-tuple-element.167), channel_id=1, source_target_pairs={{0,2},{1,3},{2,0},{3,1},{4,6},{5,7},{6,4},{7,5},{8,10},{9,11},{10,... | collective-permute-start | bytes 589832 | tf_op jit(solution)/shard_map/ppermute | solution.py:32
  233.2 30.6 %collective-permute-start.30 = (bf16[384,256]{1,0:T(8,128)(2,1)S(1)}, bf16[384,256]{1,0:T(8,128)(2,1)S(1)}, u32[]{:S(2)}, u32[]{:S(2)}) collective-permute-start(bf16[384,256]{1,0:T(8,128)(2,1)S(1)} %copy-done.65), channel_id=1, source_target_pairs={{0,3},{1,2},{2,1},{3,0},{4,7},{5,6},{6,5},{7,4},{8,11},{9,10},{10,... | collective-permute-start | bytes 589832 | tf_op jit(solution)/shard_map/ppermute | solution.py:32
  256.3 16.3 %collective-permute-start.35 = (bf16[48,768]{1,0:T(8,128)(2,1)}, bf16[48,768]{1,0:T(8,128)(2,1)}, u32[]{:S(2)}, u32[]{:S(2)}) collective-permute-start(bf16[48,768]{1,0:T(8,128)(2,1)} %select_bitcast_fusion), channel_id=1, source_target_pairs={{0,16},{16,0},{1,17},{17,1},{2,18},{18,2},{3,19},{19,3},{4,20},{20... | collective-permute-start | bytes 221192 | tf_op jit(solution)/shard_map/ppermute | solution.py:32
  273.5 25.1 %collective-permute-start.36 = (bf16[4,48,768]{2,1,0:T(8,128)(2,1)S(1)}, bf16[4,48,768]{2,1,0:T(8,128)(2,1)S(1)}, u32[]{:S(2)}, u32[]{:S(2)}) collective-permute-start(bf16[4,48,768]{2,1,0:T(8,128)(2,1)S(1)} %pad_maximum_fusion.27), channel_id=1, source_target_pairs={{0,2},{1,3},{2,0},{3,1},{4,6},{5,7},{6,4},{7,5},{8,10},{9,11},{10,... | collective-permute-start | bytes 884744 | tf_op jit(solution)/shard_map/ppermute | solution.py:32
  278.9 25.9 %collective-permute-start.38 = (bf16[6,48,384]{2,1,0:T(8,128)(2,1)S(1)}, bf16[6,48,384]{2,1,0:T(8,128)(2,1)S(1)}, u32[]{:S(2)}, u32[]{:S(2)}) collective-permute-start(bf16[6,48,384]{2,1,0:T(8,128)(2,1)S(1)} %add_convert_fusion.9), channel_id=1, source_target_pairs={{0,3},{1,2},{2,1},{3,0},{4,7},{5,6},{6,5},{7,4},{8,11},{9,10},{10,... | collective-permute-start | bytes 663560 | tf_op jit(solution)/shard_map/ppermute | solution.py:32
  279.7 28.4 %collective-permute-start.39 = (bf16[6,48,384]{2,1,0:T(8,128)(2,1)S(1)}, bf16[6,48,384]{2,1,0:T(8,128)(2,1)S(1)}, u32[]{:S(2)}, u32[]{:S(2)}) collective-permute-start(bf16[6,48,384]{2,1,0:T(8,128)(2,1)S(1)} %add_convert_fusion.9), channel_id=1, source_target_pairs={{0,2},{1,3},{2,0},{3,1},{4,6},{5,7},{6,4},{7,5},{8,10},{9,11},{10,... | collective-permute-start | bytes 663560 | tf_op jit(solution)/shard_map/ppermute | solution.py:32
  283.7 24.4 %collective-permute-start.40 = (bf16[6,48,384]{2,1,0:T(8,128)(2,1)S(1)}, bf16[6,48,384]{2,1,0:T(8,128)(2,1)S(1)}, u32[]{:S(2)}, u32[]{:S(2)}) collective-permute-start(bf16[6,48,384]{2,1,0:T(8,128)(2,1)S(1)} %add_convert_fusion.9), channel_id=1, source_target_pairs={{0,1},{1,0},{2,3},{3,2},{4,5},{5,4},{6,7},{7,6},{8,9},{9,8},{10,11... | collective-permute-start | bytes 663560 | tf_op jit(solution)/shard_map/ppermute | solution.py:32
  298.7 19.5 %collective-permute-start.43 = (bf16[4,1,96,768]{3,2,1,0:T(8,128)(2,1)S(1)}, bf16[4,1,96,768]{3,2,1,0:T(8,128)(2,1)S(1)}, u32[]{:S(2)}, u32[]{:S(2)}) collective-permute-start(bf16[4,1,96,768]{3,2,1,0:T(8,128)(2,1)S(1)} %fusion.84), channel_id=1, source_target_pairs={{0,1},{1,0},{2,3},{3,2},{4,5},{5,4},{6,7},{7,6},{8,9},{9,8},{10,11... | collective-permute-start | bytes 1769480 | tf_op jit(solution)/shard_map/ppermute | solution.py:32
  318.5 26.1 %collective-permute-start.44 = (bf16[4,2,1,96,768]{4,3,2,1,0:T(8,128)(2,1)S(1)}, bf16[4,2,1,96,768]{4,3,2,1,0:T(8,128)(2,1)S(1)}, u32[]{:S(2)}, u32[]{:S(2)}) collective-permute-start(bf16[4,2,1,96,768]{4,3,2,1,0:T(8,128)(2,1)S(1)} %maximum_bitcast_fusion), channel_id=1, source_target_pairs={{0,8},{4,12},{8,0},{12,4},{1,9},{5,13},{9,1},{13,5},{2,10},{6,14},... | collective-permute-start | bytes 3538952 | tf_op jit(solution)/shard_map/ppermute | solution.py:32
  323.8 34.3 %collective-permute-start.41 = (bf16[17,48,384]{2,1,0:T(8,128)(2,1)}, bf16[17,48,384]{2,1,0:T(8,128)(2,1)}, u32[]{:S(2)}, u32[]{:S(2)}) collective-permute-start(bf16[17,48,384]{2,1,0:T(8,128)(2,1)} %get-tuple-element.117), channel_id=1, source_target_pairs={{0,8},{4,12},{8,0},{12,4},{1,9},{5,13},{9,1},{13,5},{2,10},{6,14},... | collective-permute-start | bytes 1880072 | tf_op jit(solution)/shard_map/ppermute | solution.py:32
  345.0 23.7 %collective-permute-start.45 = (bf16[4,384,768]{2,1,0:T(8,128)(2,1)S(1)}, bf16[4,384,768]{2,1,0:T(8,128)(2,1)}, u32[]{:S(2)}, u32[]{:S(2)}) collective-permute-start(bf16[4,384,768]{2,1,0:T(8,128)(2,1)S(1)} %bitcast.88), channel_id=1, source_target_pairs={{0,4},{4,0},{8,12},{12,8},{1,5},{5,1},{9,13},{13,9},{2,6},{6,2},{1... | collective-permute-start | bytes 7077896 | tf_op jit(solution)/shard_map/ppermute | solution.py:32
  (111 other events, 806.0 us)

commit v3 on v1

--- a/solution.py
+++ b/solution.py
@@ -207,7 +207,7 @@
         i, at = t // own, (t % own) * STRETCH
         to = keep_ref if i % 2 == 0 else send_ref
         for h in heads:
-            turned = sums[h, rank[t]].T.astype(bf16)
+            turned = sums[h, rank[t]].astype(bf16).T
             first = h * HEAD
             to[i // 2, cols + first : cols + first + HEAD, at : at + STRETCH] = turned[:HEAD]
             to[i // 2, first : first + HEAD, at : at + STRETCH] = turned[HEAD:]
@@ -382,10 +382,7 @@
     got = swap(jnp.where(side == 0, sums[0, 1], sums[0, 0]), "fsdp", 1)
     kept = jnp.where(side == 0, sums[0, 0], sums[0, 1])
     sums = jnp.concatenate([in_order(side, kept[None], got[None]), sums[1]], 0)
-    return share_half(sums, "ulysses", 2, 1)
-
-
-def spread_pair(sums):
+    sums = share_half(sums, "ulysses", 2, 1)
     sums = share_half(sums, "ulysses", 1, 1)
     sums = share_half(sums, "blk", 2, 1)
     return place_mlp(bit_of("blk", 1), sums, swap(sums, "blk", 1))
@@ -496,7 +493,7 @@
     return add_half(halves_of(add_half(halves_of(grads, 1), "blk", 1), 1), "blk", 2)
 
 
-def attention_grads(grads, vector, output, g_up):
+def attention_grads(grads, vector, output):
     side = lax.axis_index("fsdp")
     group = lax.axis_index("ulysses")
     groups = lax.axis_size("ulysses")
@@ -528,7 +525,7 @@
     kept = in_order(bit_of("blk", 2), kept, got[:units], 1)
     small = (small.astype(f32) + got[units:].astype(f32)).astype(bf16)
     wide = jnp.pad(small, ((0, 0), (0, rows), (0, 0)))
-    got = after(swap(jnp.concatenate([kept, wide]), "blk", 1), g_up)
+    got = swap(jnp.concatenate([kept, wide]), "blk", 1)
     small = small.astype(f32) + got[units:, :rows].astype(f32)
     g_qkv, g_out = place_qkv(bit_of("blk", 1), kept, got)
     return g_qkv, g_out, small.reshape(-1)[:size]
@@ -577,17 +574,15 @@
         half_up = jnp.concatenate([units_of(up_weight, 1 - side), out_weight], 1)
         part_up = swap(after(quarter_of(half_up), part_qkv), "fsdp", 1)
         x_e = swap(after(jnp.stack([tokens, cotangent]), part_up), "fsdp", 1)
-        half_qkv = share_half(part_qkv, "blk", 2, 0)
-        w_qkv = both_shards(qkv_weight, half_qkv)
-        half_up = share_half(after(part_up, half_qkv), "blk", 2, 0)
+        w_qkv = both_shards(qkv_weight, share_half(part_qkv, "blk", 2, 0))
+        half_up = share_half(part_up, "blk", 2, 0)
         x_all = around(x_ranks)
         mine = jnp.concatenate([units_of(up_weight, side), out_weight], 1)
         half_up = both_shards(mine, half_up)
         w_up, w_out = half_up[:, :-width], half_up[:, -width:]
         x_mlp = jnp.concatenate([tokens, x_e[0]])
         e_mlp = jnp.concatenate([cotangent, x_e[1]])
-        b_up, w_down = up_bias, down_weight
-        mlp, finish, spread = mlp_pair, finish_pair, spread_pair
+        b_up, w_down, mlp, finish = up_bias, down_weight, mlp_pair, finish_pair
     else:
         x_all, part_qkv = around(x_ranks), x_ranks
         w_qkv, w_up, w_out, w_down = (
@@ -595,8 +590,7 @@
             for w in (qkv_weight, up_weight, out_weight, down_weight)
         )
         b_up = gather_small(up_bias).reshape(-1)
-        x_mlp, e_mlp = tokens, cotangent
-        mlp, finish, spread = mlp_gathered, lambda v, _: v, lambda v: v
+        x_mlp, e_mlp, mlp, finish = tokens, cotangent, mlp_gathered, lambda v, _: v
     small = jnp.concatenate([ln1_gain, ln1_bias, ln2_gain, ln2_bias, out_bias, down_bias, qkv_bias])
     small = gather_small(after(small, part_qkv))
     part = width // shards
@@ -639,9 +633,9 @@
     while len(kept) > 1:
         step *= 2
         sent = sum(v.astype(f32) for v in stacked_terms(kept[1::2])).astype(bf16)
-        terms = finish(terms, sent) if step == 2 else terms
         got = swap(sent, "blk", step)
         kept = [kept[2 * i] + [got[i]] for i in range(got.shape[0])]
+    g_up, g_down = finish(terms, sent)
     total = sum(v.astype(f32) for v in kept[0])
     d_q = rotate(d_q, cosine, -sine).astype(bf16).reshape(cols, rows)
     mixed = mixed.reshape(cols, rows)
@@ -656,8 +650,6 @@
     back_kv = to_tokens(d_kv)
     grads = jnp.concatenate([g_qkv.reshape(3, cols, width), g_out[None]])
     grads = add_blks(grads)
-    back_kv = after(back_kv, grads, terms)
-    g_up, g_down = spread(terms)
     back_q, back_kv = by_device(back_q, group), by_device(back_kv, group)
     d_mine = jnp.concatenate(
         [v[:cols] for v in back_q] + [v[:cols] for v in back_kv] + [v[cols:] for v in back_kv], 0
@@ -678,7 +670,7 @@
     output = (x_float + (attn_out + b_out) + (mlp_out + b_down)).astype(bf16)
     input_grad = (e_float + d_x_one + d_x_two).astype(bf16)
 
-    g_qkv, g_out, summed = attention_grads(grads, jnp.concatenate(vectors), output, g_up)
+    g_qkv, g_out, summed = attention_grads(grads, jnp.concatenate(vectors), output)
     results, start = [], 0
     for vector in vectors:
         mine = vector.shape[0] // shards

time: 337 us -> 327 us (0.970)
  starting transfers between devices: 68.9 us -> 79.7 us
  waiting for transfers between devices: 95.3 us -> 85.1 us
  Pallas kernels: 59.2 us -> 49.9 us
    ppermute x46, starting transfers between devices: 68.9 us -> 79.7 us  [swap(): return lax.ppermute(values, axis, [(i, i ^ bits) for i in range(count)])]
    ppermute x46, waiting for transfers between devices: 95.3 us -> 85.1 us  [swap(): return lax.ppermute(values, axis, [(i, i ^ bits) for i in range(count)])]
    pallas_call x1, Pallas kernels: 45.7 us -> 37.2 us  [attend(): pl.pallas_call(attend_kernel, grid_spec=pltpu.PrefetchScalarGridSpec(num_...]
    unnamed x181 -> x185, local copies, waits for them, and re-layouts: 19.2 us -> 18.5 us
    select_n x11 -> x10, other arithmetic: 6.64 us -> 6.88 us  [in_order(): jnp.where(bit == 0, mine, other)]
  transfers between devices with their start and end apart: 46 -> 46, of which waited for: 18 -> 19; matrix products, arithmetic and copies ran while one was open for 25% -> 26% of each run, Pallas kernels for 17% -> 13%
where the time goes in v3:
time: 327 us; the launch traced here: 323 us
  waiting for transfers between devices  85.1 us (26%)
  starting transfers between devices  79.7 us (24%)
  other arithmetic  54.1 us (17%)
  Pallas kernels  49.9 us (15%)
  local copies, waits for them, and re-layouts  28 us (9%)
  matrix products  23.6 us (7%)
    ppermute x46, waiting for transfers between devices, swap(): return lax.ppermute(values, axis, [(i, i ^ bits) for i in range(count)])  85.1 us
    ppermute x46, starting transfers between devices, swap(): return lax.ppermute(values, axis, [(i, i ^ bits) for i in range(count)])  79.7 us
    pallas_call x1, Pallas kernels, attend(): pl.pallas_call(attend_kernel, grid_spec=pltpu.PrefetchScalarGridSpec(num_...  37.2 us
    unnamed x185, local copies, waits for them, and re-layouts  18.5 us
    dot_general x1, matrix products, mlp_pair(): jnp.dot(normed, up, preferred_element_type=f32) + up_bias.astype(f32)  8.15 us
    select_n x10, other arithmetic, in_order(): jnp.where(bit == 0, mine, other)  6.88 us
  transfers between devices with their start and end apart: 46, of which 19 were waited for; matrix products, arithmetic and copies ran while one was open for 26% of the time, Pallas kernels for 13%

profile of v3, /device:TPU:9, one launch (start us, length us, event | category | flops | bytes accessed | tf_op | source)
XLA Modules:
  0.0 322.8 jit_solution(9373135999408247975)
XLA Ops:
  9.3 3.2 %broadcast_select_fusion.10 = (bf16[384,1536]{1,0:T(8,128)(2,1)}, bf16[384,1536]{1,0:T(8,128)(2,1)}) fusion(pred[]{:T(512)S(6)} %eq.45, bf16[384,3072]{1,0:T(8,128)(2,1)} %param.27, pred[]{:T(512)S(6)} %eq.48), kind=kLoop, calls=%fused_computation.100 | loop fusion | flops 1179648 | bytes 4718594 | tf_op jit(solution)/shard_map/jit(_where)/select_n | solution.py:344
  16.1 2.6 collective-permute-done
  23.0 7.8 %collective-permute-done.10 = bf16[96,2304]{1,0:T(8,128)(2,1)} collective-permute-done((bf16[96,2304]{1,0:T(8,128)(2,1)}, bf16[96,2304]{1,0:T(8,128)(2,1)}, u32[]{:S(2)}, u32[]{:S(2)}) %collective-permute-start.10) | collective-permute-done | bytes 442400 | tf_op jit(solution)/shard_map/ppermute | solution.py:32
  32.5 7.9 %collective-permute-done.11 = bf16[96,2304]{1,0:T(8,128)(2,1)} collective-permute-done((bf16[96,2304]{1,0:T(8,128)(2,1)}, bf16[96,2304]{1,0:T(8,128)(2,1)}, u32[]{:S(2)}, u32[]{:S(2)}) %collective-permute-start.11) | collective-permute-done | bytes 442400 | tf_op jit(solution)/shard_map/ppermute | solution.py:32
  43.9 3.7 %collective-permute-start.3 = (bf16[192,2304]{1,0:T(8,128)(2,1)}, bf16[192,2304]{1,0:T(8,128)(2,1)}, u32[]{:S(2)}, u32[]{:S(2)}) collective-permute-start(bf16[192,2304]{1,0:T(8,128)(2,1)} %pad_maximum_fusion.13), channel_id=1, source_target_pairs={{0,4},{4,0},{8,12},{12,8},{1,5},{5,1},{9,13},{13,9},{2,6},{6,2},{1... | collective-permute-start | bytes 2654216 | tf_op jit(solution)/shard_map/ppermute | solution.py:32
  49.1 3.4 %collective-permute-start.12 = (bf16[192,2304]{1,0:T(8,128)(2,1)S(1)}, bf16[192,2304]{1,0:T(8,128)(2,1)S(1)}, u32[]{:S(2)}, u32[]{:S(2)}) collective-permute-start(bf16[192,2304]{1,0:T(8,128)(2,1)S(1)} %pad_maximum_fusion.14), channel_id=1, source_target_pairs={{0,4},{4,0},{8,12},{12,8},{1,5},{5,1},{9,13},{13,9},{2,6},{6,2},{1... | collective-permute-start | bytes 2654216 | tf_op jit(solution)/shard_map/ppermute | solution.py:32
  58.7 3.5 %prepare.1 = (bf16[1024,768]{1,0:T(8,128)(2,1)S(1)}, bf16[192,1024]{1,0:T(8,128)(2,1)S(1)}, bf16[400,1024]{1,0:T(8,128)(2,1)S(1)}, f32[8,1024]{1,0:T(8,128)S(1)}, f32[8,1024]{1,0:T(8,128)S(1)}) custom-call(f32[8,1]{1,0:T(8,128)S(1)} %copy-done.6, f32[1,768]{1,0:T(1,128)S(1)} %bitcast.78, f32[1,768]{1,0:T(1,128)S(1)} %bitcast.77, ...), custom_call_target="tpu_custom_call" | custom-call | flops 905969664 | bytes 6291456 | tf_op jit(solution)/shard_map/prepare/pallas_call | solution.py:301
  71.3 8.2 %multiply_convert_fusion = (bf16[512,1536]{1,0:T(8,128)(2,1)S(1)}, f32[512,1536]{1,0:T(8,128)S(1)}, f32[512,1536]{1,0:T(8,128)S(1)}) fusion(f32[1536]{0:T(1024)S(1)} %convert_element_type.285, bf16[768,1536]{1,0:T(8,128)(2,1)S(1)} %pad_maximum_fusion.3, bf16[512,768]{1,0:T(8,128)(2,1)S(1)} %pad_maximum_fusion.16, f32[768]{0:T(1024)S(1)} %reshape.234, ...), kind=kOutput, calls=%fused_computation.18 | convolution fusion | flops 1262223360 | bytes 11026432 | tf_op jit(solution)/shard_map/dot_general | solution.py:352
  98.9 37.2 %attend.1 = (bf16[3,64,1024]{2,1,0:T(8,128)(2,1)}, f32[3,64,1024]{2,1,0:T(8,128)}, bf16[2,384,1024]{2,1,0:T(8,128)(2,1)}, bf16[2,384,1024]{2,1,0:T(8,128)(2,1)}) custom-call(s32[32]{0:T(128)} %maximum_convert_fusion.5.rank, bf16[3,64,1024]{2,1,0:T(8,128)(2,1)} %bitcast.79, bf16[3,64,1024]{2,1,0:T(8,128)(2,1)} %bitcast.96, bf16[400,1024]{1,0:T(8,128)(2,1)} %copy-done.4, ...), custom_call_target="tpu_custom_call" | custom-call | flops 38654705664 | bytes 12582912 | tf_op jit(solution)/shard_map/attend/pallas_call | solution.py:224
  141.8 4.4 %collective-permute-start.23 = (bf16[2,384,1024]{2,1,0:T(8,128)(2,1)}, bf16[2,384,1024]{2,1,0:T(8,128)(2,1)}, u32[]{:S(2)}, u32[]{:S(2)}) collective-permute-start(bf16[2,384,1024]{2,1,0:T(8,128)(2,1)} %get-tuple-element.76), channel_id=1, source_target_pairs={{0,4},{4,0},{8,12},{12,8},{1,5},{5,1},{9,13},{13,9},{2,6},{6,2},{1... | collective-permute-start | bytes 4718600 | tf_op jit(solution)/shard_map/ppermute | solution.py:32
  146.3 3.2 %collective-permute-done.23 = bf16[2,384,1024]{2,1,0:T(8,128)(2,1)} collective-permute-done((bf16[2,384,1024]{2,1,0:T(8,128)(2,1)}, bf16[2,384,1024]{2,1,0:T(8,128)(2,1)}, u32[]{:S(2)}, u32[]{:S(2)}) %collective-permute-start.23) | collective-permute-done | bytes 1572896 | tf_op jit(solution)/shard_map/ppermute | solution.py:32
  155.8 8.1 %collective-permute-start.27 = (bf16[1,384,1024]{2,1,0:T(8,128)(2,1)}, bf16[1,384,1024]{2,1,0:T(8,128)(2,1)S(1)}, u32[]{:S(2)}, u32[]{:S(2)}) collective-permute-start(bf16[1,384,1024]{2,1,0:T(8,128)(2,1)} %add_convert_fusion.2), channel_id=1, source_target_pairs={{0,8},{4,12},{8,0},{12,4},{1,9},{5,13},{9,1},{13,5},{2,10},{6,14},... | collective-permute-start | bytes 2359304 | tf_op jit(solution)/shard_map/ppermute | solution.py:32
  170.7 2.6 collective-permute-start.40
  173.3 8.2 %collective-permute-done.27 = bf16[1,384,1024]{2,1,0:T(8,128)(2,1)S(1)} collective-permute-done((bf16[1,384,1024]{2,1,0:T(8,128)(2,1)}, bf16[1,384,1024]{2,1,0:T(8,128)(2,1)S(1)}, u32[]{:S(2)}, u32[]{:S(2)}) %collective-permute-start.27) | collective-permute-done | bytes 786464 | tf_op jit(solution)/shard_map/ppermute | solution.py:32
  198.0 3.5 %collective-permute-done.41 = bf16[48,768]{1,0:T(8,128)(2,1)S(1)} collective-permute-done((bf16[48,768]{1,0:T(8,128)(2,1)S(1)}, bf16[48,768]{1,0:T(8,128)(2,1)S(1)}, u32[]{:S(2)}, u32[]{:S(2)}) %collective-permute-start.41) | collective-permute-done | bytes 73760 | tf_op jit(solution)/shard_map/ppermute | solution.py:32
  204.6 3.2 collective-permute-start.31
  207.8 8.3 %collective-permute-done.24 = bf16[384,256]{1,0:T(8,128)(2,1)S(1)} collective-permute-done((bf16[384,256]{1,0:T(8,128)(2,1)S(1)}, bf16[384,256]{1,0:T(8,128)(2,1)S(1)}, u32[]{:S(2)}, u32[]{:S(2)}) %collective-permute-start.24) | collective-permute-done | bytes 196640 | tf_op jit(solution)/shard_map/ppermute | solution.py:32
  219.7 3.8 %collective-permute-done.28 = bf16[384,256]{1,0:T(8,128)(2,1)S(1)} collective-permute-done((bf16[384,256]{1,0:T(8,128)(2,1)S(1)}, bf16[384,256]{1,0:T(8,128)(2,1)S(1)}, u32[]{:S(2)}, u32[]{:S(2)}) %collective-permute-start.28) | collective-permute-done | bytes 196640 | tf_op jit(solution)/shard_map/ppermute | solution.py:32
  223.5 7.5 %collective-permute-done.29 = bf16[384,256]{1,0:T(8,128)(2,1)S(1)} collective-permute-done((bf16[384,256]{1,0:T(8,128)(2,1)S(1)}, bf16[384,256]{1,0:T(8,128)(2,1)S(1)}, u32[]{:S(2)}, u32[]{:S(2)}) %collective-permute-start.29) | collective-permute-done | bytes 196640 | tf_op jit(solution)/shard_map/ppermute | solution.py:32
  240.7 3.8 %collective-permute-start.32 = (bf16[4,48,768]{2,1,0:T(8,128)(2,1)S(1)}, bf16[4,48,768]{2,1,0:T(8,128)(2,1)S(1)}, u32[]{:S(2)}, u32[]{:S(2)}) collective-permute-start(bf16[4,48,768]{2,1,0:T(8,128)(2,1)S(1)} %broadcast_select_fusion.28), channel_id=1, source_target_pairs={{0,8},{4,12},{8,0},{12,4},{1,9},{5,13},{9,1},{13,5},{2,10},{6,14},... | collective-permute-start | bytes 884744 | tf_op jit(solution)/shard_map/ppermute | solution.py:32
  247.4 3.4 %collective-permute-done.32 = bf16[4,48,768]{2,1,0:T(8,128)(2,1)S(1)} collective-permute-done((bf16[4,48,768]{2,1,0:T(8,128)(2,1)S(1)}, bf16[4,48,768]{2,1,0:T(8,128)(2,1)S(1)}, u32[]{:S(2)}, u32[]{:S(2)}) %collective-permute-start.32) | collective-permute-done | bytes 294944 | tf_op jit(solution)/shard_map/ppermute | solution.py:32
  251.1 5.3 %collective-permute-done.33 = bf16[6,48,384]{2,1,0:T(8,128)(2,1)} collective-permute-done((bf16[6,48,384]{2,1,0:T(8,128)(2,1)S(1)}, bf16[6,48,384]{2,1,0:T(8,128)(2,1)}, u32[]{:S(2)}, u32[]{:S(2)}) %collective-permute-start.33) | collective-permute-done | bytes 221216 | tf_op jit(solution)/shard_map/ppermute | solution.py:32
  257.5 3.2 collective-permute-start.35
  263.1 2.6 collective-permute-done.36
  265.7 6.2 %collective-permute-done.35 = bf16[6,48,384]{2,1,0:T(8,128)(2,1)S(1)} collective-permute-done((bf16[6,48,384]{2,1,0:T(8,128)(2,1)S(1)}, bf16[6,48,384]{2,1,0:T(8,128)(2,1)S(1)}, u32[]{:S(2)}, u32[]{:S(2)}) %collective-permute-start.35) | collective-permute-done | bytes 221216 | tf_op jit(solution)/shard_map/ppermute | solution.py:32
  271.9 6.2 %collective-permute-done.34 = bf16[6,48,384]{2,1,0:T(8,128)(2,1)S(1)} collective-permute-done((bf16[6,48,384]{2,1,0:T(8,128)(2,1)S(1)}, bf16[6,48,384]{2,1,0:T(8,128)(2,1)S(1)}, u32[]{:S(2)}, u32[]{:S(2)}) %collective-permute-start.34) | collective-permute-done | bytes 221216 | tf_op jit(solution)/shard_map/ppermute | solution.py:32
  278.5 2.6 collective-permute-start.37
  281.1 3.3 %collective-permute-done.44 = bf16[4,192,768]{2,1,0:T(8,128)(2,1)S(1)} collective-permute-done((bf16[4,192,768]{2,1,0:T(8,128)(2,1)S(1)}, bf16[4,192,768]{2,1,0:T(8,128)(2,1)S(1)}, u32[]{:S(2)}, u32[]{:S(2)}) %collective-permute-start.44) | collective-permute-done | bytes 1179680 | tf_op jit(solution)/shard_map/ppermute | solution.py:32
  286.5 11.8 %collective-permute-start.45 = (bf16[4,384,768]{2,1,0:T(8,128)(2,1)}, bf16[4,384,768]{2,1,0:T(8,128)(2,1)}, u32[]{:S(2)}, u32[]{:S(2)}) collective-permute-start(bf16[4,384,768]{2,1,0:T(8,128)(2,1)} %pad_maximum_fusion.4.mine), channel_id=1, source_target_pairs={{0,4},{4,0},{8,12},{12,8},{1,5},{5,1},{9,13},{13,9},{2,6},{6,2},{1... | collective-permute-start | bytes 7077896 | tf_op jit(solution)/shard_map/ppermute | solution.py:32
  301.8 3.8 %collective-permute-start.38 = (bf16[17,96,384]{2,1,0:T(8,128)(2,1)}, bf16[17,96,384]{2,1,0:T(8,128)(2,1)S(1)}, u32[]{:S(2)}, u32[]{:S(2)}) collective-permute-start(bf16[17,96,384]{2,1,0:T(8,128)(2,1)} %fusion.27), channel_id=1, source_target_pairs={{0,4},{4,0},{8,12},{12,8},{1,5},{5,1},{9,13},{13,9},{2,6},{6,2},{1... | collective-permute-start | bytes 3760136 | tf_op jit(solution)/shard_map/ppermute | solution.py:32
  312.8 2.8 place_qkv.1
  315.5 6.4 %place_mlp.1 = (f32[384,3072]{1,0:T(8,128)}, f32[2,2,384,768]{3,2,1,0:T(8,128)}) custom-call(s32[1]{0:T(128)} %bitcast.24.which, bf16[4,384,768]{2,1,0:T(8,128)(2,1)} %pad_maximum_fusion.4.mine, bf16[4,384,768]{2,1,0:T(8,128)(2,1)} %collective-permute-done.45.other), custom_call_target="tpu_custom_call" | custom-call | bytes 14155776 | tf_op jit(solution)/shard_map/place_mlp/pallas_call | solution.py:404
  (388 shorter events, 128.6 us)
Async XLA Ops:
  2.6 55.7 %collective-permute-start.6 = (bf16[272,768]{1,0:T(8,128)(2,1)S(1)}, bf16[272,768]{1,0:T(8,128)(2,1)S(1)}, u32[]{:S(2)}, u32[]{:S(2)}) collective-permute-start(bf16[272,768]{1,0:T(8,128)(2,1)S(1)} %fusion.52.refs_0_), channel_id=1, source_target_pairs={{0,3},{1,2},{2,1},{3,0},{4,7},{5,6},{6,5},{7,4},{8,11},{9,10},{10,... | collective-permute-start | bytes 1253384 | tf_op jit(solution)/shard_map/ppermute | solution.py:32
  4.0 54.4 %collective-permute-start.5 = (bf16[272,768]{1,0:T(8,128)(2,1)S(1)}, bf16[272,768]{1,0:T(8,128)(2,1)}, u32[]{:S(2)}, u32[]{:S(2)}) collective-permute-start(bf16[272,768]{1,0:T(8,128)(2,1)S(1)} %fusion.52.refs_0_), channel_id=1, source_target_pairs={{0,2},{1,3},{2,0},{3,1},{4,6},{5,7},{6,4},{7,5},{8,10},{9,11},{10,... | collective-permute-start | bytes 1253384 | tf_op jit(solution)/shard_map/ppermute | solution.py:32
  5.1 53.3 %collective-permute-start.4 = (bf16[272,768]{1,0:T(8,128)(2,1)S(1)}, bf16[272,768]{1,0:T(8,128)(2,1)}, u32[]{:S(2)}, u32[]{:S(2)}) collective-permute-start(bf16[272,768]{1,0:T(8,128)(2,1)S(1)} %fusion.52.refs_0_), channel_id=1, source_target_pairs={{0,1},{1,0},{2,3},{3,2},{4,5},{5,4},{6,7},{7,6},{8,9},{9,8},{10,11... | collective-permute-start | bytes 1253384 | tf_op jit(solution)/shard_map/ppermute | solution.py:32
  32.2 16.9 %collective-permute-start.16 = (bf16[2,256,768]{2,1,0:T(8,128)(2,1)}, bf16[2,256,768]{2,1,0:T(8,128)(2,1)}, u32[]{:S(2)}, u32[]{:S(2)}) collective-permute-start(bf16[2,256,768]{2,1,0:T(8,128)(2,1)} %pad_maximum_fusion.15), channel_id=1, source_target_pairs={{0,16},{16,0},{1,17},{17,1},{2,18},{18,2},{3,19},{19,3},{4,20},{20... | collective-permute-start | bytes 2359304 | tf_op jit(solution)/shard_map/ppermute | solution.py:32
  49.1 13.8 %collective-permute-start.12 = (bf16[192,2304]{1,0:T(8,128)(2,1)S(1)}, bf16[192,2304]{1,0:T(8,128)(2,1)S(1)}, u32[]{:S(2)}, u32[]{:S(2)}) collective-permute-start(bf16[192,2304]{1,0:T(8,128)(2,1)S(1)} %pad_maximum_fusion.14), channel_id=1, source_target_pairs={{0,4},{4,0},{8,12},{12,8},{1,5},{5,1},{9,13},{13,9},{2,6},{6,2},{1... | collective-permute-start | bytes 2654216 | tf_op jit(solution)/shard_map/ppermute | solution.py:32
  62.3 20.3 %collective-permute-start.8 = (bf16[400,1024]{1,0:T(8,128)(2,1)S(1)}, bf16[400,1024]{1,0:T(8,128)(2,1)S(1)}, u32[]{:S(2)}, u32[]{:S(2)}) collective-permute-start(bf16[400,1024]{1,0:T(8,128)(2,1)S(1)} %get-tuple-element.58.refs_0_), channel_id=1, source_target_pairs={{0,8},{4,12},{8,0},{12,4},{1,9},{5,13},{9,1},{13,5},{2,10},{6,14},... | collective-permute-start | bytes 2457608 | tf_op jit(solution)/shard_map/ppermute | solution.py:32
  62.6 20.0 %collective-permute-start.7 = (bf16[400,1024]{1,0:T(8,128)(2,1)S(1)}, bf16[400,1024]{1,0:T(8,128)(2,1)S(1)}, u32[]{:S(2)}, u32[]{:S(2)}) collective-permute-start(bf16[400,1024]{1,0:T(8,128)(2,1)S(1)} %get-tuple-element.58.refs_0_), channel_id=1, source_target_pairs={{0,4},{4,0},{8,12},{12,8},{1,5},{5,1},{9,13},{13,9},{2,6},{6,2},{1... | collective-permute-start | bytes 2457608 | tf_op jit(solution)/shard_map/ppermute | solution.py:32
  67.7 14.1 %collective-permute-start.15 = (bf16[192,256]{1,0:T(8,128)(2,1)S(1)}, bf16[192,256]{1,0:T(8,128)(2,1)S(1)}, u32[]{:S(2)}, u32[]{:S(2)}) collective-permute-start(bf16[192,256]{1,0:T(8,128)(2,1)S(1)} %get-tuple-element.171), channel_id=1, source_target_pairs={{0,3},{1,2},{2,1},{3,0},{4,7},{5,6},{6,5},{7,4},{8,11},{9,10},{10,... | collective-permute-start | bytes 294920 | tf_op jit(solution)/shard_map/ppermute | solution.py:32
  69.0 12.9 %collective-permute-start.14 = (bf16[192,256]{1,0:T(8,128)(2,1)S(1)}, bf16[192,256]{1,0:T(8,128)(2,1)S(1)}, u32[]{:S(2)}, u32[]{:S(2)}) collective-permute-start(bf16[192,256]{1,0:T(8,128)(2,1)S(1)} %get-tuple-element.172), channel_id=1, source_target_pairs={{0,2},{1,3},{2,0},{3,1},{4,6},{5,7},{6,4},{7,5},{8,10},{9,11},{10,... | collective-permute-start | bytes 294920 | tf_op jit(solution)/shard_map/ppermute | solution.py:32
  70.0 11.9 %collective-permute-start.13 = (bf16[192,256]{1,0:T(8,128)(2,1)S(1)}, bf16[192,256]{1,0:T(8,128)(2,1)S(1)}, u32[]{:S(2)}, u32[]{:S(2)}) collective-permute-start(bf16[192,256]{1,0:T(8,128)(2,1)S(1)} %get-tuple-element.173), channel_id=1, source_target_pairs={{0,1},{1,0},{2,3},{3,2},{4,5},{5,4},{6,7},{7,6},{8,9},{9,8},{10,11... | collective-permute-start | bytes 294920 | tf_op jit(solution)/shard_map/ppermute | solution.py:32
  94.0 47.7 %collective-permute-start.20 = (bf16[256,768]{1,0:T(8,128)(2,1)S(1)}, bf16[256,768]{1,0:T(8,128)(2,1)}, u32[]{:S(2)}, u32[]{:S(2)}) collective-permute-start(bf16[256,768]{1,0:T(8,128)(2,1)S(1)} %copy-done.21), channel_id=1, source_target_pairs={{0,3},{1,2},{2,1},{3,0},{4,7},{5,6},{6,5},{7,4},{8,11},{9,10},{10,... | collective-permute-start | bytes 1179656 | tf_op jit(solution)/shard_map/ppermute | solution.py:32
  95.3 46.5 %collective-permute-start.19 = (bf16[256,768]{1,0:T(8,128)(2,1)S(1)}, bf16[256,768]{1,0:T(8,128)(2,1)}, u32[]{:S(2)}, u32[]{:S(2)}) collective-permute-start(bf16[256,768]{1,0:T(8,128)(2,1)S(1)} %copy-done.21), channel_id=1, source_target_pairs={{0,2},{1,3},{2,0},{3,1},{4,6},{5,7},{6,4},{7,5},{8,10},{9,11},{10,... | collective-permute-start | bytes 1179656 | tf_op jit(solution)/shard_map/ppermute | solution.py:32
  97.2 44.6 %collective-permute-start.18 = (bf16[256,768]{1,0:T(8,128)(2,1)S(1)}, bf16[256,768]{1,0:T(8,128)(2,1)}, u32[]{:S(2)}, u32[]{:S(2)}) collective-permute-start(bf16[256,768]{1,0:T(8,128)(2,1)S(1)} %copy-done.21), channel_id=1, source_target_pairs={{0,1},{1,0},{2,3},{3,2},{4,5},{5,4},{6,7},{7,6},{8,9},{9,8},{10,11... | collective-permute-start | bytes 1179656 | tf_op jit(solution)/shard_map/ppermute | solution.py:32
  98.1 38.0 %collective-permute-start.22 = (bf16[512,768]{1,0:T(8,128)(2,1)S(1)}, bf16[512,768]{1,0:T(8,128)(2,1)}, u32[]{:S(2)}, u32[]{:S(2)}) collective-permute-start(bf16[512,768]{1,0:T(8,128)(2,1)S(1)} %pad_maximum_fusion.19), channel_id=1, source_target_pairs={{0,16},{16,0},{1,17},{17,1},{2,18},{18,2},{3,19},{19,3},{4,20},{20... | collective-permute-start | bytes 2359304 | tf_op jit(solution)/shard_map/ppermute | solution.py:32
  98.3 41.7 %collective-permute-start.21 = (bf16[2,2,192,768]{3,2,1,0:T(8,128)(2,1)S(1)}, bf16[2,2,192,768]{3,2,1,0:T(8,128)(2,1)}, u32[]{:S(2)}, u32[]{:S(2)}) collective-permute-start(bf16[2,2,192,768]{3,2,1,0:T(8,128)(2,1)S(1)} %broadcast_select_fusion.8), channel_id=1, source_target_pairs={{0,8},{4,12},{8,0},{12,4},{1,9},{5,13},{9,1},{13,5},{2,10},{6,14},... | collective-permute-start | bytes 3538952 | tf_op jit(solution)/shard_map/ppermute | solution.py:32
  153.0 14.9 %collective-permute-start.39 = (bf16[2,2,96,768]{3,2,1,0:T(8,128)(2,1)}, bf16[2,2,96,768]{3,2,1,0:T(8,128)(2,1)}, u32[]{:S(2)}, u32[]{:S(2)}) collective-permute-start(bf16[2,2,96,768]{3,2,1,0:T(8,128)(2,1)} %broadcast_select_fusion.15), channel_id=1, source_target_pairs={{0,1},{1,0},{2,3},{3,2},{4,5},{5,4},{6,7},{7,6},{8,9},{9,8},{10,11... | collective-permute-start | bytes 1769480 | tf_op jit(solution)/shard_map/ppermute | solution.py:32
  155.8 25.8 %collective-permute-start.27 = (bf16[1,384,1024]{2,1,0:T(8,128)(2,1)}, bf16[1,384,1024]{2,1,0:T(8,128)(2,1)S(1)}, u32[]{:S(2)}, u32[]{:S(2)}) collective-permute-start(bf16[1,384,1024]{2,1,0:T(8,128)(2,1)} %add_convert_fusion.2), channel_id=1, source_target_pairs={{0,8},{4,12},{8,0},{12,4},{1,9},{5,13},{9,1},{13,5},{2,10},{6,14},... | collective-permute-start | bytes 2359304 | tf_op jit(solution)/shard_map/ppermute | solution.py:32
  170.7 25.6 %collective-permute-start.40 = (bf16[2,2,48,768]{3,2,1,0:T(8,128)(2,1)}, bf16[2,2,48,768]{3,2,1,0:T(8,128)(2,1)}, u32[]{:S(2)}, u32[]{:S(2)}) collective-permute-start(bf16[2,2,48,768]{3,2,1,0:T(8,128)(2,1)} %broadcast_select_fusion.25), channel_id=1, source_target_pairs={{0,2},{1,3},{2,0},{3,1},{4,6},{5,7},{6,4},{7,5},{8,10},{9,11},{10,... | collective-permute-start | bytes 884744 | tf_op jit(solution)/shard_map/ppermute | solution.py:32
  188.5 14.7 %collective-permute-start.26 = (bf16[384,256]{1,0:T(8,128)(2,1)S(1)}, bf16[384,256]{1,0:T(8,128)(2,1)S(1)}, u32[]{:S(2)}, u32[]{:S(2)}) collective-permute-start(bf16[384,256]{1,0:T(8,128)(2,1)S(1)} %get-tuple-element.156), channel_id=1, source_target_pairs={{0,1},{1,0},{2,3},{3,2},{4,5},{5,4},{6,7},{7,6},{8,9},{9,8},{10,11... | collective-permute-start | bytes 589832 | tf_op jit(solution)/shard_map/ppermute | solution.py:32
  189.4 15.2 %collective-permute-start.25 = (bf16[384,256]{1,0:T(8,128)(2,1)S(1)}, bf16[384,256]{1,0:T(8,128)(2,1)S(1)}, u32[]{:S(2)}, u32[]{:S(2)}) collective-permute-start(bf16[384,256]{1,0:T(8,128)(2,1)S(1)} %get-tuple-element.157), channel_id=1, source_target_pairs={{0,2},{1,3},{2,0},{3,1},{4,6},{5,7},{6,4},{7,5},{8,10},{9,11},{10,... | collective-permute-start | bytes 589832 | tf_op jit(solution)/shard_map/ppermute | solution.py:32
  191.8 24.4 %collective-permute-start.24 = (bf16[384,256]{1,0:T(8,128)(2,1)S(1)}, bf16[384,256]{1,0:T(8,128)(2,1)S(1)}, u32[]{:S(2)}, u32[]{:S(2)}) collective-permute-start(bf16[384,256]{1,0:T(8,128)(2,1)S(1)} %get-tuple-element.158), channel_id=1, source_target_pairs={{0,3},{1,2},{2,1},{3,0},{4,7},{5,6},{6,5},{7,4},{8,11},{9,10},{10,... | collective-permute-start | bytes 589832 | tf_op jit(solution)/shard_map/ppermute | solution.py:32
  191.8 28.0 %collective-permute-start.30 = (bf16[384,256]{1,0:T(8,128)(2,1)}, bf16[384,256]{1,0:T(8,128)(2,1)S(1)}, u32[]{:S(2)}, u32[]{:S(2)}) collective-permute-start(bf16[384,256]{1,0:T(8,128)(2,1)} %get-tuple-element.153), channel_id=1, source_target_pairs={{0,1},{1,0},{2,3},{3,2},{4,5},{5,4},{6,7},{7,6},{8,9},{9,8},{10,11... | collective-permute-start | bytes 589832 | tf_op jit(solution)/shard_map/ppermute | solution.py:32
  201.5 22.0 %collective-permute-start.28 = (bf16[384,256]{1,0:T(8,128)(2,1)S(1)}, bf16[384,256]{1,0:T(8,128)(2,1)S(1)}, u32[]{:S(2)}, u32[]{:S(2)}) collective-permute-start(bf16[384,256]{1,0:T(8,128)(2,1)S(1)} %copy-done.56), channel_id=1, source_target_pairs={{0,3},{1,2},{2,1},{3,0},{4,7},{5,6},{6,5},{7,4},{8,11},{9,10},{10,... | collective-permute-start | bytes 589832 | tf_op jit(solution)/shard_map/ppermute | solution.py:32
  203.2 27.8 %collective-permute-start.29 = (bf16[384,256]{1,0:T(8,128)(2,1)S(1)}, bf16[384,256]{1,0:T(8,128)(2,1)S(1)}, u32[]{:S(2)}, u32[]{:S(2)}) collective-permute-start(bf16[384,256]{1,0:T(8,128)(2,1)S(1)} %copy-done.55), channel_id=1, source_target_pairs={{0,2},{1,3},{2,0},{3,1},{4,6},{5,7},{6,4},{7,5},{8,10},{9,11},{10,... | collective-permute-start | bytes 589832 | tf_op jit(solution)/shard_map/ppermute | solution.py:32
  204.6 34.7 %collective-permute-start.31 = (bf16[4,96,768]{2,1,0:T(8,128)(2,1)}, bf16[4,96,768]{2,1,0:T(8,128)(2,1)}, u32[]{:S(2)}, u32[]{:S(2)}) collective-permute-start(bf16[4,96,768]{2,1,0:T(8,128)(2,1)} %broadcast_select_fusion.20), channel_id=1, source_target_pairs={{0,4},{4,0},{8,12},{12,8},{1,5},{5,1},{9,13},{13,9},{2,6},{6,2},{1... | collective-permute-start | bytes 1769480 | tf_op jit(solution)/shard_map/ppermute | solution.py:32
  216.2 28.3 %collective-permute-start.42 = (bf16[4,48,768]{2,1,0:T(8,128)(2,1)}, bf16[4,48,768]{2,1,0:T(8,128)(2,1)}, u32[]{:S(2)}, u32[]{:S(2)}) collective-permute-start(bf16[4,48,768]{2,1,0:T(8,128)(2,1)} %pad_maximum_fusion.30), channel_id=1, source_target_pairs={{0,2},{1,3},{2,0},{3,1},{4,6},{5,7},{6,4},{7,5},{8,10},{9,11},{10,... | collective-permute-start | bytes 884744 | tf_op jit(solution)/shard_map/ppermute | solution.py:32
  246.3 14.6 %collective-permute-start.43 = (bf16[4,96,768]{2,1,0:T(8,128)(2,1)}, bf16[4,96,768]{2,1,0:T(8,128)(2,1)S(1)}, u32[]{:S(2)}, u32[]{:S(2)}) collective-permute-start(bf16[4,96,768]{2,1,0:T(8,128)(2,1)} %pad_maximum_fusion.21), channel_id=1, source_target_pairs={{0,1},{1,0},{2,3},{3,2},{4,5},{5,4},{6,7},{7,6},{8,9},{9,8},{10,11... | collective-permute-start | bytes 1769480 | tf_op jit(solution)/shard_map/ppermute | solution.py:32
  257.5 14.4 %collective-permute-start.35 = (bf16[6,48,384]{2,1,0:T(8,128)(2,1)S(1)}, bf16[6,48,384]{2,1,0:T(8,128)(2,1)S(1)}, u32[]{:S(2)}, u32[]{:S(2)}) collective-permute-start(bf16[6,48,384]{2,1,0:T(8,128)(2,1)S(1)} %add_convert_fusion.9), channel_id=1, source_target_pairs={{0,2},{1,3},{2,0},{3,1},{4,6},{5,7},{6,4},{7,5},{8,10},{9,11},{10,... | collective-permute-start | bytes 663560 | tf_op jit(solution)/shard_map/ppermute | solution.py:32
  260.7 17.4 %collective-permute-start.34 = (bf16[6,48,384]{2,1,0:T(8,128)(2,1)S(1)}, bf16[6,48,384]{2,1,0:T(8,128)(2,1)S(1)}, u32[]{:S(2)}, u32[]{:S(2)}) collective-permute-start(bf16[6,48,384]{2,1,0:T(8,128)(2,1)S(1)} %add_convert_fusion.9), channel_id=1, source_target_pairs={{0,3},{1,2},{2,1},{3,0},{4,7},{5,6},{6,5},{7,4},{8,11},{9,10},{10,... | collective-permute-start | bytes 663560 | tf_op jit(solution)/shard_map/ppermute | solution.py:32
  261.2 23.2 %collective-permute-start.44 = (bf16[4,192,768]{2,1,0:T(8,128)(2,1)S(1)}, bf16[4,192,768]{2,1,0:T(8,128)(2,1)S(1)}, u32[]{:S(2)}, u32[]{:S(2)}) collective-permute-start(bf16[4,192,768]{2,1,0:T(8,128)(2,1)S(1)} %pad_maximum_fusion.11), channel_id=1, source_target_pairs={{0,8},{4,12},{8,0},{12,4},{1,9},{5,13},{9,1},{13,5},{2,10},{6,14},... | collective-permute-start | bytes 3538952 | tf_op jit(solution)/shard_map/ppermute | solution.py:32
  278.5 21.1 %collective-permute-start.37 = (bf16[17,48,384]{2,1,0:T(8,128)(2,1)S(1)}, bf16[17,48,384]{2,1,0:T(8,128)(2,1)S(1)}, u32[]{:S(2)}, u32[]{:S(2)}) collective-permute-start(bf16[17,48,384]{2,1,0:T(8,128)(2,1)S(1)} %get-tuple-element.103), channel_id=1, source_target_pairs={{0,8},{4,12},{8,0},{12,4},{1,9},{5,13},{9,1},{13,5},{2,10},{6,14},... | collective-permute-start | bytes 1880072 | tf_op jit(solution)/shard_map/ppermute | solution.py:32
  286.5 29.0 %collective-permute-start.45 = (bf16[4,384,768]{2,1,0:T(8,128)(2,1)}, bf16[4,384,768]{2,1,0:T(8,128)(2,1)}, u32[]{:S(2)}, u32[]{:S(2)}) collective-permute-start(bf16[4,384,768]{2,1,0:T(8,128)(2,1)} %pad_maximum_fusion.4.mine), channel_id=1, source_target_pairs={{0,4},{4,0},{8,12},{12,8},{1,5},{5,1},{9,13},{13,9},{2,6},{6,2},{1... | collective-permute-start | bytes 7077896 | tf_op jit(solution)/shard_map/ppermute | solution.py:32
  (91 other events, 693.0 us)

commit v4 on v3

--- a/solution.py
+++ b/solution.py
@@ -383,8 +383,11 @@
     kept = jnp.where(side == 0, sums[0, 0], sums[0, 1])
     sums = jnp.concatenate([in_order(side, kept[None], got[None]), sums[1]], 0)
     sums = share_half(sums, "ulysses", 2, 1)
-    sums = share_half(sums, "ulysses", 1, 1)
-    sums = share_half(sums, "blk", 2, 1)
+    return share_half(sums, "ulysses", 1, 1)
+
+
+def spread_pair(sums, *earlier):
+    sums = after(share_half(sums, "blk", 2, 1), *earlier)
     return place_mlp(bit_of("blk", 1), sums, swap(sums, "blk", 1))
 
 
@@ -582,7 +585,8 @@
         w_up, w_out = half_up[:, :-width], half_up[:, -width:]
         x_mlp = jnp.concatenate([tokens, x_e[0]])
         e_mlp = jnp.concatenate([cotangent, x_e[1]])
-        b_up, w_down, mlp, finish = up_bias, down_weight, mlp_pair, finish_pair
+        b_up, w_down = up_bias, down_weight
+        mlp, finish, spread = mlp_pair, finish_pair, spread_pair
     else:
         x_all, part_qkv = around(x_ranks), x_ranks
         w_qkv, w_up, w_out, w_down = (
@@ -590,7 +594,8 @@
             for w in (qkv_weight, up_weight, out_weight, down_weight)
         )
         b_up = gather_small(up_bias).reshape(-1)
-        x_mlp, e_mlp, mlp, finish = tokens, cotangent, mlp_gathered, lambda v, _: v
+        x_mlp, e_mlp = tokens, cotangent
+        mlp, finish, spread = mlp_gathered, lambda v, _: v, lambda v, *_: v
     small = jnp.concatenate([ln1_gain, ln1_bias, ln2_gain, ln2_bias, out_bias, down_bias, qkv_bias])
     small = gather_small(after(small, part_qkv))
     part = width // shards
@@ -628,18 +633,20 @@
     mixed, d_q, kept, sent = attend(ranks, queries, d_heads, kv_all)
 
     sent, e_around, terms, mlp_out, d_norm_two = after((sent, e_around, terms, mlp_out, d_norm_two))
+    d_q = rotate(d_q, cosine, -sine).astype(bf16).reshape(cols, rows)
+    mixed = mixed.reshape(cols, rows)
+    back_q = to_tokens(jnp.concatenate([d_q, mixed]))
     got = swap(sent, "blk", 1)
     step, kept = 1, [[kept[i], got[i]] for i in range(kept.shape[0])]
     while len(kept) > 1:
         step *= 2
         sent = sum(v.astype(f32) for v in stacked_terms(kept[1::2])).astype(bf16)
+        if step == 2:
+            terms = finish(terms, sent)
+        sent, back_q = after((sent, back_q))
         got = swap(sent, "blk", step)
         kept = [kept[2 * i] + [got[i]] for i in range(got.shape[0])]
-    g_up, g_down = finish(terms, sent)
     total = sum(v.astype(f32) for v in kept[0])
-    d_q = rotate(d_q, cosine, -sine).astype(bf16).reshape(cols, rows)
-    mixed = mixed.reshape(cols, rows)
-    back_q = to_tokens(after(jnp.concatenate([d_q, mixed]), sent))
     e_all = jnp.concatenate(e_around, 0)
     g_out = jnp.dot(mixed, e_all, preferred_element_type=f32).astype(bf16)
     d_k = rotate(total[:cols].reshape(heads, HEAD, rows), cosine, -sine).reshape(cols, rows)
@@ -650,6 +657,7 @@
     back_kv = to_tokens(d_kv)
     grads = jnp.concatenate([g_qkv.reshape(3, cols, width), g_out[None]])
     grads = add_blks(grads)
+    back_kv = after(back_kv, grads)
     back_q, back_kv = by_device(back_q, group), by_device(back_kv, group)
     d_mine = jnp.concatenate(
         [v[:cols] for v in back_q] + [v[:cols] for v in back_kv] + [v[cols:] for v in back_kv], 0
@@ -671,6 +679,7 @@
     input_grad = (e_float + d_x_one + d_x_two).astype(bf16)
 
     g_qkv, g_out, summed = attention_grads(grads, jnp.concatenate(vectors), output)
+    g_up, g_down = spread(terms, output, input_grad)
     results, start = [], 0
     for vector in vectors:
         mine = vector.shape[0] // shards

time: 327 us -> 321 us (0.982)
  the two profiles are of different devices: /device:TPU:9 before, /device:TPU:0 now
where the time goes in v4:
time: 321 us; the launch traced here: 316 us
  waiting for transfers between devices  102 us (32%)
  starting transfers between devices  65.4 us (20%)
  other arithmetic  50 us (16%)
  Pallas kernels  49.8 us (16%)
  local copies, waits for them, and re-layouts  24.4 us (8%)
  matrix products  22.2 us (7%)
    ppermute x46, waiting for transfers between devices, swap(): return lax.ppermute(values, axis, [(i, i ^ bits) for i in range(count)])  102 us
    ppermute x46, starting transfers between devices, swap(): return lax.ppermute(values, axis, [(i, i ^ bits) for i in range(count)])  65.4 us
    pallas_call x1, Pallas kernels, attend(): pl.pallas_call(attend_kernel, grid_spec=pltpu.PrefetchScalarGridSpec(num_...  37 us
    unnamed x177, local copies, waits for them, and re-layouts  15.3 us
    dot_general x1, matrix products, mlp_pair(): jnp.dot(normed, up, preferred_element_type=f32) + up_bias.astype(f32)  8.12 us
    select_n x10, other arithmetic, in_order(): jnp.where(bit == 0, mine, other)  7.94 us
    concatenate x8, other arithmetic, in_order(): jnp.concatenate([jnp.where(bit == 0, mine, other), jnp.where(bit == 0, ot...  7.4 us
    pallas_call x1, Pallas kernels, place_mlp(): pl.pallas_call(place_mlp_kernel, grid_spec=pltpu.PrefetchScalarGridSpec(n...  6.44 us
  transfers between devices with their start and end apart: 46, of which 18 were waited for; matrix products, arithmetic and copies ran while one was open for 26% of the time, Pallas kernels for 14%

profile of v4, /device:TPU:0, one launch (start us, length us, event | category | flops | bytes accessed | tf_op | source)
XLA Modules:
  0.0 315.8 jit_solution(14368103492312800587)
XLA Ops:
  2.6 3.1 collective-permute-start.4
  5.7 2.6 collective-permute-start.5
  11.9 3.2 %broadcast_select_fusion.10 = (bf16[384,1536]{1,0:T(8,128)(2,1)}, bf16[384,1536]{1,0:T(8,128)(2,1)}) fusion(pred[]{:T(512)S(6)} %eq.45, bf16[384,3072]{1,0:T(8,128)(2,1)} %param.27, pred[]{:T(512)S(6)} %eq.48), kind=kLoop, calls=%fused_computation.100 | loop fusion | flops 1179648 | bytes 4718594 | tf_op jit(solution)/shard_map/jit(_where)/select_n | solution.py:344
  18.8 3.0 collective-permute-done
  27.1 7.6 %collective-permute-done.10 = bf16[96,2304]{1,0:T(8,128)(2,1)} collective-permute-done((bf16[96,2304]{1,0:T(8,128)(2,1)}, bf16[96,2304]{1,0:T(8,128)(2,1)}, u32[]{:S(2)}, u32[]{:S(2)}) %collective-permute-start.10) | collective-permute-done | bytes 442400 | tf_op jit(solution)/shard_map/ppermute | solution.py:32
  38.0 7.0 %collective-permute-done.11 = bf16[96,2304]{1,0:T(8,128)(2,1)} collective-permute-done((bf16[96,2304]{1,0:T(8,128)(2,1)}, bf16[96,2304]{1,0:T(8,128)(2,1)}, u32[]{:S(2)}, u32[]{:S(2)}) %collective-permute-start.11) | collective-permute-done | bytes 442400 | tf_op jit(solution)/shard_map/ppermute | solution.py:32
  45.0 2.5 broadcast_select_fusion.22
  50.1 2.9 collective-permute-done.16
  59.1 3.5 %prepare.1 = (bf16[1024,768]{1,0:T(8,128)(2,1)S(1)}, bf16[192,1024]{1,0:T(8,128)(2,1)S(1)}, bf16[400,1024]{1,0:T(8,128)(2,1)S(1)}, f32[8,1024]{1,0:T(8,128)S(1)}, f32[8,1024]{1,0:T(8,128)S(1)}) custom-call(f32[8,1]{1,0:T(8,128)S(1)} %copy-done.6, f32[1,768]{1,0:T(1,128)S(1)} %bitcast.77, f32[1,768]{1,0:T(1,128)S(1)} %bitcast.78, ...), custom_call_target="tpu_custom_call" | custom-call | flops 905969664 | bytes 6291456 | tf_op jit(solution)/shard_map/prepare/pallas_call | solution.py:301
  69.3 3.5 %collective-permute-start.14 = (bf16[192,256]{1,0:T(8,128)(2,1)S(1)}, bf16[192,256]{1,0:T(8,128)(2,1)S(1)}, u32[]{:S(2)}, u32[]{:S(2)}) collective-permute-start(bf16[192,256]{1,0:T(8,128)(2,1)S(1)} %get-tuple-element.191), channel_id=1, source_target_pairs={{0,2},{1,3},{2,0},{3,1},{4,6},{5,7},{6,4},{7,5},{8,10},{9,11},{10,... | collective-permute-start | bytes 294920 | tf_op jit(solution)/shard_map/ppermute | solution.py:32
  73.2 8.1 %multiply_convert_fusion = (bf16[512,1536]{1,0:T(8,128)(2,1)S(1)}, f32[512,1536]{1,0:T(8,128)S(1)}, f32[512,1536]{1,0:T(8,128)S(1)}) fusion(f32[1536]{0:T(1024)S(1)} %convert_element_type.285, bf16[768,1536]{1,0:T(8,128)(2,1)S(1)} %pad_maximum_fusion.3, bf16[512,768]{1,0:T(8,128)(2,1)S(1)} %pad_maximum_fusion.16, f32[768]{0:T(1024)S(1)} %reshape.234, ...), kind=kOutput, calls=%fused_computation.18 | convolution fusion | flops 1262223360 | bytes 11026432 | tf_op jit(solution)/shard_map/dot_general | solution.py:352
  81.3 2.2 convert_reduce_fusion
  96.0 3.8 %collective-permute-start.19 = (bf16[256,768]{1,0:T(8,128)(2,1)S(1)}, bf16[256,768]{1,0:T(8,128)(2,1)}, u32[]{:S(2)}, u32[]{:S(2)}) collective-permute-start(bf16[256,768]{1,0:T(8,128)(2,1)S(1)} %copy-done.21), channel_id=1, source_target_pairs={{0,2},{1,3},{2,0},{3,1},{4,6},{5,7},{6,4},{7,5},{8,10},{9,11},{10,... | collective-permute-start | bytes 1179656 | tf_op jit(solution)/shard_map/ppermute | solution.py:32
  101.7 37.0 %attend.1 = (bf16[3,64,1024]{2,1,0:T(8,128)(2,1)}, f32[3,64,1024]{2,1,0:T(8,128)}, bf16[2,384,1024]{2,1,0:T(8,128)(2,1)}, bf16[2,384,1024]{2,1,0:T(8,128)(2,1)}) custom-call(s32[32]{0:T(128)} %maximum_convert_fusion.5.rank, bf16[3,64,1024]{2,1,0:T(8,128)(2,1)} %bitcast.79, bf16[3,64,1024]{2,1,0:T(8,128)(2,1)} %bitcast.95, bf16[400,1024]{1,0:T(8,128)(2,1)} %copy-done.4, ...), custom_call_target="tpu_custom_call" | custom-call | flops 38654705664 | bytes 12582912 | tf_op jit(solution)/shard_map/attend/pallas_call | solution.py:224
  140.1 2.2 slice_add_fusion
  150.3 3.5 %collective-permute-start.25 = (bf16[384,256]{1,0:T(8,128)(2,1)S(1)}, bf16[384,256]{1,0:T(8,128)(2,1)S(1)}, u32[]{:S(2)}, u32[]{:S(2)}) collective-permute-start(bf16[384,256]{1,0:T(8,128)(2,1)S(1)} %get-tuple-element.177), channel_id=1, source_target_pairs={{0,2},{1,3},{2,0},{3,1},{4,6},{5,7},{6,4},{7,5},{8,10},{9,11},{10,... | collective-permute-start | bytes 589832 | tf_op jit(solution)/shard_map/ppermute | solution.py:32
  157.9 3.3 %collective-permute-done.24 = bf16[384,256]{1,0:T(8,128)(2,1)S(1)} collective-permute-done((bf16[384,256]{1,0:T(8,128)(2,1)S(1)}, bf16[384,256]{1,0:T(8,128)(2,1)S(1)}, u32[]{:S(2)}, u32[]{:S(2)}) %collective-permute-start.24) | collective-permute-done | bytes 196640 | tf_op jit(solution)/shard_map/ppermute | solution.py:32
  161.2 6.9 %collective-permute-done.25 = bf16[384,256]{1,0:T(8,128)(2,1)S(1)} collective-permute-done((bf16[384,256]{1,0:T(8,128)(2,1)S(1)}, bf16[384,256]{1,0:T(8,128)(2,1)S(1)}, u32[]{:S(2)}, u32[]{:S(2)}) %collective-permute-start.25) | collective-permute-done | bytes 196640 | tf_op jit(solution)/shard_map/ppermute | solution.py:32
  168.1 5.3 %collective-permute-start.27 = (bf16[1,384,1024]{2,1,0:T(8,128)(2,1)S(1)}, bf16[1,384,1024]{2,1,0:T(8,128)(2,1)S(1)}, u32[]{:S(2)}, u32[]{:S(2)}) collective-permute-start(bf16[1,384,1024]{2,1,0:T(8,128)(2,1)S(1)} %add_convert_fusion.2), channel_id=1, source_target_pairs={{0,8},{4,12},{8,0},{12,4},{1,9},{5,13},{9,1},{13,5},{2,10},{6,14},... | collective-permute-start | bytes 2359304 | tf_op jit(solution)/shard_map/ppermute | solution.py:32
  178.9 4.8 %collective-permute-start.40 = (bf16[2,2,48,768]{3,2,1,0:T(8,128)(2,1)}, bf16[2,2,48,768]{3,2,1,0:T(8,128)(2,1)}, u32[]{:S(2)}, u32[]{:S(2)}) collective-permute-start(bf16[2,2,48,768]{3,2,1,0:T(8,128)(2,1)} %broadcast_select_fusion.25), channel_id=1, source_target_pairs={{0,2},{1,3},{2,0},{3,1},{4,6},{5,7},{6,4},{7,5},{8,10},{9,11},{10,... | collective-permute-start | bytes 884744 | tf_op jit(solution)/shard_map/ppermute | solution.py:32
  183.7 6.5 %collective-permute-done.27 = bf16[1,384,1024]{2,1,0:T(8,128)(2,1)S(1)} collective-permute-done((bf16[1,384,1024]{2,1,0:T(8,128)(2,1)S(1)}, bf16[1,384,1024]{2,1,0:T(8,128)(2,1)S(1)}, u32[]{:S(2)}, u32[]{:S(2)}) %collective-permute-start.27) | collective-permute-done | bytes 786464 | tf_op jit(solution)/shard_map/ppermute | solution.py:32
  196.3 4.8 %collective-permute-start.28 = (bf16[384,256]{1,0:T(8,128)(2,1)}, bf16[384,256]{1,0:T(8,128)(2,1)}, u32[]{:S(2)}, u32[]{:S(2)}) collective-permute-start(bf16[384,256]{1,0:T(8,128)(2,1)} %get-tuple-element.168), channel_id=1, source_target_pairs={{0,1},{1,0},{2,3},{3,2},{4,5},{5,4},{6,7},{7,6},{8,9},{9,8},{10,11... | collective-permute-start | bytes 589832 | tf_op jit(solution)/shard_map/ppermute | solution.py:32
  207.1 2.6 collective-permute-done.41
  215.0 19.6 %collective-permute-done.42 = bf16[4,48,768]{2,1,0:T(8,128)(2,1)S(1)} collective-permute-done((bf16[4,48,768]{2,1,0:T(8,128)(2,1)S(1)}, bf16[4,48,768]{2,1,0:T(8,128)(2,1)S(1)}, u32[]{:S(2)}, u32[]{:S(2)}) %collective-permute-start.42) | collective-permute-done | bytes 294944 | tf_op jit(solution)/shard_map/ppermute | solution.py:32
  244.8 5.0 %collective-permute-done.33 = bf16[6,48,384]{2,1,0:T(8,128)(2,1)S(1)} collective-permute-done((bf16[6,48,384]{2,1,0:T(8,128)(2,1)S(1)}, bf16[6,48,384]{2,1,0:T(8,128)(2,1)S(1)}, u32[]{:S(2)}, u32[]{:S(2)}) %collective-permute-start.33) | collective-permute-done | bytes 221216 | tf_op jit(solution)/shard_map/ppermute | solution.py:32
  249.9 2.5 collective-permute-start.34
  257.7 2.5 collective-permute-done.34
  260.2 10.8 %collective-permute-done.35 = bf16[6,48,384]{2,1,0:T(8,128)(2,1)S(1)} collective-permute-done((bf16[6,48,384]{2,1,0:T(8,128)(2,1)S(1)}, bf16[6,48,384]{2,1,0:T(8,128)(2,1)S(1)}, u32[]{:S(2)}, u32[]{:S(2)}) %collective-permute-start.35) | collective-permute-done | bytes 221216 | tf_op jit(solution)/shard_map/ppermute | solution.py:32
  274.5 10.4 %collective-permute-done.44 = bf16[4,192,768]{2,1,0:T(8,128)(2,1)S(1)} collective-permute-done((bf16[4,192,768]{2,1,0:T(8,128)(2,1)S(1)}, bf16[4,192,768]{2,1,0:T(8,128)(2,1)S(1)}, u32[]{:S(2)}, u32[]{:S(2)}) %collective-permute-start.44) | collective-permute-done | bytes 1179680 | tf_op jit(solution)/shard_map/ppermute | solution.py:32
  286.9 8.2 %collective-permute-done.37 = bf16[17,48,384]{2,1,0:T(8,128)(2,1)S(1)} collective-permute-done((bf16[17,48,384]{2,1,0:T(8,128)(2,1)S(1)}, bf16[17,48,384]{2,1,0:T(8,128)(2,1)S(1)}, u32[]{:S(2)}, u32[]{:S(2)}) %collective-permute-start.37) | collective-permute-done | bytes 626720 | tf_op jit(solution)/shard_map/ppermute | solution.py:32
  305.8 2.8 place_qkv.1
  308.6 6.4 %place_mlp.1 = (f32[384,3072]{1,0:T(8,128)}, f32[2,2,384,768]{3,2,1,0:T(8,128)}) custom-call(s32[1]{0:T(128)} %bitcast.24.which, bf16[4,384,768]{2,1,0:T(8,128)(2,1)} %pad_maximum_fusion.4.mine, bf16[4,384,768]{2,1,0:T(8,128)(2,1)} %collective-permute-done.45.other), custom_call_target="tpu_custom_call" | custom-call | bytes 14155776 | tf_op jit(solution)/shard_map/place_mlp/pallas_call | solution.py:407
  (379 shorter events, 115.1 us)
Async XLA Ops:
  2.6 56.2 %collective-permute-start.4 = (bf16[272,768]{1,0:T(8,128)(2,1)S(1)}, bf16[272,768]{1,0:T(8,128)(2,1)S(1)}, u32[]{:S(2)}, u32[]{:S(2)}) collective-permute-start(bf16[272,768]{1,0:T(8,128)(2,1)S(1)} %fusion.52.refs_0_), channel_id=1, source_target_pairs={{0,1},{1,0},{2,3},{3,2},{4,5},{5,4},{6,7},{7,6},{8,9},{9,8},{10,11... | collective-permute-start | bytes 1253384 | tf_op jit(solution)/shard_map/ppermute | solution.py:32
  5.7 53.1 %collective-permute-start.5 = (bf16[272,768]{1,0:T(8,128)(2,1)S(1)}, bf16[272,768]{1,0:T(8,128)(2,1)}, u32[]{:S(2)}, u32[]{:S(2)}) collective-permute-start(bf16[272,768]{1,0:T(8,128)(2,1)S(1)} %fusion.52.refs_0_), channel_id=1, source_target_pairs={{0,2},{1,3},{2,0},{3,1},{4,6},{5,7},{6,4},{7,5},{8,10},{9,11},{10,... | collective-permute-start | bytes 1253384 | tf_op jit(solution)/shard_map/ppermute | solution.py:32
  8.3 50.5 %collective-permute-start.6 = (bf16[272,768]{1,0:T(8,128)(2,1)S(1)}, bf16[272,768]{1,0:T(8,128)(2,1)}, u32[]{:S(2)}, u32[]{:S(2)}) collective-permute-start(bf16[272,768]{1,0:T(8,128)(2,1)S(1)} %fusion.52.refs_0_), channel_id=1, source_target_pairs={{0,3},{1,2},{2,1},{3,0},{4,7},{5,6},{6,5},{7,4},{8,11},{9,10},{10,... | collective-permute-start | bytes 1253384 | tf_op jit(solution)/shard_map/ppermute | solution.py:32
  10.1 11.7 %collective-permute-start = (bf16[96,2304]{1,0:T(8,128)(2,1)}, bf16[96,2304]{1,0:T(8,128)(2,1)}, u32[]{:S(2)}, u32[]{:S(2)}) collective-permute-start(bf16[96,2304]{1,0:T(8,128)(2,1)} %constant_dynamic-slice_fusion.4), channel_id=1, source_target_pairs={{0,16},{16,0},{1,17},{17,1},{2,18},{18,2},{3,19},{19,3},{4,20},{20... | collective-permute-start | bytes 1327112 | tf_op jit(solution)/shard_map/ppermute | solution.py:32
  36.4 16.6 %collective-permute-start.16 = (bf16[2,256,768]{2,1,0:T(8,128)(2,1)}, bf16[2,256,768]{2,1,0:T(8,128)(2,1)}, u32[]{:S(2)}, u32[]{:S(2)}) collective-permute-start(bf16[2,256,768]{2,1,0:T(8,128)(2,1)} %pad_maximum_fusion.15), channel_id=1, source_target_pairs={{0,16},{16,0},{1,17},{17,1},{2,18},{18,2},{3,19},{19,3},{4,20},{20... | collective-permute-start | bytes 2359304 | tf_op jit(solution)/shard_map/ppermute | solution.py:32
  62.7 21.6 %collective-permute-start.7 = (bf16[400,1024]{1,0:T(8,128)(2,1)S(1)}, bf16[400,1024]{1,0:T(8,128)(2,1)S(1)}, u32[]{:S(2)}, u32[]{:S(2)}) collective-permute-start(bf16[400,1024]{1,0:T(8,128)(2,1)S(1)} %get-tuple-element.67.refs_0_), channel_id=1, source_target_pairs={{0,4},{4,0},{8,12},{12,8},{1,5},{5,1},{9,13},{13,9},{2,6},{6,2},{1... | collective-permute-start | bytes 2457608 | tf_op jit(solution)/shard_map/ppermute | solution.py:32
  63.3 21.1 %collective-permute-start.8 = (bf16[400,1024]{1,0:T(8,128)(2,1)S(1)}, bf16[400,1024]{1,0:T(8,128)(2,1)S(1)}, u32[]{:S(2)}, u32[]{:S(2)}) collective-permute-start(bf16[400,1024]{1,0:T(8,128)(2,1)S(1)} %get-tuple-element.67.refs_0_), channel_id=1, source_target_pairs={{0,8},{4,12},{8,0},{12,4},{1,9},{5,13},{9,1},{13,5},{2,10},{6,14},... | collective-permute-start | bytes 2457608 | tf_op jit(solution)/shard_map/ppermute | solution.py:32
  68.7 14.8 %collective-permute-start.13 = (bf16[192,256]{1,0:T(8,128)(2,1)S(1)}, bf16[192,256]{1,0:T(8,128)(2,1)S(1)}, u32[]{:S(2)}, u32[]{:S(2)}) collective-permute-start(bf16[192,256]{1,0:T(8,128)(2,1)S(1)} %get-tuple-element.192), channel_id=1, source_target_pairs={{0,1},{1,0},{2,3},{3,2},{4,5},{5,4},{6,7},{7,6},{8,9},{9,8},{10,11... | collective-permute-start | bytes 294920 | tf_op jit(solution)/shard_map/ppermute | solution.py:32
  69.3 14.3 %collective-permute-start.14 = (bf16[192,256]{1,0:T(8,128)(2,1)S(1)}, bf16[192,256]{1,0:T(8,128)(2,1)S(1)}, u32[]{:S(2)}, u32[]{:S(2)}) collective-permute-start(bf16[192,256]{1,0:T(8,128)(2,1)S(1)} %get-tuple-element.191), channel_id=1, source_target_pairs={{0,2},{1,3},{2,0},{3,1},{4,6},{5,7},{6,4},{7,5},{8,10},{9,11},{10,... | collective-permute-start | bytes 294920 | tf_op jit(solution)/shard_map/ppermute | solution.py:32
  95.7 48.4 %collective-permute-start.18 = (bf16[256,768]{1,0:T(8,128)(2,1)S(1)}, bf16[256,768]{1,0:T(8,128)(2,1)}, u32[]{:S(2)}, u32[]{:S(2)}) collective-permute-start(bf16[256,768]{1,0:T(8,128)(2,1)S(1)} %copy-done.21), channel_id=1, source_target_pairs={{0,1},{1,0},{2,3},{3,2},{4,5},{5,4},{6,7},{7,6},{8,9},{9,8},{10,11... | collective-permute-start | bytes 1179656 | tf_op jit(solution)/shard_map/ppermute | solution.py:32
  96.0 48.2 %collective-permute-start.19 = (bf16[256,768]{1,0:T(8,128)(2,1)S(1)}, bf16[256,768]{1,0:T(8,128)(2,1)}, u32[]{:S(2)}, u32[]{:S(2)}) collective-permute-start(bf16[256,768]{1,0:T(8,128)(2,1)S(1)} %copy-done.21), channel_id=1, source_target_pairs={{0,2},{1,3},{2,0},{3,1},{4,6},{5,7},{6,4},{7,5},{8,10},{9,11},{10,... | collective-permute-start | bytes 1179656 | tf_op jit(solution)/shard_map/ppermute | solution.py:32
  99.8 44.3 %collective-permute-start.20 = (bf16[256,768]{1,0:T(8,128)(2,1)S(1)}, bf16[256,768]{1,0:T(8,128)(2,1)}, u32[]{:S(2)}, u32[]{:S(2)}) collective-permute-start(bf16[256,768]{1,0:T(8,128)(2,1)S(1)} %copy-done.21), channel_id=1, source_target_pairs={{0,3},{1,2},{2,1},{3,0},{4,7},{5,6},{6,5},{7,4},{8,11},{9,10},{10,... | collective-permute-start | bytes 1179656 | tf_op jit(solution)/shard_map/ppermute | solution.py:32
  100.2 38.5 %collective-permute-start.22 = (bf16[512,768]{1,0:T(8,128)(2,1)S(1)}, bf16[512,768]{1,0:T(8,128)(2,1)S(1)}, u32[]{:S(2)}, u32[]{:S(2)}) collective-permute-start(bf16[512,768]{1,0:T(8,128)(2,1)S(1)} %pad_maximum_fusion.18), channel_id=1, source_target_pairs={{0,16},{16,0},{1,17},{17,1},{2,18},{18,2},{3,19},{19,3},{4,20},{20... | collective-permute-start | bytes 2359304 | tf_op jit(solution)/shard_map/ppermute | solution.py:32
  100.7 41.6 %collective-permute-start.21 = (bf16[2,2,192,768]{3,2,1,0:T(8,128)(2,1)S(1)}, bf16[2,2,192,768]{3,2,1,0:T(8,128)(2,1)}, u32[]{:S(2)}, u32[]{:S(2)}) collective-permute-start(bf16[2,2,192,768]{3,2,1,0:T(8,128)(2,1)S(1)} %broadcast_select_fusion.8), channel_id=1, source_target_pairs={{0,8},{4,12},{8,0},{12,4},{1,9},{5,13},{9,1},{13,5},{2,10},{6,14},... | collective-permute-start | bytes 3538952 | tf_op jit(solution)/shard_map/ppermute | solution.py:32
  144.1 12.0 %collective-permute-start.23 = (bf16[2,384,1024]{2,1,0:T(8,128)(2,1)}, bf16[2,384,1024]{2,1,0:T(8,128)(2,1)}, u32[]{:S(2)}, u32[]{:S(2)}) collective-permute-start(bf16[2,384,1024]{2,1,0:T(8,128)(2,1)} %get-tuple-element.81), channel_id=1, source_target_pairs={{0,4},{4,0},{8,12},{12,8},{1,5},{5,1},{9,13},{13,9},{2,6},{6,2},{1... | collective-permute-start | bytes 4718600 | tf_op jit(solution)/shard_map/ppermute | solution.py:32
  150.3 17.8 %collective-permute-start.25 = (bf16[384,256]{1,0:T(8,128)(2,1)S(1)}, bf16[384,256]{1,0:T(8,128)(2,1)S(1)}, u32[]{:S(2)}, u32[]{:S(2)}) collective-permute-start(bf16[384,256]{1,0:T(8,128)(2,1)S(1)} %get-tuple-element.177), channel_id=1, source_target_pairs={{0,2},{1,3},{2,0},{3,1},{4,6},{5,7},{6,4},{7,5},{8,10},{9,11},{10,... | collective-permute-start | bytes 589832 | tf_op jit(solution)/shard_map/ppermute | solution.py:32
  153.9 14.2 %collective-permute-start.26 = (bf16[384,256]{1,0:T(8,128)(2,1)S(1)}, bf16[384,256]{1,0:T(8,128)(2,1)S(1)}, u32[]{:S(2)}, u32[]{:S(2)}) collective-permute-start(bf16[384,256]{1,0:T(8,128)(2,1)S(1)} %get-tuple-element.174), channel_id=1, source_target_pairs={{0,3},{1,2},{2,1},{3,0},{4,7},{5,6},{6,5},{7,4},{8,11},{9,10},{10,... | collective-permute-start | bytes 589832 | tf_op jit(solution)/shard_map/ppermute | solution.py:32
  157.8 20.1 %collective-permute-start.39 = (bf16[2,2,96,768]{3,2,1,0:T(8,128)(2,1)S(1)}, bf16[2,2,96,768]{3,2,1,0:T(8,128)(2,1)S(1)}, u32[]{:S(2)}, u32[]{:S(2)}) collective-permute-start(bf16[2,2,96,768]{3,2,1,0:T(8,128)(2,1)S(1)} %broadcast_select_fusion.15), channel_id=1, source_target_pairs={{0,1},{1,0},{2,3},{3,2},{4,5},{5,4},{6,7},{7,6},{8,9},{9,8},{10,11... | collective-permute-start | bytes 1769480 | tf_op jit(solution)/shard_map/ppermute | solution.py:32
  168.1 22.1 %collective-permute-start.27 = (bf16[1,384,1024]{2,1,0:T(8,128)(2,1)S(1)}, bf16[1,384,1024]{2,1,0:T(8,128)(2,1)S(1)}, u32[]{:S(2)}, u32[]{:S(2)}) collective-permute-start(bf16[1,384,1024]{2,1,0:T(8,128)(2,1)S(1)} %add_convert_fusion.2), channel_id=1, source_target_pairs={{0,8},{4,12},{8,0},{12,4},{1,9},{5,13},{9,1},{13,5},{2,10},{6,14},... | collective-permute-start | bytes 2359304 | tf_op jit(solution)/shard_map/ppermute | solution.py:32
  178.9 25.2 %collective-permute-start.40 = (bf16[2,2,48,768]{3,2,1,0:T(8,128)(2,1)}, bf16[2,2,48,768]{3,2,1,0:T(8,128)(2,1)}, u32[]{:S(2)}, u32[]{:S(2)}) collective-permute-start(bf16[2,2,48,768]{3,2,1,0:T(8,128)(2,1)} %broadcast_select_fusion.25), channel_id=1, source_target_pairs={{0,2},{1,3},{2,0},{3,1},{4,6},{5,7},{6,4},{7,5},{8,10},{9,11},{10,... | collective-permute-start | bytes 884744 | tf_op jit(solution)/shard_map/ppermute | solution.py:32
  195.4 16.5 %collective-permute-start.31 = (bf16[4,96,768]{2,1,0:T(8,128)(2,1)}, bf16[4,96,768]{2,1,0:T(8,128)(2,1)}, u32[]{:S(2)}, u32[]{:S(2)}) collective-permute-start(bf16[4,96,768]{2,1,0:T(8,128)(2,1)} %broadcast_select_fusion.20), channel_id=1, source_target_pairs={{0,4},{4,0},{8,12},{12,8},{1,5},{5,1},{9,13},{13,9},{2,6},{6,2},{1... | collective-permute-start | bytes 1769480 | tf_op jit(solution)/shard_map/ppermute | solution.py:32
  196.3 40.8 %collective-permute-start.28 = (bf16[384,256]{1,0:T(8,128)(2,1)}, bf16[384,256]{1,0:T(8,128)(2,1)}, u32[]{:S(2)}, u32[]{:S(2)}) collective-permute-start(bf16[384,256]{1,0:T(8,128)(2,1)} %get-tuple-element.168), channel_id=1, source_target_pairs={{0,1},{1,0},{2,3},{3,2},{4,5},{5,4},{6,7},{7,6},{8,9},{9,8},{10,11... | collective-permute-start | bytes 589832 | tf_op jit(solution)/shard_map/ppermute | solution.py:32
  201.2 35.9 %collective-permute-start.29 = (bf16[384,256]{1,0:T(8,128)(2,1)}, bf16[384,256]{1,0:T(8,128)(2,1)}, u32[]{:S(2)}, u32[]{:S(2)}) collective-permute-start(bf16[384,256]{1,0:T(8,128)(2,1)} %get-tuple-element.169), channel_id=1, source_target_pairs={{0,2},{1,3},{2,0},{3,1},{4,6},{5,7},{6,4},{7,5},{8,10},{9,11},{10,... | collective-permute-start | bytes 589832 | tf_op jit(solution)/shard_map/ppermute | solution.py:32
  202.2 35.0 %collective-permute-start.30 = (bf16[384,256]{1,0:T(8,128)(2,1)}, bf16[384,256]{1,0:T(8,128)(2,1)}, u32[]{:S(2)}, u32[]{:S(2)}) collective-permute-start(bf16[384,256]{1,0:T(8,128)(2,1)} %get-tuple-element.166), channel_id=1, source_target_pairs={{0,3},{1,2},{2,1},{3,0},{4,7},{5,6},{6,5},{7,4},{8,11},{9,10},{10,... | collective-permute-start | bytes 589832 | tf_op jit(solution)/shard_map/ppermute | solution.py:32
  209.8 24.9 %collective-permute-start.42 = (bf16[4,48,768]{2,1,0:T(8,128)(2,1)S(1)}, bf16[4,48,768]{2,1,0:T(8,128)(2,1)S(1)}, u32[]{:S(2)}, u32[]{:S(2)}) collective-permute-start(bf16[4,48,768]{2,1,0:T(8,128)(2,1)S(1)} %pad_maximum_fusion.29), channel_id=1, source_target_pairs={{0,2},{1,3},{2,0},{3,1},{4,6},{5,7},{6,4},{7,5},{8,10},{9,11},{10,... | collective-permute-start | bytes 884744 | tf_op jit(solution)/shard_map/ppermute | solution.py:32
  213.2 22.4 %collective-permute-start.32 = (bf16[4,48,768]{2,1,0:T(8,128)(2,1)S(1)}, bf16[4,48,768]{2,1,0:T(8,128)(2,1)S(1)}, u32[]{:S(2)}, u32[]{:S(2)}) collective-permute-start(bf16[4,48,768]{2,1,0:T(8,128)(2,1)S(1)} %broadcast_select_fusion.28), channel_id=1, source_target_pairs={{0,8},{4,12},{8,0},{12,4},{1,9},{5,13},{9,1},{13,5},{2,10},{6,14},... | collective-permute-start | bytes 884744 | tf_op jit(solution)/shard_map/ppermute | solution.py:32
  235.6 18.8 %collective-permute-start.43 = (bf16[4,96,768]{2,1,0:T(8,128)(2,1)}, bf16[4,96,768]{2,1,0:T(8,128)(2,1)}, u32[]{:S(2)}, u32[]{:S(2)}) collective-permute-start(bf16[4,96,768]{2,1,0:T(8,128)(2,1)} %pad_maximum_fusion.20), channel_id=1, source_target_pairs={{0,1},{1,0},{2,3},{3,2},{4,5},{5,4},{6,7},{7,6},{8,9},{9,8},{10,11... | collective-permute-start | bytes 1769480 | tf_op jit(solution)/shard_map/ppermute | solution.py:32
  252.4 18.6 %collective-permute-start.35 = (bf16[6,48,384]{2,1,0:T(8,128)(2,1)S(1)}, bf16[6,48,384]{2,1,0:T(8,128)(2,1)S(1)}, u32[]{:S(2)}, u32[]{:S(2)}) collective-permute-start(bf16[6,48,384]{2,1,0:T(8,128)(2,1)S(1)} %add_convert_fusion.9), channel_id=1, source_target_pairs={{0,2},{1,3},{2,0},{3,1},{4,6},{5,7},{6,4},{7,5},{8,10},{9,11},{10,... | collective-permute-start | bytes 663560 | tf_op jit(solution)/shard_map/ppermute | solution.py:32
  253.2 17.9 %collective-permute-start.36 = (bf16[6,48,384]{2,1,0:T(8,128)(2,1)S(1)}, bf16[6,48,384]{2,1,0:T(8,128)(2,1)S(1)}, u32[]{:S(2)}, u32[]{:S(2)}) collective-permute-start(bf16[6,48,384]{2,1,0:T(8,128)(2,1)S(1)} %add_convert_fusion.9), channel_id=1, source_target_pairs={{0,1},{1,0},{2,3},{3,2},{4,5},{5,4},{6,7},{7,6},{8,9},{9,8},{10,11... | collective-permute-start | bytes 663560 | tf_op jit(solution)/shard_map/ppermute | solution.py:32
  255.9 29.0 %collective-permute-start.44 = (bf16[4,192,768]{2,1,0:T(8,128)(2,1)S(1)}, bf16[4,192,768]{2,1,0:T(8,128)(2,1)S(1)}, u32[]{:S(2)}, u32[]{:S(2)}) collective-permute-start(bf16[4,192,768]{2,1,0:T(8,128)(2,1)S(1)} %pad_maximum_fusion.11), channel_id=1, source_target_pairs={{0,8},{4,12},{8,0},{12,4},{1,9},{5,13},{9,1},{13,5},{2,10},{6,14},... | collective-permute-start | bytes 3538952 | tf_op jit(solution)/shard_map/ppermute | solution.py:32
  271.4 23.7 %collective-permute-start.37 = (bf16[17,48,384]{2,1,0:T(8,128)(2,1)S(1)}, bf16[17,48,384]{2,1,0:T(8,128)(2,1)S(1)}, u32[]{:S(2)}, u32[]{:S(2)}) collective-permute-start(bf16[17,48,384]{2,1,0:T(8,128)(2,1)S(1)} %get-tuple-element.121), channel_id=1, source_target_pairs={{0,8},{4,12},{8,0},{12,4},{1,9},{5,13},{9,1},{13,5},{2,10},{6,14},... | collective-permute-start | bytes 1880072 | tf_op jit(solution)/shard_map/ppermute | solution.py:32
  286.9 21.7 %collective-permute-start.45 = (bf16[4,384,768]{2,1,0:T(8,128)(2,1)}, bf16[4,384,768]{2,1,0:T(8,128)(2,1)}, u32[]{:S(2)}, u32[]{:S(2)}) collective-permute-start(bf16[4,384,768]{2,1,0:T(8,128)(2,1)} %pad_maximum_fusion.4.mine), channel_id=1, source_target_pairs={{0,4},{4,0},{8,12},{12,8},{1,5},{5,1},{9,13},{13,9},{2,6},{6,2},{1... | collective-permute-start | bytes 7077896 | tf_op jit(solution)/shard_map/ppermute | solution.py:32
  (87 other events, 616.1 us)

commit v5 on v4

--- a/solution.py
+++ b/solution.py
@@ -383,33 +383,38 @@
     kept = jnp.where(side == 0, sums[0, 0], sums[0, 1])
     sums = jnp.concatenate([in_order(side, kept[None], got[None]), sums[1]], 0)
     sums = share_half(sums, "ulysses", 2, 1)
-    return share_half(sums, "ulysses", 1, 1)
-
-
-def spread_pair(sums, *earlier):
-    sums = after(share_half(sums, "blk", 2, 1), *earlier)
-    return place_mlp(bit_of("blk", 1), sums, swap(sums, "blk", 1))
-
-
-def place_mlp_kernel(which, mine, other, up_ref, down_ref):
-    width = mine.shape[-1]
-    for c, ref in ((which[0], mine), (1 - which[0], other)):
+    return sums
+
+
+def spread_pair(sums, near, *earlier):
+    mine, other = [], []
+    sums = after(sums, near)
+    for part in (sums[:2], sums[2:]):
+        part = share_half(share_half(part, "ulysses", 1, 1), "blk", 2, 1)
+        mine.append(after(part, *earlier))
+        other.append(swap(mine[-1], "blk", 1))
+    return place_mlp(bit_of("blk", 1), mine, other)
+
+
+def place_mlp_kernel(which, mine_up, mine_down, other_up, other_down, up_ref, down_ref):
+    width = mine_up.shape[-1]
+    for c, up, down in ((which[0], mine_up, mine_down), (1 - which[0], other_up, other_down)):
         for f in range(2):
             at = pl.multiple_of((2 * f + c) * width, STRETCH)
-            up_ref[:, pl.ds(at, width)] = ref[f].astype(f32)
-            down_ref[c, f] = ref[2 + f].astype(f32)
+            up_ref[:, pl.ds(at, width)] = up[f].astype(f32)
+            down_ref[c, f] = down[f].astype(f32)
 
 
 def place_mlp(which, mine, other):
-    _, rows, width = mine.shape
+    _, rows, width = mine[0].shape
     step = rows // 4
-    whole = pl.BlockSpec((4, step, width), lambda i, *_: (0, i, 0))
+    whole = pl.BlockSpec((2, step, width), lambda i, *_: (0, i, 0))
     up, down = pl.pallas_call(
         place_mlp_kernel,
         grid_spec=pltpu.PrefetchScalarGridSpec(
             num_scalar_prefetch=1,
             grid=(4,),
-            in_specs=[whole, whole],
+            in_specs=[whole] * 4,
             out_specs=[
                 pl.BlockSpec((step, 4 * width), lambda i, *_: (i, 0)),
                 pl.BlockSpec((2, 2, step, width), lambda i, *_: (0, 0, i, 0)),
@@ -420,9 +425,9 @@
             jax.ShapeDtypeStruct((2, 2, rows, width), f32),
         ],
         compiler_params=pltpu.CompilerParams(vmem_limit_bytes=32 * 2**20),
-        cost_estimate=pl.CostEstimate(flops=0, bytes_accessed=12 * mine.size, transcendentals=0),
+        cost_estimate=pl.CostEstimate(flops=0, bytes_accessed=24 * mine[0].size, transcendentals=0),
         name="place_mlp",
-    )(which[None], mine, other)
+    )(which[None], *mine, *other)
     return up, down.reshape(4 * rows, width)
 
 
@@ -496,7 +501,7 @@
     return add_half(halves_of(add_half(halves_of(grads, 1), "blk", 1), 1), "blk", 2)
 
 
-def attention_grads(grads, vector, output):
+def attention_grads(grads, vector, output, g_up):
     side = lax.axis_index("fsdp")
     group = lax.axis_index("ulysses")
     groups = lax.axis_size("ulysses")
@@ -528,7 +533,7 @@
     kept = in_order(bit_of("blk", 2), kept, got[:units], 1)
     small = (small.astype(f32) + got[units:].astype(f32)).astype(bf16)
     wide = jnp.pad(small, ((0, 0), (0, rows), (0, 0)))
-    got = swap(jnp.concatenate([kept, wide]), "blk", 1)
+    got = after(swap(jnp.concatenate([kept, wide]), "blk", 1), g_up)
     small = small.astype(f32) + got[units:, :rows].astype(f32)
     g_qkv, g_out = place_qkv(bit_of("blk", 1), kept, got)
     return g_qkv, g_out, small.reshape(-1)[:size]
@@ -678,8 +683,9 @@
     output = (x_float + (attn_out + b_out) + (mlp_out + b_down)).astype(bf16)
     input_grad = (e_float + d_x_one + d_x_two).astype(bf16)
 
-    g_qkv, g_out, summed = attention_grads(grads, jnp.concatenate(vectors), output)
-    g_up, g_down = spread(terms, output, input_grad)
+    vector = jnp.concatenate(vectors)
+    g_up, g_down = spread(terms, vector, output, input_grad)
+    g_qkv, g_out, summed = attention_grads(grads, vector, output, g_up)
     results, start = [], 0
     for vector in vectors:
         mine = vector.shape[0] // shards

time: 321 us -> 339 us (1.056)
  the two profiles are of different devices: /device:TPU:0 before, /device:TPU:9 now
where the time goes in v5:
time: 339 us; the launch traced here: 332 us
  waiting for transfers between devices  91.9 us (27%)
  starting transfers between devices  68.9 us (20%)
  Pallas kernels  55.5 us (16%)
  other arithmetic  49.8 us (15%)
  local copies, waits for them, and re-layouts  37.3 us (11%)
  matrix products  26.8 us (8%)
    ppermute x49, waiting for transfers between devices, swap(): return lax.ppermute(values, axis, [(i, i ^ bits) for i in range(count)])  91.9 us
    ppermute x49, starting transfers between devices, swap(): return lax.ppermute(values, axis, [(i, i ^ bits) for i in range(count)])  68.9 us
    pallas_call x1, Pallas kernels, attend(): pl.pallas_call(attend_kernel, grid_spec=pltpu.PrefetchScalarGridSpec(num_...  42.5 us
    unnamed x172, local copies, waits for them, and re-layouts  23.3 us
    dot_general x1, matrix products, mlp_pair(): jnp.dot(normed, up, preferred_element_type=f32) + up_bias.astype(f32)  8.41 us
    concatenate x10, other arithmetic, in_order(): jnp.concatenate([jnp.where(bit == 0, mine, other), jnp.where(bit == 0, ot...  7.22 us
  transfers between devices with their start and end apart: 49, of which 21 were waited for; matrix products, arithmetic and copies ran while one was open for 22% of the time, Pallas kernels for 15%

profile of v5, /device:TPU:9, one launch (start us, length us, event | category | flops | bytes accessed | tf_op | source)
XLA Modules:
  0.0 332.5 jit_solution(16239778939626366671)
XLA Ops:
  9.3 3.2 broadcast_select_fusion.8
  16.2 2.5 collective-permute-done
  23.0 7.8 %collective-permute-done.10 = bf16[96,2304]{1,0:T(8,128)(2,1)} collective-permute-done((bf16[96,2304]{1,0:T(8,128)(2,1)}, bf16[96,2304]{1,0:T(8,128)(2,1)}, u32[]{:S(2)}, u32[]{:S(2)}) %collective-permute-start.10) | collective-permute-done | bytes 442400 | tf_op jit(solution)/shard_map/ppermute | solution.py:32
  32.5 7.9 %collective-permute-done.11 = bf16[96,2304]{1,0:T(8,128)(2,1)} collective-permute-done((bf16[96,2304]{1,0:T(8,128)(2,1)}, bf16[96,2304]{1,0:T(8,128)(2,1)}, u32[]{:S(2)}, u32[]{:S(2)}) %collective-permute-start.11) | collective-permute-done | bytes 442400 | tf_op jit(solution)/shard_map/ppermute | solution.py:32
  40.4 2.5 broadcast_select_fusion.22
  43.9 3.7 %collective-permute-start.3 = (bf16[192,2304]{1,0:T(8,128)(2,1)}, bf16[192,2304]{1,0:T(8,128)(2,1)}, u32[]{:S(2)}, u32[]{:S(2)}) collective-permute-start(bf16[192,2304]{1,0:T(8,128)(2,1)} %pad_maximum_fusion.13), channel_id=1, source_target_pairs={{0,4},{4,0},{8,12},{12,8},{1,5},{5,1},{9,13},{13,9},{2,6},{6,2},{1... | collective-permute-start | bytes 2654216 | tf_op jit(solution)/shard_map/ppermute | solution.py:32
  49.1 3.4 %collective-permute-start.12 = (bf16[192,2304]{1,0:T(8,128)(2,1)S(1)}, bf16[192,2304]{1,0:T(8,128)(2,1)S(1)}, u32[]{:S(2)}, u32[]{:S(2)}) collective-permute-start(bf16[192,2304]{1,0:T(8,128)(2,1)S(1)} %pad_maximum_fusion.14), channel_id=1, source_target_pairs={{0,4},{4,0},{8,12},{12,8},{1,5},{5,1},{9,13},{13,9},{2,6},{6,2},{1... | collective-permute-start | bytes 2654216 | tf_op jit(solution)/shard_map/ppermute | solution.py:32
  58.7 3.5 %prepare.1 = (bf16[1024,768]{1,0:T(8,128)(2,1)S(1)}, bf16[192,1024]{1,0:T(8,128)(2,1)S(1)}, bf16[400,1024]{1,0:T(8,128)(2,1)S(1)}, f32[8,1024]{1,0:T(8,128)S(1)}, f32[8,1024]{1,0:T(8,128)S(1)}) custom-call(f32[8,1]{1,0:T(8,128)S(1)} %copy-done.9, f32[1,768]{1,0:T(1,128)S(1)} %bitcast.78, f32[1,768]{1,0:T(1,128)S(1)} %bitcast.77, ...), custom_call_target="tpu_custom_call" | custom-call | flops 905969664 | bytes 6291456 | tf_op jit(solution)/shard_map/prepare/pallas_call | solution.py:301
  71.3 8.4 %multiply_convert_fusion = (bf16[512,1536]{1,0:T(8,128)(2,1)S(1)}, f32[512,1536]{1,0:T(8,128)S(1)}, f32[512,1536]{1,0:T(8,128)S(1)}) fusion(f32[1536]{0:T(1024)S(1)} %convert_element_type.287, bf16[768,1536]{1,0:T(8,128)(2,1)S(1)} %pad_maximum_fusion.3, bf16[512,768]{1,0:T(8,128)(2,1)S(1)} %pad_maximum_fusion.16, f32[768]{0:T(1024)S(1)} %reshape.233, ...), kind=kOutput, calls=%fused_computation.18 | convolution fusion | flops 1262223360 | bytes 11026432 | tf_op jit(solution)/shard_map/dot_general | solution.py:352
  79.7 2.9 convert_reduce_fusion
  99.5 42.5 %attend.1 = (bf16[3,64,1024]{2,1,0:T(8,128)(2,1)}, f32[3,64,1024]{2,1,0:T(8,128)}, bf16[2,384,1024]{2,1,0:T(8,128)(2,1)}, bf16[2,384,1024]{2,1,0:T(8,128)(2,1)}) custom-call(s32[32]{0:T(128)} %maximum_convert_fusion.5.rank, bf16[3,64,1024]{2,1,0:T(8,128)(2,1)} %bitcast.79, bf16[3,64,1024]{2,1,0:T(8,128)(2,1)} %bitcast.95, bf16[400,1024]{1,0:T(8,128)(2,1)} %copy-done.7, ...), custom_call_target="tpu_custom_call" | custom-call | flops 38654705664 | bytes 12582912 | tf_op jit(solution)/shard_map/attend/pallas_call | solution.py:224
  154.0 2.4 collective-permute-start.24
  156.4 2.7 fusion.37
  160.5 2.6 collective-permute-done.26
  165.4 5.0 %collective-permute-done.25 = bf16[384,256]{1,0:T(8,128)(2,1)S(1)} collective-permute-done((bf16[384,256]{1,0:T(8,128)(2,1)S(1)}, bf16[384,256]{1,0:T(8,128)(2,1)S(1)}, u32[]{:S(2)}, u32[]{:S(2)}) %collective-permute-start.25) | collective-permute-done | bytes 196640 | tf_op jit(solution)/shard_map/ppermute | solution.py:32
  176.5 8.7 %collective-permute-done.39 = bf16[2,2,96,768]{3,2,1,0:T(8,128)(2,1)S(1)} collective-permute-done((bf16[2,2,96,768]{3,2,1,0:T(8,128)(2,1)S(1)}, bf16[2,2,96,768]{3,2,1,0:T(8,128)(2,1)S(1)}, u32[]{:S(2)}, u32[]{:S(2)}) %collective-permute-start.39) | collective-permute-done | bytes 589856 | tf_op jit(solution)/shard_map/ppermute | solution.py:32
  199.4 3.4 %collective-permute-start.31 = (bf16[4,96,768]{2,1,0:T(8,128)(2,1)S(1)}, bf16[4,96,768]{2,1,0:T(8,128)(2,1)S(1)}, u32[]{:S(2)}, u32[]{:S(2)}) collective-permute-start(bf16[4,96,768]{2,1,0:T(8,128)(2,1)S(1)} %broadcast_select_fusion.20), channel_id=1, source_target_pairs={{0,4},{4,0},{8,12},{12,8},{1,5},{5,1},{9,13},{13,9},{2,6},{6,2},{1... | collective-permute-start | bytes 1769480 | tf_op jit(solution)/shard_map/ppermute | solution.py:32
  202.7 5.1 %collective-permute-done.40 = bf16[2,2,48,768]{3,2,1,0:T(8,128)(2,1)} collective-permute-done((bf16[2,2,48,768]{3,2,1,0:T(8,128)(2,1)}, bf16[2,2,48,768]{3,2,1,0:T(8,128)(2,1)}, u32[]{:S(2)}, u32[]{:S(2)}) %collective-permute-start.40) | collective-permute-done | bytes 294944 | tf_op jit(solution)/shard_map/ppermute | solution.py:32
  209.0 3.5 %collective-permute-done.41 = bf16[48,768]{1,0:T(8,128)(2,1)S(1)} collective-permute-done((bf16[48,768]{1,0:T(8,128)(2,1)S(1)}, bf16[48,768]{1,0:T(8,128)(2,1)S(1)}, u32[]{:S(2)}, u32[]{:S(2)}) %collective-permute-start.41) | collective-permute-done | bytes 73760 | tf_op jit(solution)/shard_map/ppermute | solution.py:32
  212.5 5.4 %collective-permute-start.42 = (bf16[4,48,768]{2,1,0:T(8,128)(2,1)S(1)}, bf16[4,48,768]{2,1,0:T(8,128)(2,1)S(1)}, u32[]{:S(2)}, u32[]{:S(2)}) collective-permute-start(bf16[4,48,768]{2,1,0:T(8,128)(2,1)S(1)} %pad_maximum_fusion.31), channel_id=1, source_target_pairs={{0,2},{1,3},{2,0},{3,1},{4,6},{5,7},{6,4},{7,5},{8,10},{9,11},{10,... | collective-permute-start | bytes 884744 | tf_op jit(solution)/shard_map/ppermute | solution.py:32
  219.2 11.9 %collective-permute-done.42 = bf16[4,48,768]{2,1,0:T(8,128)(2,1)S(1)} collective-permute-done((bf16[4,48,768]{2,1,0:T(8,128)(2,1)S(1)}, bf16[4,48,768]{2,1,0:T(8,128)(2,1)S(1)}, u32[]{:S(2)}, u32[]{:S(2)}) %collective-permute-start.42) | collective-permute-done | bytes 294944 | tf_op jit(solution)/shard_map/ppermute | solution.py:32
  241.9 2.6 convert_reduce_fusion.4
  256.9 2.8 add_convert_fusion.5
  267.1 4.7 %collective-permute-done.36 = bf16[6,48,384]{2,1,0:T(8,128)(2,1)S(1)} collective-permute-done((bf16[6,48,384]{2,1,0:T(8,128)(2,1)S(1)}, bf16[6,48,384]{2,1,0:T(8,128)(2,1)S(1)}, u32[]{:S(2)}, u32[]{:S(2)}) %collective-permute-start.36) | collective-permute-done | bytes 221216 | tf_op jit(solution)/shard_map/ppermute | solution.py:32
  274.0 8.2 %collective-permute-done.34 = bf16[6,48,384]{2,1,0:T(8,128)(2,1)S(1)} collective-permute-done((bf16[6,48,384]{2,1,0:T(8,128)(2,1)S(1)}, bf16[6,48,384]{2,1,0:T(8,128)(2,1)S(1)}, u32[]{:S(2)}, u32[]{:S(2)}) %collective-permute-start.34) | collective-permute-done | bytes 221216 | tf_op jit(solution)/shard_map/ppermute | solution.py:32
  287.8 8.2 %collective-permute-done.37 = bf16[17,48,384]{2,1,0:T(8,128)(2,1)S(1)} collective-permute-done((bf16[17,48,384]{2,1,0:T(8,128)(2,1)S(1)}, bf16[17,48,384]{2,1,0:T(8,128)(2,1)S(1)}, u32[]{:S(2)}, u32[]{:S(2)}) %collective-permute-start.37) | collective-permute-done | bytes 626720 | tf_op jit(solution)/shard_map/ppermute | solution.py:32
  297.5 5.9 %collective-permute-start.38 = (bf16[17,96,384]{2,1,0:T(8,128)(2,1)}, bf16[17,96,384]{2,1,0:T(8,128)(2,1)}, u32[]{:S(2)}, u32[]{:S(2)}) collective-permute-start(bf16[17,96,384]{2,1,0:T(8,128)(2,1)} %fusion.27), channel_id=1, source_target_pairs={{0,4},{4,0},{8,12},{12,8},{1,5},{5,1},{9,13},{13,9},{2,6},{6,2},{1... | collective-permute-start | bytes 3760136 | tf_op jit(solution)/shard_map/ppermute | solution.py:32
  303.4 5.3 %collective-permute-done.44 = bf16[2,192,768]{2,1,0:T(8,128)(2,1)S(1)} collective-permute-done((bf16[2,192,768]{2,1,0:T(8,128)(2,1)S(1)}, bf16[2,192,768]{2,1,0:T(8,128)(2,1)S(1)}, u32[]{:S(2)}, u32[]{:S(2)}) %collective-permute-start.44) | collective-permute-done | bytes 589856 | tf_op jit(solution)/shard_map/ppermute | solution.py:32
  309.0 3.2 collective-permute-start.47
  312.2 2.4 pad_maximum_fusion.9.mine
  318.1 5.4 %place_mlp.1 = (f32[384,3072]{1,0:T(8,128)}, f32[2,2,384,768]{3,2,1,0:T(8,128)}) custom-call(s32[1]{0:T(128)} %bitcast.24.which, bf16[2,384,768]{2,1,0:T(8,128)(2,1)S(1)} %copy-done.3, bf16[2,384,768]{2,1,0:T(8,128)(2,1)S(1)} %pad_maximum_fusion.11.mine_down, bf16[2,384,768]{2,1,0:T(8,128)(2,1)} %collective-permute-done.47.other_up, ...), custom_call_target="tpu_custom_call" | custom-call | bytes 14155776 | tf_op jit(solution)/shard_map/place_mlp/pallas_call | solution.py:412
  327.6 4.1 %place_qkv.1 = (f32[384,2304]{1,0:T(8,128)}, f32[384,768]{1,0:T(8,128)}) custom-call(s32[1]{0:T(128)} %bitcast.24.which, bf16[16,96,384]{2,1,0:T(8,128)(2,1)S(1)} %copy-done.4, bf16[17,96,384]{2,1,0:T(8,128)(2,1)} %collective-permute-done.38.other), custom_call_target="tpu_custom_call" | custom-call | bytes 7077888 | tf_op jit(solution)/shard_map/place_qkv/pallas_call | solution.py:456
  (385 shorter events, 138.5 us)
Async XLA Ops:
  2.6 55.7 %collective-permute-start.6 = (bf16[272,768]{1,0:T(8,128)(2,1)S(1)}, bf16[272,768]{1,0:T(8,128)(2,1)S(1)}, u32[]{:S(2)}, u32[]{:S(2)}) collective-permute-start(bf16[272,768]{1,0:T(8,128)(2,1)S(1)} %fusion.54.refs_0_), channel_id=1, source_target_pairs={{0,3},{1,2},{2,1},{3,0},{4,7},{5,6},{6,5},{7,4},{8,11},{9,10},{10,... | collective-permute-start | bytes 1253384 | tf_op jit(solution)/shard_map/ppermute | solution.py:32
  4.0 54.4 %collective-permute-start.5 = (bf16[272,768]{1,0:T(8,128)(2,1)S(1)}, bf16[272,768]{1,0:T(8,128)(2,1)}, u32[]{:S(2)}, u32[]{:S(2)}) collective-permute-start(bf16[272,768]{1,0:T(8,128)(2,1)S(1)} %fusion.54.refs_0_), channel_id=1, source_target_pairs={{0,2},{1,3},{2,0},{3,1},{4,6},{5,7},{6,4},{7,5},{8,10},{9,11},{10,... | collective-permute-start | bytes 1253384 | tf_op jit(solution)/shard_map/ppermute | solution.py:32
  5.1 53.3 %collective-permute-start.4 = (bf16[272,768]{1,0:T(8,128)(2,1)S(1)}, bf16[272,768]{1,0:T(8,128)(2,1)}, u32[]{:S(2)}, u32[]{:S(2)}) collective-permute-start(bf16[272,768]{1,0:T(8,128)(2,1)S(1)} %fusion.54.refs_0_), channel_id=1, source_target_pairs={{0,1},{1,0},{2,3},{3,2},{4,5},{5,4},{6,7},{7,6},{8,9},{9,8},{10,11... | collective-permute-start | bytes 1253384 | tf_op jit(solution)/shard_map/ppermute | solution.py:32
  32.2 16.9 %collective-permute-start.16 = (bf16[2,256,768]{2,1,0:T(8,128)(2,1)}, bf16[2,256,768]{2,1,0:T(8,128)(2,1)}, u32[]{:S(2)}, u32[]{:S(2)}) collective-permute-start(bf16[2,256,768]{2,1,0:T(8,128)(2,1)} %pad_maximum_fusion.15), channel_id=1, source_target_pairs={{0,16},{16,0},{1,17},{17,1},{2,18},{18,2},{3,19},{19,3},{4,20},{20... | collective-permute-start | bytes 2359304 | tf_op jit(solution)/shard_map/ppermute | solution.py:32
  49.1 13.8 %collective-permute-start.12 = (bf16[192,2304]{1,0:T(8,128)(2,1)S(1)}, bf16[192,2304]{1,0:T(8,128)(2,1)S(1)}, u32[]{:S(2)}, u32[]{:S(2)}) collective-permute-start(bf16[192,2304]{1,0:T(8,128)(2,1)S(1)} %pad_maximum_fusion.14), channel_id=1, source_target_pairs={{0,4},{4,0},{8,12},{12,8},{1,5},{5,1},{9,13},{13,9},{2,6},{6,2},{1... | collective-permute-start | bytes 2654216 | tf_op jit(solution)/shard_map/ppermute | solution.py:32
  62.3 21.2 %collective-permute-start.8 = (bf16[400,1024]{1,0:T(8,128)(2,1)S(1)}, bf16[400,1024]{1,0:T(8,128)(2,1)S(1)}, u32[]{:S(2)}, u32[]{:S(2)}) collective-permute-start(bf16[400,1024]{1,0:T(8,128)(2,1)S(1)} %get-tuple-element.70.refs_0_), channel_id=1, source_target_pairs={{0,8},{4,12},{8,0},{12,4},{1,9},{5,13},{9,1},{13,5},{2,10},{6,14},... | collective-permute-start | bytes 2457608 | tf_op jit(solution)/shard_map/ppermute | solution.py:32
  62.6 20.9 %collective-permute-start.7 = (bf16[400,1024]{1,0:T(8,128)(2,1)S(1)}, bf16[400,1024]{1,0:T(8,128)(2,1)S(1)}, u32[]{:S(2)}, u32[]{:S(2)}) collective-permute-start(bf16[400,1024]{1,0:T(8,128)(2,1)S(1)} %get-tuple-element.70.refs_0_), channel_id=1, source_target_pairs={{0,4},{4,0},{8,12},{12,8},{1,5},{5,1},{9,13},{13,9},{2,6},{6,2},{1... | collective-permute-start | bytes 2457608 | tf_op jit(solution)/shard_map/ppermute | solution.py:32
  67.7 15.0 %collective-permute-start.15 = (bf16[192,256]{1,0:T(8,128)(2,1)S(1)}, bf16[192,256]{1,0:T(8,128)(2,1)S(1)}, u32[]{:S(2)}, u32[]{:S(2)}) collective-permute-start(bf16[192,256]{1,0:T(8,128)(2,1)S(1)} %get-tuple-element.203), channel_id=1, source_target_pairs={{0,3},{1,2},{2,1},{3,0},{4,7},{5,6},{6,5},{7,4},{8,11},{9,10},{10,... | collective-permute-start | bytes 294920 | tf_op jit(solution)/shard_map/ppermute | solution.py:32
  68.9 13.7 %collective-permute-start.14 = (bf16[192,256]{1,0:T(8,128)(2,1)S(1)}, bf16[192,256]{1,0:T(8,128)(2,1)S(1)}, u32[]{:S(2)}, u32[]{:S(2)}) collective-permute-start(bf16[192,256]{1,0:T(8,128)(2,1)S(1)} %get-tuple-element.204), channel_id=1, source_target_pairs={{0,2},{1,3},{2,0},{3,1},{4,6},{5,7},{6,4},{7,5},{8,10},{9,11},{10,... | collective-permute-start | bytes 294920 | tf_op jit(solution)/shard_map/ppermute | solution.py:32
  70.0 12.7 %collective-permute-start.13 = (bf16[192,256]{1,0:T(8,128)(2,1)S(1)}, bf16[192,256]{1,0:T(8,128)(2,1)S(1)}, u32[]{:S(2)}, u32[]{:S(2)}) collective-permute-start(bf16[192,256]{1,0:T(8,128)(2,1)S(1)} %get-tuple-element.205), channel_id=1, source_target_pairs={{0,1},{1,0},{2,3},{3,2},{4,5},{5,4},{6,7},{7,6},{8,9},{9,8},{10,11... | collective-permute-start | bytes 294920 | tf_op jit(solution)/shard_map/ppermute | solution.py:32
  94.6 53.2 %collective-permute-start.20 = (bf16[256,768]{1,0:T(8,128)(2,1)S(1)}, bf16[256,768]{1,0:T(8,128)(2,1)}, u32[]{:S(2)}, u32[]{:S(2)}) collective-permute-start(bf16[256,768]{1,0:T(8,128)(2,1)S(1)} %copy-done.36), channel_id=1, source_target_pairs={{0,3},{1,2},{2,1},{3,0},{4,7},{5,6},{6,5},{7,4},{8,11},{9,10},{10,... | collective-permute-start | bytes 1179656 | tf_op jit(solution)/shard_map/ppermute | solution.py:32
  95.8 52.0 %collective-permute-start.19 = (bf16[256,768]{1,0:T(8,128)(2,1)S(1)}, bf16[256,768]{1,0:T(8,128)(2,1)}, u32[]{:S(2)}, u32[]{:S(2)}) collective-permute-start(bf16[256,768]{1,0:T(8,128)(2,1)S(1)} %copy-done.36), channel_id=1, source_target_pairs={{0,2},{1,3},{2,0},{3,1},{4,6},{5,7},{6,4},{7,5},{8,10},{9,11},{10,... | collective-permute-start | bytes 1179656 | tf_op jit(solution)/shard_map/ppermute | solution.py:32
  97.7 50.1 %collective-permute-start.18 = (bf16[256,768]{1,0:T(8,128)(2,1)S(1)}, bf16[256,768]{1,0:T(8,128)(2,1)}, u32[]{:S(2)}, u32[]{:S(2)}) collective-permute-start(bf16[256,768]{1,0:T(8,128)(2,1)S(1)} %copy-done.36), channel_id=1, source_target_pairs={{0,1},{1,0},{2,3},{3,2},{4,5},{5,4},{6,7},{7,6},{8,9},{9,8},{10,11... | collective-permute-start | bytes 1179656 | tf_op jit(solution)/shard_map/ppermute | solution.py:32
  98.6 43.3 %collective-permute-start.22 = (bf16[512,768]{1,0:T(8,128)(2,1)S(1)}, bf16[512,768]{1,0:T(8,128)(2,1)}, u32[]{:S(2)}, u32[]{:S(2)}) collective-permute-start(bf16[512,768]{1,0:T(8,128)(2,1)S(1)} %pad_maximum_fusion.18), channel_id=1, source_target_pairs={{0,16},{16,0},{1,17},{17,1},{2,18},{18,2},{3,19},{19,3},{4,20},{20... | collective-permute-start | bytes 2359304 | tf_op jit(solution)/shard_map/ppermute | solution.py:32
  98.9 46.9 %collective-permute-start.21 = (bf16[2,2,192,768]{3,2,1,0:T(8,128)(2,1)S(1)}, bf16[2,2,192,768]{3,2,1,0:T(8,128)(2,1)}, u32[]{:S(2)}, u32[]{:S(2)}) collective-permute-start(bf16[2,2,192,768]{3,2,1,0:T(8,128)(2,1)S(1)} %broadcast_select_fusion.6), channel_id=1, source_target_pairs={{0,8},{4,12},{8,0},{12,4},{1,9},{5,13},{9,1},{13,5},{2,10},{6,14},... | collective-permute-start | bytes 3538952 | tf_op jit(solution)/shard_map/ppermute | solution.py:32
  156.4 14.1 %collective-permute-start.25 = (bf16[384,256]{1,0:T(8,128)(2,1)S(1)}, bf16[384,256]{1,0:T(8,128)(2,1)S(1)}, u32[]{:S(2)}, u32[]{:S(2)}) collective-permute-start(bf16[384,256]{1,0:T(8,128)(2,1)S(1)} %get-tuple-element.187), channel_id=1, source_target_pairs={{0,2},{1,3},{2,0},{3,1},{4,6},{5,7},{6,4},{7,5},{8,10},{9,11},{10,... | collective-permute-start | bytes 589832 | tf_op jit(solution)/shard_map/ppermute | solution.py:32
  170.5 14.7 %collective-permute-start.39 = (bf16[2,2,96,768]{3,2,1,0:T(8,128)(2,1)S(1)}, bf16[2,2,96,768]{3,2,1,0:T(8,128)(2,1)S(1)}, u32[]{:S(2)}, u32[]{:S(2)}) collective-permute-start(bf16[2,2,96,768]{3,2,1,0:T(8,128)(2,1)S(1)} %broadcast_select_fusion.13), channel_id=1, source_target_pairs={{0,1},{1,0},{2,3},{3,2},{4,5},{5,4},{6,7},{7,6},{8,9},{9,8},{10,11... | collective-permute-start | bytes 1769480 | tf_op jit(solution)/shard_map/ppermute | solution.py:32
  172.8 17.5 %collective-permute-start.27 = (bf16[1,384,1024]{2,1,0:T(8,128)(2,1)S(1)}, bf16[1,384,1024]{2,1,0:T(8,128)(2,1)S(1)}, u32[]{:S(2)}, u32[]{:S(2)}) collective-permute-start(bf16[1,384,1024]{2,1,0:T(8,128)(2,1)S(1)} %add_convert_fusion.2), channel_id=1, source_target_pairs={{0,8},{4,12},{8,0},{12,4},{1,9},{5,13},{9,1},{13,5},{2,10},{6,14},... | collective-permute-start | bytes 2359304 | tf_op jit(solution)/shard_map/ppermute | solution.py:32
  186.2 21.6 %collective-permute-start.40 = (bf16[2,2,48,768]{3,2,1,0:T(8,128)(2,1)}, bf16[2,2,48,768]{3,2,1,0:T(8,128)(2,1)}, u32[]{:S(2)}, u32[]{:S(2)}) collective-permute-start(bf16[2,2,48,768]{3,2,1,0:T(8,128)(2,1)} %broadcast_select_fusion.25), channel_id=1, source_target_pairs={{0,2},{1,3},{2,0},{3,1},{4,6},{5,7},{6,4},{7,5},{8,10},{9,11},{10,... | collective-permute-start | bytes 884744 | tf_op jit(solution)/shard_map/ppermute | solution.py:32
  194.2 39.3 %collective-permute-start.30 = (bf16[384,256]{1,0:T(8,128)(2,1)}, bf16[384,256]{1,0:T(8,128)(2,1)S(1)}, u32[]{:S(2)}, u32[]{:S(2)}) collective-permute-start(bf16[384,256]{1,0:T(8,128)(2,1)} %get-tuple-element.176), channel_id=1, source_target_pairs={{0,3},{1,2},{2,1},{3,0},{4,7},{5,6},{6,5},{7,4},{8,11},{9,10},{10,... | collective-permute-start | bytes 589832 | tf_op jit(solution)/shard_map/ppermute | solution.py:32
  195.4 38.1 %collective-permute-start.28 = (bf16[384,256]{1,0:T(8,128)(2,1)}, bf16[384,256]{1,0:T(8,128)(2,1)S(1)}, u32[]{:S(2)}, u32[]{:S(2)}) collective-permute-start(bf16[384,256]{1,0:T(8,128)(2,1)} %get-tuple-element.178), channel_id=1, source_target_pairs={{0,1},{1,0},{2,3},{3,2},{4,5},{5,4},{6,7},{7,6},{8,9},{9,8},{10,11... | collective-permute-start | bytes 589832 | tf_op jit(solution)/shard_map/ppermute | solution.py:32
  196.6 36.8 %collective-permute-start.29 = (bf16[384,256]{1,0:T(8,128)(2,1)}, bf16[384,256]{1,0:T(8,128)(2,1)S(1)}, u32[]{:S(2)}, u32[]{:S(2)}) collective-permute-start(bf16[384,256]{1,0:T(8,128)(2,1)} %get-tuple-element.179), channel_id=1, source_target_pairs={{0,2},{1,3},{2,0},{3,1},{4,6},{5,7},{6,4},{7,5},{8,10},{9,11},{10,... | collective-permute-start | bytes 589832 | tf_op jit(solution)/shard_map/ppermute | solution.py:32
  199.4 18.6 %collective-permute-start.31 = (bf16[4,96,768]{2,1,0:T(8,128)(2,1)S(1)}, bf16[4,96,768]{2,1,0:T(8,128)(2,1)S(1)}, u32[]{:S(2)}, u32[]{:S(2)}) collective-permute-start(bf16[4,96,768]{2,1,0:T(8,128)(2,1)S(1)} %broadcast_select_fusion.20), channel_id=1, source_target_pairs={{0,4},{4,0},{8,12},{12,8},{1,5},{5,1},{9,13},{13,9},{2,6},{6,2},{1... | collective-permute-start | bytes 1769480 | tf_op jit(solution)/shard_map/ppermute | solution.py:32
  212.5 18.5 %collective-permute-start.42 = (bf16[4,48,768]{2,1,0:T(8,128)(2,1)S(1)}, bf16[4,48,768]{2,1,0:T(8,128)(2,1)S(1)}, u32[]{:S(2)}, u32[]{:S(2)}) collective-permute-start(bf16[4,48,768]{2,1,0:T(8,128)(2,1)S(1)} %pad_maximum_fusion.31), channel_id=1, source_target_pairs={{0,2},{1,3},{2,0},{3,1},{4,6},{5,7},{6,4},{7,5},{8,10},{9,11},{10,... | collective-permute-start | bytes 884744 | tf_op jit(solution)/shard_map/ppermute | solution.py:32
  218.2 13.7 %collective-permute-start.32 = (bf16[4,48,768]{2,1,0:T(8,128)(2,1)S(1)}, bf16[4,48,768]{2,1,0:T(8,128)(2,1)S(1)}, u32[]{:S(2)}, u32[]{:S(2)}) collective-permute-start(bf16[4,48,768]{2,1,0:T(8,128)(2,1)S(1)} %broadcast_select_fusion.32), channel_id=1, source_target_pairs={{0,8},{4,12},{8,0},{12,4},{1,9},{5,13},{9,1},{13,5},{2,10},{6,14},... | collective-permute-start | bytes 884744 | tf_op jit(solution)/shard_map/ppermute | solution.py:32
  263.4 18.7 %collective-permute-start.34 = (bf16[6,48,384]{2,1,0:T(8,128)(2,1)S(1)}, bf16[6,48,384]{2,1,0:T(8,128)(2,1)S(1)}, u32[]{:S(2)}, u32[]{:S(2)}) collective-permute-start(bf16[6,48,384]{2,1,0:T(8,128)(2,1)S(1)} %add_convert_fusion.8), channel_id=1, source_target_pairs={{0,3},{1,2},{2,1},{3,0},{4,7},{5,6},{6,5},{7,4},{8,11},{9,10},{10,... | collective-permute-start | bytes 663560 | tf_op jit(solution)/shard_map/ppermute | solution.py:32
  263.8 20.3 %collective-permute-start.43 = (bf16[2,96,768]{2,1,0:T(8,128)(2,1)S(1)}, bf16[2,96,768]{2,1,0:T(8,128)(2,1)S(1)}, u32[]{:S(2)}, u32[]{:S(2)}) collective-permute-start(bf16[2,96,768]{2,1,0:T(8,128)(2,1)S(1)} %get-tuple-element.190), channel_id=1, source_target_pairs={{0,1},{1,0},{2,3},{3,2},{4,5},{5,4},{6,7},{7,6},{8,9},{9,8},{10,11... | collective-permute-start | bytes 884744 | tf_op jit(solution)/shard_map/ppermute | solution.py:32
  266.2 19.6 %collective-permute-start.46 = (bf16[2,192,768]{2,1,0:T(8,128)(2,1)S(1)}, bf16[2,192,768]{2,1,0:T(8,128)(2,1)S(1)}, u32[]{:S(2)}, u32[]{:S(2)}) collective-permute-start(bf16[2,192,768]{2,1,0:T(8,128)(2,1)S(1)} %pad_maximum_fusion.22), channel_id=1, source_target_pairs={{0,8},{4,12},{8,0},{12,4},{1,9},{5,13},{9,1},{13,5},{2,10},{6,14},... | collective-permute-start | bytes 1769480 | tf_op jit(solution)/shard_map/ppermute | solution.py:32
  282.5 13.4 %collective-permute-start.37 = (bf16[17,48,384]{2,1,0:T(8,128)(2,1)S(1)}, bf16[17,48,384]{2,1,0:T(8,128)(2,1)S(1)}, u32[]{:S(2)}, u32[]{:S(2)}) collective-permute-start(bf16[17,48,384]{2,1,0:T(8,128)(2,1)S(1)} %get-tuple-element.127), channel_id=1, source_target_pairs={{0,8},{4,12},{8,0},{12,4},{1,9},{5,13},{9,1},{13,5},{2,10},{6,14},... | collective-permute-start | bytes 1880072 | tf_op jit(solution)/shard_map/ppermute | solution.py:32
  284.3 24.4 %collective-permute-start.44 = (bf16[2,192,768]{2,1,0:T(8,128)(2,1)S(1)}, bf16[2,192,768]{2,1,0:T(8,128)(2,1)S(1)}, u32[]{:S(2)}, u32[]{:S(2)}) collective-permute-start(bf16[2,192,768]{2,1,0:T(8,128)(2,1)S(1)} %pad_maximum_fusion.21), channel_id=1, source_target_pairs={{0,8},{4,12},{8,0},{12,4},{1,9},{5,13},{9,1},{13,5},{2,10},{6,14},... | collective-permute-start | bytes 1769480 | tf_op jit(solution)/shard_map/ppermute | solution.py:32
  286.1 28.5 %collective-permute-start.48 = (bf16[2,384,768]{2,1,0:T(8,128)(2,1)S(1)}, bf16[2,384,768]{2,1,0:T(8,128)(2,1)S(1)}, u32[]{:S(2)}, u32[]{:S(2)}) collective-permute-start(bf16[2,384,768]{2,1,0:T(8,128)(2,1)S(1)} %pad_maximum_fusion.11.mine_down), channel_id=1, source_target_pairs={{0,4},{4,0},{8,12},{12,8},{1,5},{5,1},{9,13},{13,9},{2,6},{6,2},{1... | collective-permute-start | bytes 3538952 | tf_op jit(solution)/shard_map/ppermute | solution.py:32
  297.5 26.1 %collective-permute-start.38 = (bf16[17,96,384]{2,1,0:T(8,128)(2,1)}, bf16[17,96,384]{2,1,0:T(8,128)(2,1)}, u32[]{:S(2)}, u32[]{:S(2)}) collective-permute-start(bf16[17,96,384]{2,1,0:T(8,128)(2,1)} %fusion.27), channel_id=1, source_target_pairs={{0,4},{4,0},{8,12},{12,8},{1,5},{5,1},{9,13},{13,9},{2,6},{6,2},{1... | collective-permute-start | bytes 3760136 | tf_op jit(solution)/shard_map/ppermute | solution.py:32
  (88 other events, 836.4 us)

commit v6 on v5

--- a/solution.py
+++ b/solution.py
@@ -386,9 +386,8 @@
     return sums
 
 
-def spread_pair(sums, near, *earlier):
+def spread_pair(sums, *earlier):
     mine, other = [], []
-    sums = after(sums, near)
     for part in (sums[:2], sums[2:]):
         part = share_half(share_half(part, "ulysses", 1, 1), "blk", 2, 1)
         mine.append(after(part, *earlier))
@@ -684,7 +683,7 @@
     input_grad = (e_float + d_x_one + d_x_two).astype(bf16)
 
     vector = jnp.concatenate(vectors)
-    g_up, g_down = spread(terms, vector, output, input_grad)
+    g_up, g_down = spread(terms, output, input_grad)
     g_qkv, g_out, summed = attention_grads(grads, vector, output, g_up)
     results, start = [], 0
     for vector in vectors:

time: 339 us -> 341 us (level)
  waiting for transfers between devices: 91.9 us -> 123 us
  local copies, waits for them, and re-layouts: 37.3 us -> 28.6 us
  other arithmetic: 49.8 us -> 43.2 us
  Pallas kernels: 55.5 us -> 50 us
  matrix products: 26.8 us -> 22.4 us
    ppermute x49, waiting for transfers between devices: 91.9 us -> 123 us  [swap(): return lax.ppermute(values, axis, [(i, i ^ bits) for i in range(count)])]
    pallas_call x1, Pallas kernels: 42.5 us -> 36.9 us  [attend(): pl.pallas_call(attend_kernel, grid_spec=pltpu.PrefetchScalarGridSpec(num_...]
    unnamed x172 -> x145, local copies, waits for them, and re-layouts: 23.3 us -> 20.5 us
  transfers between devices with their start and end apart: 49 -> 49, of which waited for: 21 -> 22; matrix products, arithmetic and copies ran while one was open for 22% -> 20% of each run, Pallas kernels for 15% -> 14%
where the time goes in v6:
time: 341 us; the launch traced here: 337 us
  waiting for transfers between devices  123 us (36%)
  starting transfers between devices  67.7 us (20%)
  Pallas kernels  50 us (15%)
  other arithmetic  43.2 us (13%)
  local copies, waits for them, and re-layouts  28.6 us (8%)
  matrix products  22.4 us (7%)
    ppermute x49, waiting for transfers between devices, swap(): return lax.ppermute(values, axis, [(i, i ^ bits) for i in range(count)])  123 us
    ppermute x49, starting transfers between devices, swap(): return lax.ppermute(values, axis, [(i, i ^ bits) for i in range(count)])  67.7 us
    pallas_call x1, Pallas kernels, attend(): pl.pallas_call(attend_kernel, grid_spec=pltpu.PrefetchScalarGridSpec(num_...  36.9 us
    unnamed x145, local copies, waits for them, and re-layouts  20.5 us
    dot_general x1, matrix products, mlp_pair(): jnp.dot(normed, up, preferred_element_type=f32) + up_bias.astype(f32)  8.14 us
  transfers between devices with their start and end apart: 49, of which 22 were waited for; matrix products, arithmetic and copies ran while one was open for 20% of the time, Pallas kernels for 14%

profile of v6, /device:TPU:9, one launch (start us, length us, event | category | flops | bytes accessed | tf_op | source)
XLA Modules:
  0.0 337.3 jit_solution(16563763759463846122)
XLA Ops:
  9.3 3.2 broadcast_select_fusion.8
  16.2 2.6 collective-permute-done
  23.3 7.5 %collective-permute-done.10 = bf16[96,2304]{1,0:T(8,128)(2,1)} collective-permute-done((bf16[96,2304]{1,0:T(8,128)(2,1)}, bf16[96,2304]{1,0:T(8,128)(2,1)}, u32[]{:S(2)}, u32[]{:S(2)}) %collective-permute-start.10) | collective-permute-done | bytes 442400 | tf_op jit(solution)/shard_map/ppermute | solution.py:32
  33.3 3.6 %collective-permute-start.3 = (bf16[192,2304]{1,0:T(8,128)(2,1)S(1)}, bf16[192,2304]{1,0:T(8,128)(2,1)S(1)}, u32[]{:S(2)}, u32[]{:S(2)}) collective-permute-start(bf16[192,2304]{1,0:T(8,128)(2,1)S(1)} %pad_maximum_fusion.13), channel_id=1, source_target_pairs={{0,4},{4,0},{8,12},{12,8},{1,5},{5,1},{9,13},{13,9},{2,6},{6,2},{1... | collective-permute-start | bytes 2654216 | tf_op jit(solution)/shard_map/ppermute | solution.py:32
  36.9 3.4 %collective-permute-done.11 = bf16[96,2304]{1,0:T(8,128)(2,1)S(1)} collective-permute-done((bf16[96,2304]{1,0:T(8,128)(2,1)}, bf16[96,2304]{1,0:T(8,128)(2,1)S(1)}, u32[]{:S(2)}, u32[]{:S(2)}) %collective-permute-start.11) | collective-permute-done | bytes 442400 | tf_op jit(solution)/shard_map/ppermute | solution.py:32
  43.7 13.5 %collective-permute-done.16 = bf16[2,256,768]{2,1,0:T(8,128)(2,1)S(1)} collective-permute-done((bf16[2,256,768]{2,1,0:T(8,128)(2,1)S(1)}, bf16[2,256,768]{2,1,0:T(8,128)(2,1)S(1)}, u32[]{:S(2)}, u32[]{:S(2)}) %collective-permute-start.16) | collective-permute-done | bytes 786464 | tf_op jit(solution)/shard_map/ppermute | solution.py:32
  57.2 3.9 %collective-permute-start.12 = (bf16[192,2304]{1,0:T(8,128)(2,1)S(1)}, bf16[192,2304]{1,0:T(8,128)(2,1)S(1)}, u32[]{:S(2)}, u32[]{:S(2)}) collective-permute-start(bf16[192,2304]{1,0:T(8,128)(2,1)S(1)} %pad_maximum_fusion.14), channel_id=1, source_target_pairs={{0,4},{4,0},{8,12},{12,8},{1,5},{5,1},{9,13},{13,9},{2,6},{6,2},{1... | collective-permute-start | bytes 2654216 | tf_op jit(solution)/shard_map/ppermute | solution.py:32
  65.8 3.5 %prepare.1 = (bf16[1024,768]{1,0:T(8,128)(2,1)S(1)}, bf16[192,1024]{1,0:T(8,128)(2,1)S(1)}, bf16[400,1024]{1,0:T(8,128)(2,1)S(1)}, f32[8,1024]{1,0:T(8,128)S(1)}, f32[8,1024]{1,0:T(8,128)S(1)}) custom-call(f32[8,1]{1,0:T(8,128)S(1)} %copy-done.9, f32[1,768]{1,0:T(1,128)S(1)} %bitcast.78, f32[1,768]{1,0:T(1,128)S(1)} %bitcast.77, ...), custom_call_target="tpu_custom_call" | custom-call | flops 905969664 | bytes 6291456 | tf_op jit(solution)/shard_map/prepare/pallas_call | solution.py:301
  78.8 8.1 %multiply_convert_fusion = (bf16[512,1536]{1,0:T(8,128)(2,1)S(1)}, f32[512,1536]{1,0:T(8,128)S(1)}, f32[512,1536]{1,0:T(8,128)S(1)}) fusion(f32[1536]{0:T(1024)S(1)} %convert_element_type.285, bf16[768,1536]{1,0:T(8,128)(2,1)S(1)} %pad_maximum_fusion.3, bf16[512,768]{1,0:T(8,128)(2,1)S(1)} %pad_maximum_fusion.16, f32[768]{0:T(1024)S(1)} %reshape.234, ...), kind=kOutput, calls=%fused_computation.18 | convolution fusion | flops 1262223360 | bytes 11026432 | tf_op jit(solution)/shard_map/dot_general | solution.py:352
  108.3 36.9 %attend.1 = (bf16[3,64,1024]{2,1,0:T(8,128)(2,1)}, f32[3,64,1024]{2,1,0:T(8,128)}, bf16[2,384,1024]{2,1,0:T(8,128)(2,1)}, bf16[2,384,1024]{2,1,0:T(8,128)(2,1)}) custom-call(s32[32]{0:T(128)} %maximum_convert_fusion.5.rank, bf16[3,64,1024]{2,1,0:T(8,128)(2,1)} %bitcast.79, bf16[3,64,1024]{2,1,0:T(8,128)(2,1)} %bitcast.95, bf16[400,1024]{1,0:T(8,128)(2,1)} %copy-done.7, ...), custom_call_target="tpu_custom_call" | custom-call | flops 38654705664 | bytes 12582912 | tf_op jit(solution)/shard_map/attend/pallas_call | solution.py:224
  150.7 7.2 %collective-permute-start.23 = (bf16[2,384,1024]{2,1,0:T(8,128)(2,1)}, bf16[2,384,1024]{2,1,0:T(8,128)(2,1)}, u32[]{:S(2)}, u32[]{:S(2)}) collective-permute-start(bf16[2,384,1024]{2,1,0:T(8,128)(2,1)} %get-tuple-element.83), channel_id=1, source_target_pairs={{0,4},{4,0},{8,12},{12,8},{1,5},{5,1},{9,13},{13,9},{2,6},{6,2},{1... | collective-permute-start | bytes 4718600 | tf_op jit(solution)/shard_map/ppermute | solution.py:32
  161.6 2.7 collective-permute-start.24
  167.7 3.4 %collective-permute-done.26 = bf16[384,256]{1,0:T(8,128)(2,1)S(1)} collective-permute-done((bf16[384,256]{1,0:T(8,128)(2,1)S(1)}, bf16[384,256]{1,0:T(8,128)(2,1)S(1)}, u32[]{:S(2)}, u32[]{:S(2)}) %collective-permute-start.26) | collective-permute-done | bytes 196640 | tf_op jit(solution)/shard_map/ppermute | solution.py:32
  171.1 2.4 collective-permute-done.24
  173.6 5.0 %collective-permute-done.25 = bf16[384,256]{1,0:T(8,128)(2,1)S(1)} collective-permute-done((bf16[384,256]{1,0:T(8,128)(2,1)S(1)}, bf16[384,256]{1,0:T(8,128)(2,1)S(1)}, u32[]{:S(2)}, u32[]{:S(2)}) %collective-permute-start.25) | collective-permute-done | bytes 196640 | tf_op jit(solution)/shard_map/ppermute | solution.py:32
  184.9 8.8 %collective-permute-done.39 = bf16[2,2,96,768]{3,2,1,0:T(8,128)(2,1)S(1)} collective-permute-done((bf16[2,2,96,768]{3,2,1,0:T(8,128)(2,1)S(1)}, bf16[2,2,96,768]{3,2,1,0:T(8,128)(2,1)S(1)}, u32[]{:S(2)}, u32[]{:S(2)}) %collective-permute-start.39) | collective-permute-done | bytes 589856 | tf_op jit(solution)/shard_map/ppermute | solution.py:32
  196.1 2.6 collective-permute-done.27
  203.0 6.1 %collective-permute-done.40 = bf16[2,2,48,768]{3,2,1,0:T(8,128)(2,1)S(1)} collective-permute-done((bf16[2,2,48,768]{3,2,1,0:T(8,128)(2,1)S(1)}, bf16[2,2,48,768]{3,2,1,0:T(8,128)(2,1)S(1)}, u32[]{:S(2)}, u32[]{:S(2)}) %collective-permute-start.40) | collective-permute-done | bytes 294944 | tf_op jit(solution)/shard_map/ppermute | solution.py:32
  209.4 3.2 collective-permute-done.41
  212.6 3.2 collective-permute-start.42
  223.1 13.0 %collective-permute-done.42 = bf16[4,48,768]{2,1,0:T(8,128)(2,1)} collective-permute-done((bf16[4,48,768]{2,1,0:T(8,128)(2,1)S(1)}, bf16[4,48,768]{2,1,0:T(8,128)(2,1)}, u32[]{:S(2)}, u32[]{:S(2)}) %collective-permute-start.42) | collective-permute-done | bytes 294944 | tf_op jit(solution)/shard_map/ppermute | solution.py:32
  237.8 3.2 collective-permute-start.45
  242.4 9.3 %collective-permute-done.45 = bf16[2,96,768]{2,1,0:T(8,128)(2,1)S(1)} collective-permute-done((bf16[2,96,768]{2,1,0:T(8,128)(2,1)S(1)}, bf16[2,96,768]{2,1,0:T(8,128)(2,1)S(1)}, u32[]{:S(2)}, u32[]{:S(2)}) %collective-permute-start.45) | collective-permute-done | bytes 294944 | tf_op jit(solution)/shard_map/ppermute | solution.py:32
  252.7 7.1 %collective-permute-done.32 = bf16[4,48,768]{2,1,0:T(8,128)(2,1)S(1)} collective-permute-done((bf16[4,48,768]{2,1,0:T(8,128)(2,1)S(1)}, bf16[4,48,768]{2,1,0:T(8,128)(2,1)S(1)}, u32[]{:S(2)}, u32[]{:S(2)}) %collective-permute-start.32) | collective-permute-done | bytes 294944 | tf_op jit(solution)/shard_map/ppermute | solution.py:32
  269.3 2.8 collective-permute-done.33
  276.6 5.3 %collective-permute-done.36 = bf16[6,48,384]{2,1,0:T(8,128)(2,1)S(1)} collective-permute-done((bf16[6,48,384]{2,1,0:T(8,128)(2,1)S(1)}, bf16[6,48,384]{2,1,0:T(8,128)(2,1)S(1)}, u32[]{:S(2)}, u32[]{:S(2)}) %collective-permute-start.36) | collective-permute-done | bytes 221216 | tf_op jit(solution)/shard_map/ppermute | solution.py:32
  283.4 11.6 %collective-permute-done.34 = bf16[6,48,384]{2,1,0:T(8,128)(2,1)S(1)} collective-permute-done((bf16[6,48,384]{2,1,0:T(8,128)(2,1)S(1)}, bf16[6,48,384]{2,1,0:T(8,128)(2,1)S(1)}, u32[]{:S(2)}, u32[]{:S(2)}) %collective-permute-start.34) | collective-permute-done | bytes 221216 | tf_op jit(solution)/shard_map/ppermute | solution.py:32
  299.1 9.6 %collective-permute-done.37 = bf16[17,48,384]{2,1,0:T(8,128)(2,1)S(1)} collective-permute-done((bf16[17,48,384]{2,1,0:T(8,128)(2,1)S(1)}, bf16[17,48,384]{2,1,0:T(8,128)(2,1)S(1)}, u32[]{:S(2)}, u32[]{:S(2)}) %collective-permute-start.37) | collective-permute-done | bytes 626720 | tf_op jit(solution)/shard_map/ppermute | solution.py:32
  310.2 3.2 collective-permute-start.38
  316.5 2.8 collective-permute-done.47.other_up
  322.9 5.4 %place_mlp.1 = (f32[384,3072]{1,0:T(8,128)}, f32[2,2,384,768]{3,2,1,0:T(8,128)}) custom-call(s32[1]{0:T(128)} %bitcast.24.which, bf16[2,384,768]{2,1,0:T(8,128)(2,1)S(1)} %copy-done.3, bf16[2,384,768]{2,1,0:T(8,128)(2,1)S(1)} %pad_maximum_fusion.11.mine_down, bf16[2,384,768]{2,1,0:T(8,128)(2,1)S(1)} %copy-done.6, ...), custom_call_target="tpu_custom_call" | custom-call | bytes 14155776 | tf_op jit(solution)/shard_map/place_mlp/pallas_call | solution.py:411
  332.4 4.1 %place_qkv.1 = (f32[384,2304]{1,0:T(8,128)}, f32[384,768]{1,0:T(8,128)}) custom-call(s32[1]{0:T(128)} %bitcast.24.which, bf16[16,96,384]{2,1,0:T(8,128)(2,1)S(1)} %copy-done.4, bf16[17,96,384]{2,1,0:T(8,128)(2,1)} %collective-permute-done.38.other), custom_call_target="tpu_custom_call" | custom-call | bytes 7077888 | tf_op jit(solution)/shard_map/place_qkv/pallas_call | solution.py:455
  (356 shorter events, 126.8 us)
Async XLA Ops:
  2.6 62.8 %collective-permute-start.6 = (bf16[272,768]{1,0:T(8,128)(2,1)S(1)}, bf16[272,768]{1,0:T(8,128)(2,1)S(1)}, u32[]{:S(2)}, u32[]{:S(2)}) collective-permute-start(bf16[272,768]{1,0:T(8,128)(2,1)S(1)} %fusion.52.refs_0_), channel_id=1, source_target_pairs={{0,3},{1,2},{2,1},{3,0},{4,7},{5,6},{6,5},{7,4},{8,11},{9,10},{10,... | collective-permute-start | bytes 1253384 | tf_op jit(solution)/shard_map/ppermute | solution.py:32
  4.0 61.5 %collective-permute-start.5 = (bf16[272,768]{1,0:T(8,128)(2,1)S(1)}, bf16[272,768]{1,0:T(8,128)(2,1)}, u32[]{:S(2)}, u32[]{:S(2)}) collective-permute-start(bf16[272,768]{1,0:T(8,128)(2,1)S(1)} %fusion.52.refs_0_), channel_id=1, source_target_pairs={{0,2},{1,3},{2,0},{3,1},{4,6},{5,7},{6,4},{7,5},{8,10},{9,11},{10,... | collective-permute-start | bytes 1253384 | tf_op jit(solution)/shard_map/ppermute | solution.py:32
  5.1 60.4 %collective-permute-start.4 = (bf16[272,768]{1,0:T(8,128)(2,1)S(1)}, bf16[272,768]{1,0:T(8,128)(2,1)}, u32[]{:S(2)}, u32[]{:S(2)}) collective-permute-start(bf16[272,768]{1,0:T(8,128)(2,1)S(1)} %fusion.52.refs_0_), channel_id=1, source_target_pairs={{0,1},{1,0},{2,3},{3,2},{4,5},{5,4},{6,7},{7,6},{8,9},{9,8},{10,11... | collective-permute-start | bytes 1253384 | tf_op jit(solution)/shard_map/ppermute | solution.py:32
  33.3 27.9 %collective-permute-start.3 = (bf16[192,2304]{1,0:T(8,128)(2,1)S(1)}, bf16[192,2304]{1,0:T(8,128)(2,1)S(1)}, u32[]{:S(2)}, u32[]{:S(2)}) collective-permute-start(bf16[192,2304]{1,0:T(8,128)(2,1)S(1)} %pad_maximum_fusion.13), channel_id=1, source_target_pairs={{0,4},{4,0},{8,12},{12,8},{1,5},{5,1},{9,13},{13,9},{2,6},{6,2},{1... | collective-permute-start | bytes 2654216 | tf_op jit(solution)/shard_map/ppermute | solution.py:32
  40.3 16.9 %collective-permute-start.16 = (bf16[2,256,768]{2,1,0:T(8,128)(2,1)S(1)}, bf16[2,256,768]{2,1,0:T(8,128)(2,1)S(1)}, u32[]{:S(2)}, u32[]{:S(2)}) collective-permute-start(bf16[2,256,768]{2,1,0:T(8,128)(2,1)S(1)} %copy-done.40), channel_id=1, source_target_pairs={{0,16},{16,0},{1,17},{17,1},{2,18},{18,2},{3,19},{19,3},{4,20},{20... | collective-permute-start | bytes 2359304 | tf_op jit(solution)/shard_map/ppermute | solution.py:32
  57.2 13.8 %collective-permute-start.12 = (bf16[192,2304]{1,0:T(8,128)(2,1)S(1)}, bf16[192,2304]{1,0:T(8,128)(2,1)S(1)}, u32[]{:S(2)}, u32[]{:S(2)}) collective-permute-start(bf16[192,2304]{1,0:T(8,128)(2,1)S(1)} %pad_maximum_fusion.14), channel_id=1, source_target_pairs={{0,4},{4,0},{8,12},{12,8},{1,5},{5,1},{9,13},{13,9},{2,6},{6,2},{1... | collective-permute-start | bytes 2654216 | tf_op jit(solution)/shard_map/ppermute | solution.py:32
  69.4 20.7 %collective-permute-start.8 = (bf16[400,1024]{1,0:T(8,128)(2,1)S(1)}, bf16[400,1024]{1,0:T(8,128)(2,1)S(1)}, u32[]{:S(2)}, u32[]{:S(2)}) collective-permute-start(bf16[400,1024]{1,0:T(8,128)(2,1)S(1)} %get-tuple-element.69.refs_0_), channel_id=1, source_target_pairs={{0,8},{4,12},{8,0},{12,4},{1,9},{5,13},{9,1},{13,5},{2,10},{6,14},... | collective-permute-start | bytes 2457608 | tf_op jit(solution)/shard_map/ppermute | solution.py:32
  70.7 19.4 %collective-permute-start.7 = (bf16[400,1024]{1,0:T(8,128)(2,1)S(1)}, bf16[400,1024]{1,0:T(8,128)(2,1)S(1)}, u32[]{:S(2)}, u32[]{:S(2)}) collective-permute-start(bf16[400,1024]{1,0:T(8,128)(2,1)S(1)} %get-tuple-element.69.refs_0_), channel_id=1, source_target_pairs={{0,4},{4,0},{8,12},{12,8},{1,5},{5,1},{9,13},{13,9},{2,6},{6,2},{1... | collective-permute-start | bytes 2457608 | tf_op jit(solution)/shard_map/ppermute | solution.py:32
  74.8 14.4 %collective-permute-start.15 = (bf16[192,256]{1,0:T(8,128)(2,1)S(1)}, bf16[192,256]{1,0:T(8,128)(2,1)S(1)}, u32[]{:S(2)}, u32[]{:S(2)}) collective-permute-start(bf16[192,256]{1,0:T(8,128)(2,1)S(1)} %get-tuple-element.200), channel_id=1, source_target_pairs={{0,3},{1,2},{2,1},{3,0},{4,7},{5,6},{6,5},{7,4},{8,11},{9,10},{10,... | collective-permute-start | bytes 294920 | tf_op jit(solution)/shard_map/ppermute | solution.py:32
  76.1 13.2 %collective-permute-start.14 = (bf16[192,256]{1,0:T(8,128)(2,1)S(1)}, bf16[192,256]{1,0:T(8,128)(2,1)S(1)}, u32[]{:S(2)}, u32[]{:S(2)}) collective-permute-start(bf16[192,256]{1,0:T(8,128)(2,1)S(1)} %get-tuple-element.201), channel_id=1, source_target_pairs={{0,2},{1,3},{2,0},{3,1},{4,6},{5,7},{6,4},{7,5},{8,10},{9,11},{10,... | collective-permute-start | bytes 294920 | tf_op jit(solution)/shard_map/ppermute | solution.py:32
  101.5 49.1 %collective-permute-start.20 = (bf16[256,768]{1,0:T(8,128)(2,1)S(1)}, bf16[256,768]{1,0:T(8,128)(2,1)}, u32[]{:S(2)}, u32[]{:S(2)}) collective-permute-start(bf16[256,768]{1,0:T(8,128)(2,1)S(1)} %copy-done.24), channel_id=1, source_target_pairs={{0,3},{1,2},{2,1},{3,0},{4,7},{5,6},{6,5},{7,4},{8,11},{9,10},{10,... | collective-permute-start | bytes 1179656 | tf_op jit(solution)/shard_map/ppermute | solution.py:32
  102.8 47.9 %collective-permute-start.19 = (bf16[256,768]{1,0:T(8,128)(2,1)S(1)}, bf16[256,768]{1,0:T(8,128)(2,1)}, u32[]{:S(2)}, u32[]{:S(2)}) collective-permute-start(bf16[256,768]{1,0:T(8,128)(2,1)S(1)} %copy-done.24), channel_id=1, source_target_pairs={{0,2},{1,3},{2,0},{3,1},{4,6},{5,7},{6,4},{7,5},{8,10},{9,11},{10,... | collective-permute-start | bytes 1179656 | tf_op jit(solution)/shard_map/ppermute | solution.py:32
  104.3 46.4 %collective-permute-start.18 = (bf16[256,768]{1,0:T(8,128)(2,1)S(1)}, bf16[256,768]{1,0:T(8,128)(2,1)}, u32[]{:S(2)}, u32[]{:S(2)}) collective-permute-start(bf16[256,768]{1,0:T(8,128)(2,1)S(1)} %copy-done.24), channel_id=1, source_target_pairs={{0,1},{1,0},{2,3},{3,2},{4,5},{5,4},{6,7},{7,6},{8,9},{9,8},{10,11... | collective-permute-start | bytes 1179656 | tf_op jit(solution)/shard_map/ppermute | solution.py:32
  105.5 39.7 %collective-permute-start.22 = (bf16[512,768]{1,0:T(8,128)(2,1)S(1)}, bf16[512,768]{1,0:T(8,128)(2,1)S(1)}, u32[]{:S(2)}, u32[]{:S(2)}) collective-permute-start(bf16[512,768]{1,0:T(8,128)(2,1)S(1)} %pad_maximum_fusion.18), channel_id=1, source_target_pairs={{0,16},{16,0},{1,17},{17,1},{2,18},{18,2},{3,19},{19,3},{4,20},{20... | collective-permute-start | bytes 2359304 | tf_op jit(solution)/shard_map/ppermute | solution.py:32
  107.1 41.8 %collective-permute-start.21 = (bf16[2,2,192,768]{3,2,1,0:T(8,128)(2,1)S(1)}, bf16[2,2,192,768]{3,2,1,0:T(8,128)(2,1)}, u32[]{:S(2)}, u32[]{:S(2)}) collective-permute-start(bf16[2,2,192,768]{3,2,1,0:T(8,128)(2,1)S(1)} %broadcast_select_fusion.6), channel_id=1, source_target_pairs={{0,8},{4,12},{8,0},{12,4},{1,9},{5,13},{9,1},{13,5},{2,10},{6,14},... | collective-permute-start | bytes 3538952 | tf_op jit(solution)/shard_map/ppermute | solution.py:32
  150.7 15.5 %collective-permute-start.23 = (bf16[2,384,1024]{2,1,0:T(8,128)(2,1)}, bf16[2,384,1024]{2,1,0:T(8,128)(2,1)}, u32[]{:S(2)}, u32[]{:S(2)}) collective-permute-start(bf16[2,384,1024]{2,1,0:T(8,128)(2,1)} %get-tuple-element.83), channel_id=1, source_target_pairs={{0,4},{4,0},{8,12},{12,8},{1,5},{5,1},{9,13},{13,9},{2,6},{6,2},{1... | collective-permute-start | bytes 4718600 | tf_op jit(solution)/shard_map/ppermute | solution.py:32
  164.3 14.3 %collective-permute-start.25 = (bf16[384,256]{1,0:T(8,128)(2,1)S(1)}, bf16[384,256]{1,0:T(8,128)(2,1)S(1)}, u32[]{:S(2)}, u32[]{:S(2)}) collective-permute-start(bf16[384,256]{1,0:T(8,128)(2,1)S(1)} %get-tuple-element.181), channel_id=1, source_target_pairs={{0,2},{1,3},{2,0},{3,1},{4,6},{5,7},{6,4},{7,5},{8,10},{9,11},{10,... | collective-permute-start | bytes 589832 | tf_op jit(solution)/shard_map/ppermute | solution.py:32
  178.7 15.1 %collective-permute-start.39 = (bf16[2,2,96,768]{3,2,1,0:T(8,128)(2,1)S(1)}, bf16[2,2,96,768]{3,2,1,0:T(8,128)(2,1)S(1)}, u32[]{:S(2)}, u32[]{:S(2)}) collective-permute-start(bf16[2,2,96,768]{3,2,1,0:T(8,128)(2,1)S(1)} %broadcast_select_fusion.13), channel_id=1, source_target_pairs={{0,1},{1,0},{2,3},{3,2},{4,5},{5,4},{6,7},{7,6},{8,9},{9,8},{10,11... | collective-permute-start | bytes 1769480 | tf_op jit(solution)/shard_map/ppermute | solution.py:32
  180.9 17.9 %collective-permute-start.27 = (bf16[1,384,1024]{2,1,0:T(8,128)(2,1)S(1)}, bf16[1,384,1024]{2,1,0:T(8,128)(2,1)S(1)}, u32[]{:S(2)}, u32[]{:S(2)}) collective-permute-start(bf16[1,384,1024]{2,1,0:T(8,128)(2,1)S(1)} %add_convert_fusion.2), channel_id=1, source_target_pairs={{0,8},{4,12},{8,0},{12,4},{1,9},{5,13},{9,1},{13,5},{2,10},{6,14},... | collective-permute-start | bytes 2359304 | tf_op jit(solution)/shard_map/ppermute | solution.py:32
  194.0 15.2 %collective-permute-start.40 = (bf16[2,2,48,768]{3,2,1,0:T(8,128)(2,1)S(1)}, bf16[2,2,48,768]{3,2,1,0:T(8,128)(2,1)S(1)}, u32[]{:S(2)}, u32[]{:S(2)}) collective-permute-start(bf16[2,2,48,768]{3,2,1,0:T(8,128)(2,1)S(1)} %broadcast_select_fusion.25), channel_id=1, source_target_pairs={{0,2},{1,3},{2,0},{3,1},{4,6},{5,7},{6,4},{7,5},{8,10},{9,11},{10,... | collective-permute-start | bytes 884744 | tf_op jit(solution)/shard_map/ppermute | solution.py:32
  212.6 23.5 %collective-permute-start.42 = (bf16[4,48,768]{2,1,0:T(8,128)(2,1)S(1)}, bf16[4,48,768]{2,1,0:T(8,128)(2,1)}, u32[]{:S(2)}, u32[]{:S(2)}) collective-permute-start(bf16[4,48,768]{2,1,0:T(8,128)(2,1)S(1)} %pad_maximum_fusion.31), channel_id=1, source_target_pairs={{0,2},{1,3},{2,0},{3,1},{4,6},{5,7},{6,4},{7,5},{8,10},{9,11},{10,... | collective-permute-start | bytes 884744 | tf_op jit(solution)/shard_map/ppermute | solution.py:32
  216.7 24.4 %collective-permute-start.31 = (bf16[4,96,768]{2,1,0:T(8,128)(2,1)}, bf16[4,96,768]{2,1,0:T(8,128)(2,1)}, u32[]{:S(2)}, u32[]{:S(2)}) collective-permute-start(bf16[4,96,768]{2,1,0:T(8,128)(2,1)} %broadcast_select_fusion.20), channel_id=1, source_target_pairs={{0,4},{4,0},{8,12},{12,8},{1,5},{5,1},{9,13},{13,9},{2,6},{6,2},{1... | collective-permute-start | bytes 1769480 | tf_op jit(solution)/shard_map/ppermute | solution.py:32
  220.4 40.5 %collective-permute-start.30 = (bf16[384,256]{1,0:T(8,128)(2,1)S(1)}, bf16[384,256]{1,0:T(8,128)(2,1)S(1)}, u32[]{:S(2)}, u32[]{:S(2)}) collective-permute-start(bf16[384,256]{1,0:T(8,128)(2,1)S(1)} %get-tuple-element.170), channel_id=1, source_target_pairs={{0,3},{1,2},{2,1},{3,0},{4,7},{5,6},{6,5},{7,4},{8,11},{9,10},{10,... | collective-permute-start | bytes 589832 | tf_op jit(solution)/shard_map/ppermute | solution.py:32
  220.7 40.2 %collective-permute-start.28 = (bf16[384,256]{1,0:T(8,128)(2,1)S(1)}, bf16[384,256]{1,0:T(8,128)(2,1)S(1)}, u32[]{:S(2)}, u32[]{:S(2)}) collective-permute-start(bf16[384,256]{1,0:T(8,128)(2,1)S(1)} %get-tuple-element.172), channel_id=1, source_target_pairs={{0,1},{1,0},{2,3},{3,2},{4,5},{5,4},{6,7},{7,6},{8,9},{9,8},{10,11... | collective-permute-start | bytes 589832 | tf_op jit(solution)/shard_map/ppermute | solution.py:32
  221.4 39.5 %collective-permute-start.29 = (bf16[384,256]{1,0:T(8,128)(2,1)S(1)}, bf16[384,256]{1,0:T(8,128)(2,1)S(1)}, u32[]{:S(2)}, u32[]{:S(2)}) collective-permute-start(bf16[384,256]{1,0:T(8,128)(2,1)S(1)} %get-tuple-element.173), channel_id=1, source_target_pairs={{0,2},{1,3},{2,0},{3,1},{4,6},{5,7},{6,4},{7,5},{8,10},{9,11},{10,... | collective-permute-start | bytes 589832 | tf_op jit(solution)/shard_map/ppermute | solution.py:32
  237.8 13.9 %collective-permute-start.45 = (bf16[2,96,768]{2,1,0:T(8,128)(2,1)S(1)}, bf16[2,96,768]{2,1,0:T(8,128)(2,1)S(1)}, u32[]{:S(2)}, u32[]{:S(2)}) collective-permute-start(bf16[2,96,768]{2,1,0:T(8,128)(2,1)S(1)} %get-tuple-element.186), channel_id=1, source_target_pairs={{0,1},{1,0},{2,3},{3,2},{4,5},{5,4},{6,7},{7,6},{8,9},{9,8},{10,11... | collective-permute-start | bytes 884744 | tf_op jit(solution)/shard_map/ppermute | solution.py:32
  241.1 25.8 %collective-permute-start.43 = (bf16[2,96,768]{2,1,0:T(8,128)(2,1)}, bf16[2,96,768]{2,1,0:T(8,128)(2,1)}, u32[]{:S(2)}, u32[]{:S(2)}) collective-permute-start(bf16[2,96,768]{2,1,0:T(8,128)(2,1)} %get-tuple-element.187), channel_id=1, source_target_pairs={{0,1},{1,0},{2,3},{3,2},{4,5},{5,4},{6,7},{7,6},{8,9},{9,8},{10,11... | collective-permute-start | bytes 884744 | tf_op jit(solution)/shard_map/ppermute | solution.py:32
  259.7 37.8 %collective-permute-start.46 = (bf16[2,192,768]{2,1,0:T(8,128)(2,1)}, bf16[2,192,768]{2,1,0:T(8,128)(2,1)}, u32[]{:S(2)}, u32[]{:S(2)}) collective-permute-start(bf16[2,192,768]{2,1,0:T(8,128)(2,1)} %pad_maximum_fusion.21), channel_id=1, source_target_pairs={{0,8},{4,12},{8,0},{12,4},{1,9},{5,13},{9,1},{13,5},{2,10},{6,14},... | collective-permute-start | bytes 1769480 | tf_op jit(solution)/shard_map/ppermute | solution.py:32
  268.1 29.4 %collective-permute-start.44 = (bf16[2,192,768]{2,1,0:T(8,128)(2,1)S(1)}, bf16[2,192,768]{2,1,0:T(8,128)(2,1)S(1)}, u32[]{:S(2)}, u32[]{:S(2)}) collective-permute-start(bf16[2,192,768]{2,1,0:T(8,128)(2,1)S(1)} %pad_maximum_fusion.20), channel_id=1, source_target_pairs={{0,8},{4,12},{8,0},{12,4},{1,9},{5,13},{9,1},{13,5},{2,10},{6,14},... | collective-permute-start | bytes 1769480 | tf_op jit(solution)/shard_map/ppermute | solution.py:32
  275.4 19.6 %collective-permute-start.34 = (bf16[6,48,384]{2,1,0:T(8,128)(2,1)S(1)}, bf16[6,48,384]{2,1,0:T(8,128)(2,1)S(1)}, u32[]{:S(2)}, u32[]{:S(2)}) collective-permute-start(bf16[6,48,384]{2,1,0:T(8,128)(2,1)S(1)} %add_convert_fusion.9), channel_id=1, source_target_pairs={{0,3},{1,2},{2,1},{3,0},{4,7},{5,6},{6,5},{7,4},{8,11},{9,10},{10,... | collective-permute-start | bytes 663560 | tf_op jit(solution)/shard_map/ppermute | solution.py:32
  295.4 13.4 %collective-permute-start.37 = (bf16[17,48,384]{2,1,0:T(8,128)(2,1)S(1)}, bf16[17,48,384]{2,1,0:T(8,128)(2,1)S(1)}, u32[]{:S(2)}, u32[]{:S(2)}) collective-permute-start(bf16[17,48,384]{2,1,0:T(8,128)(2,1)S(1)} %get-tuple-element.125), channel_id=1, source_target_pairs={{0,8},{4,12},{8,0},{12,4},{1,9},{5,13},{9,1},{13,5},{2,10},{6,14},... | collective-permute-start | bytes 1880072 | tf_op jit(solution)/shard_map/ppermute | solution.py:32
  310.2 18.1 %collective-permute-start.38 = (bf16[17,96,384]{2,1,0:T(8,128)(2,1)}, bf16[17,96,384]{2,1,0:T(8,128)(2,1)}, u32[]{:S(2)}, u32[]{:S(2)}) collective-permute-start(bf16[17,96,384]{2,1,0:T(8,128)(2,1)} %fusion.27), channel_id=1, source_target_pairs={{0,4},{4,0},{8,12},{12,8},{1,5},{5,1},{9,13},{13,9},{2,6},{6,2},{1... | collective-permute-start | bytes 3760136 | tf_op jit(solution)/shard_map/ppermute | solution.py:32
  (74 other events, 591.4 us)
